TPU v7x, 32 devices: a whole 2x2x4 slice. The times are simulated.
32 devices in a mesh: groups: 2 (over y), lat: 4 (over z), tok: 2 (over x), sub: 2 (over core).
Axes of the slice: x: 2, y: 2, z: 4, core: 2. Of those that a mesh axis runs over, the one named last changes fastest.
Arguments:
- acts: bfloat16 [4, 768, 2, 4096], P('groups', 'lat', 'sub', 'tok'), parts along dimension 0, may hold values from -6 to 6
- err_grad: bfloat16 [4, 768, 2, 4096], P(('groups', 'tok'), 'lat', 'sub'), parts along dimension 0, may hold values from -6 to 6
- codes: bfloat16 [4, 768, 512], P(('groups', 'tok'), None, 'lat'), parts along dimension 0, may hold values from 0.19921875 to 2
- dec_weight: bfloat16 [1024, 2, 4096], P(('groups', 'lat'), 'sub'), parts along dimension 0, may hold values from -0.0625 to 0.0625
- act_ids: int32 [4, 3, 3], P('groups'), parts along dimension 0, may hold values from 0 to 3, as said below
- act_count: int32 [4, 3], P('groups'), parts along dimension 0, may hold values from 1 to 3
Outputs:
- grad_dec: bfloat16 [1024, 2, 4096], P(('groups', 'lat'), 'sub', 'tok'), parts along dimension 0
- grad_enc: bfloat16 [2, 4096, 1024], P('sub', 'tok', ('groups', 'lat')), parts along dimension 2
There are 2 independent parts, one for each index of `groups`. A program takes and returns all parts, laid end to end along the dimension named above; each array names one. Nothing has to cross between parts.
Inputs may be any that keep to these rules, and one draw needn't show every extreme that they name: In every row act_ids[t, b, :] holds distinct latent block ids; only the first act_count[t, b] of them are active.
All inputs are finite; a program needn't handle non-finite values.
Results may differ from a plain program's by a relative error of at most 0.0049.
Values may be sent and summed in bfloat16 or wider, within the bound.
No kernel may reach another device: no remote copies, remote signals or barrier semaphores. Data moves between devices by JAX's collectives and lax.ppermute only.
A program may use at most 64 MiB of HBM per device.

v0:
```python
import jax
import jax.numpy as jnp
from jax import lax
from jax.sharding import PartitionSpec as P

TBLK = 256


def shards(acts, err_grad, codes, dec_weight, act_ids, act_count):
    tok_index = lax.axis_index("tok")
    lat_index = lax.axis_index("lat")
    local_tiles = lax.all_to_all(acts, "tok", split_axis=0, concat_axis=3, tiled=True)
    full_acts = lax.all_gather(local_tiles, "lat", axis=1, tiled=True)
    full_grad = lax.all_gather(err_grad, "lat", axis=1, tiled=True)
    row_total = codes.shape[1]
    lat_width = dec_weight.shape[0]
    half_width = dec_weight.shape[2]
    act_rows = full_acts.reshape(row_total, half_width)
    grad_rows = full_grad.reshape(row_total, half_width)
    weight_rows = dec_weight.reshape(lat_width, half_width)
    block_ids = lax.dynamic_index_in_dim(act_ids, tok_index, 0, keepdims=False)
    block_count = lax.dynamic_index_in_dim(act_count, tok_index, 0, keepdims=False)
    slot_index = jnp.arange(block_ids.shape[1], dtype=jnp.int32)
    matched = (block_ids == lat_index) & (slot_index[None, :] < block_count[:, None])
    block_on = jnp.any(matched, axis=1).astype(jnp.float32)
    row_mask = jnp.repeat(block_on, TBLK)
    contract_rows = (((0,), (0,)), ((), ()))
    contract_feat = (((1,), (1,)), ((), ()))
    partial_lat = lax.dot_general(
        grad_rows, weight_rows, contract_feat, preferred_element_type=jnp.float32
    )
    dlat = lax.psum(partial_lat, "sub")
    dcodes = (dlat * row_mask[:, None]).astype(jnp.bfloat16)
    used_codes = codes[0] * row_mask.astype(jnp.bfloat16)[:, None]
    dec_term = lax.dot_general(
        used_codes, grad_rows, contract_rows, preferred_element_type=jnp.float32
    )
    enc_term = lax.dot_general(act_rows, dcodes, contract_rows, preferred_element_type=jnp.float32)
    dec_sum, enc_sum = (
        lax.psum_scatter(
            dec_term.reshape(lat_width, 1, half_width), "tok", scatter_dimension=2, tiled=True
        ),
        lax.psum_scatter(
            enc_term.reshape(1, half_width, lat_width), "tok", scatter_dimension=1, tiled=True
        ),
    )
    return (dec_sum.astype(jnp.bfloat16), enc_sum.astype(jnp.bfloat16))


def solution(mesh):
    return jax.shard_map(
        shards,
        mesh=mesh,
        in_specs=(
            P("groups", "lat", "sub", "tok"),
            P(("groups", "tok"), "lat", "sub", None),
            P(("groups", "tok"), None, "lat"),
            P(("groups", "lat"), "sub", None),
            P("groups", None, None),
            P("groups", None),
        ),
        out_specs=(P(("groups", "lat"), "sub", "tok"), P("sub", "tok", ("groups", "lat"))),
        check_vma=False,
    )
```

profile of v0, /device:TPU:12, one launch (start us, length us, event | category | flops | bytes accessed | tf_op | source)
XLA Modules:
  0.0 341.6 jit_solution(12820839697393875679)
XLA Ops:
  7.2 0.0 all-gather.3.cloned.1.call-start
  7.2 0.7 all-gather.3.cloned.1.call-update
  7.9 3.7 %all-to-all-start = ((bf16[2,192,1,2048]{3,1,2,0:T(8,128)(2,1)}), bf16[2,192,1,2048]{3,1,2,0:T(8,128)(2,1)S(1)}, u32[]{:S(2)}, u32[]{:S(2)}) async-start(bf16[2,192,1,2048]{3,1,2,0:T(8,128)(2,1)} %param.6), calls=%async_computation.1 | async-start | bytes 3145728 | tf_op jit(solution)/shard_map/all_to_all | solution.py:12
  11.6 0.0 all-reduce.2.cloned.1.call-start
  11.7 111.7 %all-gather.3.cloned.1.call-done = bf16[1,768,1,4096]{3,1,2,0:T(8,128)(2,1)} async-done(((bf16[1,192,1,4096]{3,1,2,0:T(8,128)(2,1)}), bf16[1,768,1,4096]{3,1,2,0:T(8,128)(2,1)}) %all-gather.3.cloned.1.call-update) | async-done | bytes 6291472 | tf_op jit(solution)/shard_map/all_gather | solution.py:14
  123.3 5.3 %fusion.2 = f32[768,128]{1,0:T(8,128)} fusion(bf16[1,768,1,4096]{3,1,2,0:T(8,128)(2,1)} %all-gather.3.cloned.1.call-done, bf16[128,1,4096]{2,0,1:T(8,128)(2,1)S(1)} %copy-done), kind=kOutput, calls=%fused_computation.2 | convolution fusion | flops 805306368 | bytes 7733248 | tf_op jit(solution)/shard_map/dot_general | solution.py:29
  128.7 0.0 all-reduce.2.cloned.1.call-update
  128.7 0.0 all-gather.5.cloned.1.call-start
  128.7 1.3 copy.12
  130.0 0.0 all-gather.5.cloned.1.call-update
  130.0 0.0 reduce-scatter.3.cloned.1.call-start
  130.2 0.2 fusion.18
  130.3 0.1 broadcast_in_dim.2
  130.4 5.2 %fusion.6 = f32[128,1,4096]{2,0,1:T(8,128)} fusion(bf16[1,768,1,4096]{3,1,2,0:T(8,128)(2,1)} %all-gather.3.cloned.1.call-done, bf16[1,768,128]{2,1,0:T(8,128)(2,1)S(1)} %copy-done.1, bf16[768]{0:T(1024)(128)(2,1)S(1)} %convert_element_type.20), kind=kOutput, calls=%fused_computation.6 | convolution fusion | flops 805404672 | bytes 8586752 | tf_op jit(solution)/shard_map/dot_general | solution.py:35
  135.7 0.0 reduce-scatter.3.cloned.1.call-update
  135.7 0.0 reduce-scatter.5.cloned.1.call-start
  135.7 12.8 %all-reduce.2.cloned.1.call-done = f32[768,128]{1,0:T(8,128)} async-done(((f32[768,128]{1,0:T(8,128)}), f32[768,128]{1,0:T(8,128)}) %all-reduce.2.cloned.1.call-update) | async-done | bytes 393232 | tf_op jit(solution)/shard_map/psum | solution.py:32
  148.6 115.2 %all-gather.5.cloned.1.call-done = bf16[1,768,1,4096]{3,1,2,0:T(8,128)(2,1)} async-done(((bf16[1,192,1,4096]{3,1,2,0:T(8,128)(2,1)}), bf16[1,768,1,4096]{3,1,2,0:T(8,128)(2,1)}) %all-gather.5.cloned.1.call-update) | async-done | bytes 6291472 | tf_op jit(solution)/shard_map/all_gather | solution.py:13
  263.8 5.4 %fusion.9 = f32[1,4096,128]{1,2,0:T(8,128)} fusion(bf16[1,768,1,4096]{3,1,2,0:T(8,128)(2,1)} %all-gather.5.cloned.1.call-done, f32[768,128]{1,0:T(8,128)} %all-reduce.2.cloned.1.call-done, f32[768]{0:T(1024)S(1)} %reshape.40), kind=kOutput, calls=%fused_computation.7 | convolution fusion | flops 805502976 | bytes 8784896 | tf_op jit(solution)/shard_map/dot_general | solution.py:38
  269.2 29.6 %reduce-scatter.3.cloned.1.call-done = f32[128,1,2048]{2,0,1:T(8,128)} async-done(((f32[128,1,4096]{2,0,1:T(8,128)}), f32[128,1,2048]{2,0,1:T(8,128)}) %reduce-scatter.3.cloned.1.call-update) | async-done | bytes 1048592 | tf_op jit(solution)/shard_map/reduce_scatter | solution.py:40
  298.8 2.1 convert_element_type.21
  300.9 31.9 %reduce-scatter.5.cloned.1.call-done = f32[1,2048,128]{1,2,0:T(8,128)} async-done(((f32[1,4096,128]{1,2,0:T(8,128)}), f32[1,2048,128]{1,2,0:T(8,128)}) %reduce-scatter.5.cloned.1.call-update) | async-done | bytes 1048592 | tf_op jit(solution)/shard_map/reduce_scatter | solution.py:43
  332.8 1.3 convert_element_type.23
  334.1 1.0 copy.10
  (15 shorter events, 0.1 us)
Async XLA Ops:
  7.2 116.2 %copy-start = (bf16[128,1,4096]{2,0,1:T(8,128)(2,1)S(1)}, bf16[128,1,4096]{2,0,1:T(8,128)(2,1)}, u32[]{:S(2)}) copy-start(bf16[128,1,4096]{2,0,1:T(8,128)(2,1)} %param.9) | copy-start | bytes 3145732
  7.2 116.2 %all-gather.3.cloned.1.call-start = ((), (), s32[]{:S(2)}) async-start(), calls=%async_computation.3 | async-start | bytes 7864320 | tf_op jit(solution)/shard_map/all_gather | solution.py:14
  7.9 120.8 %all-to-all-start = ((bf16[2,192,1,2048]{3,1,2,0:T(8,128)(2,1)}), bf16[2,192,1,2048]{3,1,2,0:T(8,128)(2,1)S(1)}, u32[]{:S(2)}, u32[]{:S(2)}) async-start(bf16[2,192,1,2048]{3,1,2,0:T(8,128)(2,1)} %param.6), calls=%async_computation.1 | async-start | bytes 3145728 | tf_op jit(solution)/shard_map/all_to_all | solution.py:12
  11.6 118.5 %copy-start.3 = (s32[2,3]{1,0:T(2,128)S(1)}, s32[2,3]{1,0:T(2,128)}, u32[]{:S(2)}) copy-start(s32[2,3]{1,0:T(2,128)} %param.11) | copy-start | bytes 76
  11.6 118.5 %copy-start.2 = (s32[2,3,3]{2,0,1:T(2,128)S(1)}, s32[2,3,3]{2,0,1:T(2,128)}, u32[]{:S(2)}) copy-start(s32[2,3,3]{2,0,1:T(2,128)} %param.10) | copy-start | bytes 220
  11.6 118.8 %copy-start.1 = (bf16[1,768,128]{2,1,0:T(8,128)(2,1)S(1)}, bf16[1,768,128]{2,1,0:T(8,128)(2,1)}, u32[]{:S(2)}) copy-start(bf16[1,768,128]{2,1,0:T(8,128)(2,1)} %param.8) | copy-start | bytes 589828
  11.6 136.9 %all-reduce.2.cloned.1.call-start = ((), (), s32[]{:S(2)}) async-start(), calls=%async_computation.5 | async-start | bytes 786432 | tf_op jit(solution)/shard_map/psum | solution.py:32
  128.7 135.1 %all-gather.5.cloned.1.call-start = ((), (), s32[]{:S(2)}) async-start(), calls=%async_computation.6 | async-start | bytes 7864320 | tf_op jit(solution)/shard_map/all_gather | solution.py:13
  130.0 168.7 %reduce-scatter.3.cloned.1.call-start = ((), (), s32[]{:S(2)}) async-start(), calls=%async_computation.4 | async-start | bytes 3145728 | tf_op jit(solution)/shard_map/reduce_scatter | solution.py:40
  135.7 197.1 %reduce-scatter.5.cloned.1.call-start = ((), (), s32[]{:S(2)}) async-start(), calls=%async_computation.7 | async-start | bytes 3145728 | tf_op jit(solution)/shard_map/reduce_scatter | solution.py:43
Sparse Core Ops, SparseCore 0:
  9.6 113.7 all-gather.2
  128.8 19.7 all-reduce.1
  150.2 113.5 all-gather.4
  266.0 32.7 reduce-scatter.2
  300.9 31.8 reduce-scatter.4
where the time goes:
time: 344 us; the launch traced here: 342 us
  waiting for transfers between devices  302 us (88%)
  matrix products  15.9 us (5%)
  between operations  13.9 us (4%)
  starting transfers between devices  3.89 us (1%)
  other arithmetic  3.58 us (1%)
    all_gather x1, waiting for transfers between devices, shards(): full_acts = lax.all_gather(local_tiles, 'lat', axis=1, tiled=True)  115 us
    all_gather x1, waiting for transfers between devices, shards(): full_grad = lax.all_gather(err_grad, 'lat', axis=1, tiled=True)  112 us
    reduce_scatter x1, waiting for transfers between devices, shards(): lax.psum_scatter(enc_term.reshape(1, half_width, lat_width), 'tok', scatt...  31.9 us
    reduce_scatter x1, waiting for transfers between devices, shards(): lax.psum_scatter(dec_term.reshape(lat_width, 1, half_width), 'tok', scatt...  29.6 us
    psum x1, waiting for transfers between devices, shards(): dlat = lax.psum(partial_lat, 'sub')  12.8 us
  transfers between devices with their start and end apart: 6, of which 5 were waited for; matrix products, arithmetic and copies ran while one was open for 6% of the time, Pallas kernels for 0%

commit v1 on v0

v1 whole, which is shorter than its diff:
```python
import jax
import jax.numpy as jnp
from jax import lax
from jax.sharding import PartitionSpec as P

TBLK = 256
CONTRACT_LAST = (((1,), (1,)), ((), ()))
CONTRACT_ROWS = (((0,), (0,)), ((), ()))


def dot32(left, right, dims):
    return lax.dot_general(left, right, dims, preferred_element_type=jnp.float32)


def valid_ids(act_ids, act_count):
    slot = jnp.arange(act_ids.shape[2], dtype=jnp.int32)
    return jnp.where(slot[None, None, :] < act_count[:, :, None], act_ids, -1)


def row_hits(ids, first_row, rows, block):
    on = jnp.any(ids == block, axis=2)
    tile = (first_row + jnp.arange(rows, dtype=jnp.int32)) // TBLK
    hit = on[:, :, None] & (tile[None, None, :] == jnp.arange(ids.shape[1])[None, :, None])
    return jnp.any(hit, axis=1).astype(jnp.float32)


def shards_line(acts, err_grad, codes, dec_weight, act_ids, act_count):
    z = lax.axis_index("lat")
    x = lax.axis_index("tok")
    rows = err_grad.shape[1]
    lat = dec_weight.shape[0]
    width = acts.shape[3]
    swap = [(0, 1), (1, 0)]
    up = [(0, 1), (1, 2), (2, 3)]
    down = [(3, 2), (2, 1), (1, 0)]

    def send(value, axis, pairs):
        return lax.ppermute(value, axis, pairs)

    w_own = lax.dynamic_slice_in_dim(dec_weight.reshape(lat, -1), x * width, width, 1)
    w_far = send(w_own, "lat", [(0, 3), (3, 0)])
    w_two = send(w_own, "lat", [(0, 2), (1, 3), (2, 0), (3, 1)])
    w_prev = send(w_own, "lat", up)
    w_next = send(w_own, "lat", down)

    err = err_grad.reshape(rows, -1)
    err_own = lax.dynamic_slice_in_dim(err, x * width, width, 1)
    err_other = send(lax.dynamic_slice_in_dim(err, (1 - x) * width, width, 1), "tok", swap)

    ids = valid_ids(act_ids, act_count)

    code_hits = row_hits(lax.dynamic_slice_in_dim(ids, x, 1, 0), 0, codes.shape[1], z)
    used = codes[0] * code_hits.astype(jnp.bfloat16).T
    codes_own = lax.all_to_all(used, "lat", split_axis=0, concat_axis=1, tiled=True)
    codes_other = send(codes_own, "tok", swap)
    dec_part = dot32(codes_own, err_own, CONTRACT_ROWS) + dot32(codes_other, err_other, CONTRACT_ROWS)
    grad_dec = lax.psum_scatter(
        dec_part.astype(jnp.bfloat16), "lat", scatter_dimension=0, tiled=True
    )

    act_rows = acts.reshape(2 * rows, width)

    def enc_terms(weights, blocks):
        w = jnp.concatenate(weights, axis=0) if len(weights) > 1 else weights[0]
        part_own = dot32(err_own, w, CONTRACT_LAST)
        part_other = dot32(err_other, w, CONTRACT_LAST)
        first = jnp.where(x == 0, part_own, part_other)
        second = jnp.where(x == 0, part_other, part_own)
        part = jnp.concatenate([first, second], axis=0)
        part = part + send(part, "sub", swap)
        part = part + send(part, "tok", swap)
        hits = [row_hits(ids, z * rows, rows, block).reshape(2 * rows, 1) for block in blocks]
        hits = jnp.concatenate([jnp.broadcast_to(h, (2 * rows, lat)) for h in hits], axis=1)
        dcodes = (part * hits).astype(jnp.bfloat16)
        return [
            dot32(act_rows, dcodes[:, i * lat : (i + 1) * lat], CONTRACT_ROWS)
            for i in range(len(blocks))
        ]

    (far,) = enc_terms([w_far], [jnp.where(z == 0, 3, 0)])
    got_far = send(far.astype(jnp.bfloat16), "lat", [(0, 1), (3, 2)])
    (two,) = enc_terms([w_two], [lax.rem(z + 2, 4)])
    two = (two + got_far.astype(jnp.float32)).astype(jnp.bfloat16)
    two_up = send(two, "lat", [(0, 1), (1, 2)])
    two_down = send(two, "lat", [(3, 2), (2, 1)])
    nxt, prev, own = enc_terms([w_next, w_prev, w_own], [z + 1, z - 1, z])
    nxt = (nxt + two_up.astype(jnp.float32)).astype(jnp.bfloat16)
    prev = (prev + two_down.astype(jnp.float32)).astype(jnp.bfloat16)
    from_prev = send(nxt, "lat", up)
    from_next = send(prev, "lat", down)
    grad_enc = own + from_prev.astype(jnp.float32) + from_next.astype(jnp.float32)
    return grad_dec[:, None, :], grad_enc.astype(jnp.bfloat16)[None]


def shards_any(acts, err_grad, codes, dec_weight, act_ids, act_count):
    z = lax.axis_index("lat")
    x = lax.axis_index("tok")
    rows = err_grad.shape[1]
    lat = dec_weight.shape[0]
    width = acts.shape[3]
    groups = acts.shape[0]
    blocks = lax.axis_size("lat")
    w_own = lax.dynamic_slice_in_dim(dec_weight.reshape(lat, -1), x * width, width, 1)
    w_all = lax.all_gather(w_own, "lat", axis=0, tiled=True)
    err = lax.all_to_all(err_grad, "tok", split_axis=3, concat_axis=0, tiled=True)
    err = err.reshape(groups * rows, width)
    ids = valid_ids(act_ids, act_count)
    code_hits = row_hits(lax.dynamic_slice_in_dim(ids, x, 1, 0), 0, codes.shape[1], z)
    used = codes[0] * code_hits.astype(jnp.bfloat16).T
    used = lax.all_to_all(used, "lat", split_axis=0, concat_axis=1, tiled=True)
    used = lax.all_gather(used, "tok", axis=0, tiled=True)
    dec_part = dot32(used, err, CONTRACT_ROWS)
    grad_dec = lax.psum_scatter(dec_part, "lat", scatter_dimension=0, tiled=True)
    dlat = lax.psum(dot32(err, w_all, CONTRACT_LAST), ("tok", "sub"))
    hits = [row_hits(ids, z * rows, rows, block).reshape(groups * rows, 1) for block in range(blocks)]
    hits = jnp.concatenate([jnp.broadcast_to(h, (groups * rows, lat)) for h in hits], axis=1)
    dcodes = (dlat * hits).astype(jnp.bfloat16)
    enc_part = dot32(acts.reshape(groups * rows, width), dcodes, CONTRACT_ROWS)
    grad_enc = lax.psum_scatter(enc_part, "lat", scatter_dimension=1, tiled=True)
    return grad_dec.astype(jnp.bfloat16)[:, None, :], grad_enc.astype(jnp.bfloat16)[None]


def solution(mesh):
    line = mesh.shape["lat"] == 4 and mesh.shape["tok"] == 2
    return jax.shard_map(
        shards_line if line else shards_any,
        mesh=mesh,
        in_specs=(
            P("groups", "lat", "sub", "tok"),
            P(("groups", "tok"), "lat", "sub", None),
            P(("groups", "tok"), None, "lat"),
            P(("groups", "lat"), "sub", None),
            P("groups", None, None),
            P("groups", None),
        ),
        out_specs=(P(("groups", "lat"), "sub", "tok"), P("sub", "tok", ("groups", "lat"))),
        check_vma=False,
    )
```

time: 344 us -> 171 us (0.50)
  waiting for transfers between devices: 302 us -> 92 us
  starting transfers between devices: 3.89 us -> 34.9 us
  local copies, waits for them, and re-layouts: 2.38 us -> 6.15 us
    all_gather x2 -> x0, waiting for transfers between devices: 227 us -> none  [the longest x1 115 us: shards(): full_acts = lax.all_gather(local_tiles, 'lat', axis=1, tiled=True)]
    reduce_scatter x2 -> x1, waiting for transfers between devices: 61.5 us -> 0.01 us  [shards_line(): lax.psum_scatter(dec_part.astype(jnp.bfloat16), 'lat', scatter_dimension=...]
    ppermute x0 -> x17, waiting for transfers between devices: none -> 58 us  [send(): return lax.ppermute(value, axis, pairs)]
    all_to_all x1, waiting for transfers between devices: 0.01 us -> 34 us  [shards_line(): lax.all_to_all(used, 'lat', split_axis=0, concat_axis=1, tiled=True)]
    ppermute x0 -> x17, starting transfers between devices: none -> 31.5 us  [send(): return lax.ppermute(value, axis, pairs)]
    psum x1 -> x0, waiting for transfers between devices: 12.8 us -> none  [shards(): dlat = lax.psum(partial_lat, 'sub')]
    dot_general x3 -> x13, matrix products: 15.9 us -> 18.4 us  [dot32(): lax.dot_general(left, right, dims, preferred_element_type=jnp.float32)]
  transfers between devices with their start and end apart: 6 -> 19, of which waited for: 5 -> 9; matrix products, arithmetic and copies ran while one was open for 6% -> 15% of each run, Pallas kernels for 0% -> 0%
where the time goes in v1:
time: 171 us; the launch traced here: 170 us
  waiting for transfers between devices  92 us (54%)
  starting transfers between devices  34.9 us (20%)
  matrix products  18.4 us (11%)
  between operations  14.4 us (8%)
  local copies, waits for them, and re-layouts  6.15 us (4%)
  other arithmetic  3.57 us (2%)
    ppermute x17, waiting for transfers between devices, send(): return lax.ppermute(value, axis, pairs)  58 us
    all_to_all x1, waiting for transfers between devices, shards_line(): lax.all_to_all(used, 'lat', split_axis=0, concat_axis=1, tiled=True)  34 us
    ppermute x17, starting transfers between devices, send(): return lax.ppermute(value, axis, pairs)  31.5 us
    dot_general x13, matrix products, dot32(): lax.dot_general(left, right, dims, preferred_element_type=jnp.float32)  18.4 us
    all_to_all x1, starting transfers between devices, shards_line(): lax.all_to_all(used, 'lat', split_axis=0, concat_axis=1, tiled=True)  3.42 us
  transfers between devices with their start and end apart: 19, of which 9 were waited for; matrix products, arithmetic and copies ran while one was open for 15% of the time, Pallas kernels for 0%

profile of v1, /device:TPU:12, one launch (start us, length us, event | category | flops | bytes accessed | tf_op | source)
XLA Modules:
  0.0 169.5 jit_solution(7952842008489660757)
XLA Ops:
  7.2 2.0 %dynamic-slice_bitcast_fusion.1 = bf16[128,2048]{1,0:T(8,128)(2,1)} fusion(bf16[128,1,4096]{2,0,1:T(8,128)(2,1)} %param.9, s32[]{:T(128)S(6)} %select_n.75), kind=kLoop, calls=%fused_computation.31 | loop fusion | bytes 1048580 | tf_op jit(solution)/shard_map/dynamic_slice | solution.py:40
  10.7 3.3 %collective-permute-start.6 = (bf16[128,2048]{1,0:T(8,128)(2,1)}, bf16[128,2048]{1,0:T(8,128)(2,1)}, u32[]{:S(2)}, u32[]{:S(2)}) collective-permute-start(bf16[128,2048]{1,0:T(8,128)(2,1)} %dynamic-slice_bitcast_fusion.1), channel_id=1, source_target_pairs={{0,8},{4,12},{8,0},{12,4},{1,9},{5,13},{9,1},{13,5},{2,10},{6,14},... | collective-permute-start | bytes 1572872 | tf_op jit(solution)/shard_map/ppermute | solution.py:38
  14.0 4.6 %collective-permute-start.3 = (bf16[128,2048]{1,0:T(8,128)(2,1)}, bf16[128,2048]{1,0:T(8,128)(2,1)}, u32[]{:S(2)}, u32[]{:S(2)}) collective-permute-start(bf16[128,2048]{1,0:T(8,128)(2,1)} %dynamic-slice_bitcast_fusion.1), channel_id=1, source_target_pairs={{0,4},{4,8},{8,12},{1,5},{5,9},{9,13},{2,6},{6,10},{10,14},{3,7},{... | collective-permute-start | bytes 1572872 | tf_op jit(solution)/shard_map/ppermute | solution.py:38
  20.9 1.8 %broadcast_multiply_fusion = bf16[4,192,128]{2,1,0:T(8,128)(2,1)} fusion(bf16[4,192,128]{2,1,0:T(8,128)(2,1)} %bitcast.83, bf16[4,192]{1,0:T(4,128)(2,1)S(1)} %convert_element_type.119), kind=kLoop, calls=%fused_computation.48 | loop fusion | flops 98304 | bytes 394752 | tf_op jit(solution)/shard_map/mul | solution.py:53
  22.7 3.4 %all-to-all-start = ((bf16[4,192,128]{2,1,0:T(8,128)(2,1)}), bf16[4,192,128]{2,1,0:T(8,128)(2,1)S(1)}, u32[]{:S(2)}, u32[]{:S(2)}) async-start(bf16[4,192,128]{2,1,0:T(8,128)(2,1)} %broadcast_multiply_fusion), calls=%async_computation | async-start | bytes 393216 | tf_op jit(solution)/shard_map/all_to_all | solution.py:54
  29.3 34.0 %all-to-all-done = bf16[4,192,128]{2,1,0:T(8,128)(2,1)S(1)} async-done(((bf16[4,192,128]{2,1,0:T(8,128)(2,1)}), bf16[4,192,128]{2,1,0:T(8,128)(2,1)S(1)}, u32[]{:S(2)}, u32[]{:S(2)}) %all-to-all-start) | async-done | bytes 196640 | tf_op jit(solution)/shard_map/all_to_all | solution.py:54
  64.9 1.9 %fusion.17 = f32[512,2048]{1,0:T(8,128)S(1)} fusion(bf16[1,192,1,4096]{3,1,2,0:T(8,128)(2,1)} %param.7, s32[]{:T(128)S(6)} %select_n.75, bf16[4,192,128]{2,1,0:T(8,128)(2,1)S(1)} %all-to-all-done), kind=kOutput, calls=%fused_computation.24 | convolution fusion | flops 402653184 | bytes 5177348 | tf_op jit(solution)/shard_map/dot_general | solution.py:12
  66.8 2.6 %collective-permute-done = bf16[192,512]{1,0:T(8,128)(2,1)S(1)} collective-permute-done((bf16[192,512]{1,0:T(8,128)(2,1)S(1)}, bf16[192,512]{1,0:T(8,128)(2,1)S(1)}, u32[]{:S(2)}, u32[]{:S(2)}) %collective-permute-start) | collective-permute-done | bytes 196640 | tf_op jit(solution)/shard_map/ppermute | solution.py:38
  69.4 1.9 %collective-permute-start.2 = (bf16[128,2048]{1,0:T(8,128)(2,1)}, bf16[128,2048]{1,0:T(8,128)(2,1)S(1)}, u32[]{:S(2)}, u32[]{:S(2)}) collective-permute-start(bf16[128,2048]{1,0:T(8,128)(2,1)} %dynamic-slice_bitcast_fusion.1), channel_id=1, source_target_pairs={{12,8},{8,4},{4,0},{13,9},{9,5},{5,1},{14,10},{10,6},{6,2},{15,11}... | collective-permute-start | bytes 1572872 | tf_op jit(solution)/shard_map/ppermute | solution.py:38
  71.3 2.1 %add_convert_fusion = bf16[512,2048]{1,0:T(8,128)(2,1)} fusion(f32[512,2048]{1,0:T(8,128)S(1)} %fusion.17, bf16[192,512]{1,0:T(8,128)(2,1)S(1)} %collective-permute-done, bf16[192,2048]{1,0:T(8,128)(2,1)S(1)} %collective-permute-done.1), kind=kOutput, calls=%fused_computation | convolution fusion | flops 404750336 | bytes 7274496 | tf_op jit(solution)/shard_map/dot_general | solution.py:12
  74.9 1.7 broadcast_select_fusion.3
  76.7 9.0 %collective-permute-done.2 = bf16[128,2048]{1,0:T(8,128)(2,1)S(1)} collective-permute-done((bf16[128,2048]{1,0:T(8,128)(2,1)}, bf16[128,2048]{1,0:T(8,128)(2,1)S(1)}, u32[]{:S(2)}, u32[]{:S(2)}) %collective-permute-start.2) | collective-permute-done | bytes 524320 | tf_op jit(solution)/shard_map/ppermute | solution.py:38
  85.6 1.9 %fusion.19 = f32[192,384]{1,0:T(8,128)S(1)} fusion(bf16[192,2048]{1,0:T(8,128)(2,1)S(1)} %collective-permute-done.1, bf16[128,2048]{1,0:T(8,128)(2,1)} %dynamic-slice_bitcast_fusion.1, bf16[128,2048]{1,0:T(8,128)(2,1)} %collective-permute-done.3, bf16[128,2048]{1,0:T(8,128)(2,1)S(1)} %collective-permute-done.2), kind=kOutput, calls=%fused_computation.27 | convolution fusion | flops 306708480 | bytes 2654208 | tf_op jit(solution)/shard_map/dot_general | solution.py:12
  87.5 1.9 %broadcast_select_fusion.1 = (f32[192,384]{1,0:T(8,128)S(1)}, f32[192,384]{1,0:T(8,128)S(1)}) fusion(f32[192,384]{1,0:T(8,128)S(1)} %fusion.19, pred[]{:T(512)S(6)} %eq.58, bf16[128,2048]{1,0:T(8,128)(2,1)} %dynamic-slice_bitcast_fusion.1, bf16[128,2048]{1,0:T(8,128)(2,1)} %collective-permute-done.3, bf16[128,2048]{1,0:T(8,128)(2,1)S(1)} %collective-permute-done.2, ...), kind=kOutput, calls=%fused_computation.42 | convolution fusion | flops 306855936 | bytes 3244037 | tf_op jit(solution)/shard_map/dot_general | solution.py:12
  94.4 4.0 %collective-permute-done.11 = f32[384,128]{1,0:T(8,128)S(1)} collective-permute-done((f32[384,128]{1,0:T(8,128)S(1)}, f32[384,128]{1,0:T(8,128)S(1)}, u32[]{:S(2)}, u32[]{:S(2)}) %collective-permute-start.11) | collective-permute-done | bytes 196640 | tf_op jit(solution)/shard_map/ppermute | solution.py:38
  102.6 5.6 %collective-permute-done.8 = f32[384,128]{1,0:T(8,128)} collective-permute-done((f32[384,128]{1,0:T(8,128)S(1)}, f32[384,128]{1,0:T(8,128)}, u32[]{:S(2)}, u32[]{:S(2)}) %collective-permute-start.8) | collective-permute-done | bytes 196640 | tf_op jit(solution)/shard_map/ppermute | solution.py:38
  108.2 18.4 %collective-permute-done.12 = bf16[2048,128]{0,1:T(8,128)(2,1)} collective-permute-done((bf16[2048,128]{0,1:T(8,128)(2,1)S(1)}, bf16[2048,128]{0,1:T(8,128)(2,1)}, u32[]{:S(2)}, u32[]{:S(2)}) %collective-permute-start.12) | collective-permute-done | bytes 524320 | tf_op jit(solution)/shard_map/ppermute | solution.py:38
  126.6 1.7 %fusion.7 = bf16[2048,128]{0,1:T(8,128)(2,1)S(1)} fusion(bf16[384,2048]{1,0:T(8,128)(2,1)S(1)} %bitcast.80, bf16[2048,128]{0,1:T(8,128)(2,1)} %collective-permute-done.12, f32[384,128]{1,0:T(8,128)S(1)} %fusion.42, f32[384,128]{1,0:T(8,128)} %collective-permute-done.8, f32[384]{0:T(512)S(1)} %reshape.199), kind=kOutput, calls=%fused_computation.12 | convolution fusion | flops 202260480 | bytes 3016192 | tf_op jit(solution)/shard_map/dot_general | solution.py:12
  129.9 4.5 %collective-permute-start.13 = (bf16[2048,128]{0,1:T(8,128)(2,1)S(1)}, bf16[2048,128]{0,1:T(8,128)(2,1)S(1)}, u32[]{:S(2)}, u32[]{:S(2)}) collective-permute-start(bf16[2048,128]{0,1:T(8,128)(2,1)S(1)} %fusion.7), channel_id=1, source_target_pairs={{0,4},{4,8},{1,5},{5,9},{2,6},{6,10},{3,7},{7,11},{16,20},{20,24},... | collective-permute-start | bytes 1572872 | tf_op jit(solution)/shard_map/ppermute | solution.py:38
  134.9 8.4 %collective-permute-done.15 = bf16[2048,128]{0,1:T(8,128)(2,1)} collective-permute-done((bf16[2048,128]{0,1:T(8,128)(2,1)S(1)}, bf16[2048,128]{0,1:T(8,128)(2,1)}, u32[]{:S(2)}, u32[]{:S(2)}) %collective-permute-start.15) | collective-permute-done | bytes 524320 | tf_op jit(solution)/shard_map/ppermute | solution.py:38
  144.8 1.9 %collective-permute-start.16 = (bf16[2048,128]{0,1:T(8,128)(2,1)S(1)}, bf16[2048,128]{0,1:T(8,128)(2,1)S(1)}, u32[]{:S(2)}, u32[]{:S(2)}) collective-permute-start(bf16[2048,128]{0,1:T(8,128)(2,1)S(1)} %fusion.8), channel_id=1, source_target_pairs={{12,8},{8,4},{4,0},{13,9},{9,5},{5,1},{14,10},{10,6},{6,2},{15,11}... | collective-permute-start | bytes 1572872 | tf_op jit(solution)/shard_map/ppermute | solution.py:38
  147.2 3.9 %collective-permute-start.14 = (bf16[2048,128]{0,1:T(8,128)(2,1)S(1)}, bf16[2048,128]{0,1:T(8,128)(2,1)S(1)}, u32[]{:S(2)}, u32[]{:S(2)}) collective-permute-start(bf16[2048,128]{0,1:T(8,128)(2,1)S(1)} %fusion.6), channel_id=1, source_target_pairs={{0,4},{4,8},{8,12},{1,5},{5,9},{9,13},{2,6},{6,10},{10,14},{3,7},{... | collective-permute-start | bytes 1572872 | tf_op jit(solution)/shard_map/ppermute | solution.py:38
  151.2 7.6 %collective-permute-done.16 = bf16[2048,128]{0,1:T(8,128)(2,1)S(1)} collective-permute-done((bf16[2048,128]{0,1:T(8,128)(2,1)S(1)}, bf16[2048,128]{0,1:T(8,128)(2,1)S(1)}, u32[]{:S(2)}, u32[]{:S(2)}) %collective-permute-start.16) | collective-permute-done | bytes 524320 | tf_op jit(solution)/shard_map/ppermute | solution.py:38
  158.8 2.4 %collective-permute-done.14 = bf16[2048,128]{0,1:T(8,128)(2,1)S(1)} collective-permute-done((bf16[2048,128]{0,1:T(8,128)(2,1)S(1)}, bf16[2048,128]{0,1:T(8,128)(2,1)S(1)}, u32[]{:S(2)}, u32[]{:S(2)}) %collective-permute-start.14) | collective-permute-done | bytes 524320 | tf_op jit(solution)/shard_map/ppermute | solution.py:38
  (74 shorter events, 24.5 us)
Async XLA Ops:
  7.2 91.2 %copy-start = (bf16[2,192,1,2048]{3,1,2,0:T(8,128)(2,1)S(1)}, bf16[2,192,1,2048]{3,1,2,0:T(8,128)(2,1)}, u32[]{:S(2)}) copy-start(bf16[2,192,1,2048]{3,1,2,0:T(8,128)(2,1)} %param.6) | copy-start | bytes 4718596
  7.2 18.9 %copy-start.1 = (bf16[1,192,1,4096]{3,1,2,0:T(8,128)(2,1)S(1)}, bf16[1,192,1,4096]{3,1,2,0:T(8,128)(2,1)}, u32[]{:S(2)}) copy-start(bf16[1,192,1,4096]{3,1,2,0:T(8,128)(2,1)} %param.7) | copy-start | bytes 4718596
  9.2 64.2 %collective-permute-start.9 = (bf16[128,2048]{1,0:T(8,128)(2,1)}, bf16[128,2048]{1,0:T(8,128)(2,1)}, u32[]{:S(2)}, u32[]{:S(2)}) collective-permute-start(bf16[128,2048]{1,0:T(8,128)(2,1)} %dynamic-slice_bitcast_fusion.1), channel_id=1, source_target_pairs={{0,12},{12,0},{1,13},{13,1},{2,14},{14,2},{3,15},{15,3},{16,28},{2... | collective-permute-start | bytes 1572872 | tf_op jit(solution)/shard_map/ppermute | solution.py:38
  10.7 78.8 %collective-permute-start.6 = (bf16[128,2048]{1,0:T(8,128)(2,1)}, bf16[128,2048]{1,0:T(8,128)(2,1)}, u32[]{:S(2)}, u32[]{:S(2)}) collective-permute-start(bf16[128,2048]{1,0:T(8,128)(2,1)} %dynamic-slice_bitcast_fusion.1), channel_id=1, source_target_pairs={{0,8},{4,12},{8,0},{12,4},{1,9},{5,13},{9,1},{13,5},{2,10},{6,14},... | collective-permute-start | bytes 1572872 | tf_op jit(solution)/shard_map/ppermute | solution.py:38
  14.0 62.6 %collective-permute-start.3 = (bf16[128,2048]{1,0:T(8,128)(2,1)}, bf16[128,2048]{1,0:T(8,128)(2,1)}, u32[]{:S(2)}, u32[]{:S(2)}) collective-permute-start(bf16[128,2048]{1,0:T(8,128)(2,1)} %dynamic-slice_bitcast_fusion.1), channel_id=1, source_target_pairs={{0,4},{4,8},{8,12},{1,5},{5,9},{9,13},{2,6},{6,10},{10,14},{3,7},{... | collective-permute-start | bytes 1572872 | tf_op jit(solution)/shard_map/ppermute | solution.py:38
  22.7 40.7 %all-to-all-start = ((bf16[4,192,128]{2,1,0:T(8,128)(2,1)}), bf16[4,192,128]{2,1,0:T(8,128)(2,1)S(1)}, u32[]{:S(2)}, u32[]{:S(2)}) async-start(bf16[4,192,128]{2,1,0:T(8,128)(2,1)} %broadcast_multiply_fusion), calls=%async_computation | async-start | bytes 393216 | tf_op jit(solution)/shard_map/all_to_all | solution.py:54
  26.1 136.6 %reduce-scatter.2.cloned.1.call-start = ((), (), s32[]{:S(2)}) async-start(), calls=%async_computation.2 | async-start | bytes 2621440 | tf_op jit(solution)/shard_map/reduce_scatter | solution.py:57
  27.0 44.3 %collective-permute-start.1 = (bf16[192,2048]{1,0:T(8,128)(2,1)}, bf16[192,2048]{1,0:T(8,128)(2,1)S(1)}, u32[]{:S(2)}, u32[]{:S(2)}) collective-permute-start(bf16[192,2048]{1,0:T(8,128)(2,1)} %dynamic-slice_bitcast_fusion), channel_id=1, source_target_pairs={{0,2},{2,0},{1,3},{3,1},{4,6},{6,4},{5,7},{7,5},{8,10},{10,8},{9,1... | collective-permute-start | bytes 2359304 | tf_op jit(solution)/shard_map/ppermute | solution.py:38
  63.3 6.0 %collective-permute-start = (bf16[192,512]{1,0:T(8,128)(2,1)S(1)}, bf16[192,512]{1,0:T(8,128)(2,1)S(1)}, u32[]{:S(2)}, u32[]{:S(2)}) collective-permute-start(bf16[192,512]{1,0:T(8,128)(2,1)S(1)} %copy_bitcast_fusion), channel_id=1, source_target_pairs={{0,2},{2,0},{1,3},{3,1},{4,6},{6,4},{5,7},{7,5},{8,10},{10,8},{9,1... | collective-permute-start | bytes 589832 | tf_op jit(solution)/shard_map/ppermute | solution.py:38
  69.4 16.2 %collective-permute-start.2 = (bf16[128,2048]{1,0:T(8,128)(2,1)}, bf16[128,2048]{1,0:T(8,128)(2,1)S(1)}, u32[]{:S(2)}, u32[]{:S(2)}) collective-permute-start(bf16[128,2048]{1,0:T(8,128)(2,1)} %dynamic-slice_bitcast_fusion.1), channel_id=1, source_target_pairs={{12,8},{8,4},{4,0},{13,9},{9,5},{5,1},{14,10},{10,6},{6,2},{15,11}... | collective-permute-start | bytes 1572872 | tf_op jit(solution)/shard_map/ppermute | solution.py:38
  76.6 10.9 %copy-start.2 = (bf16[1,192,1,4096]{3,1,2,0:T(8,128)(2,1)S(1)}, bf16[1,192,1,4096]{3,1,2,0:T(8,128)(2,1)}, u32[]{:S(2)}) copy-start(bf16[1,192,1,4096]{3,1,2,0:T(8,128)(2,1)} %param.7) | copy-start | bytes 4718596
  76.6 14.4 %collective-permute-start.10 = (f32[384,128]{1,0:T(8,128)S(1)}, f32[384,128]{1,0:T(8,128)S(1)}, u32[]{:S(2)}, u32[]{:S(2)}) collective-permute-start(f32[384,128]{1,0:T(8,128)S(1)} %pad_maximum_fusion.5), channel_id=1, source_target_pairs={{0,1},{1,0},{2,3},{3,2},{4,5},{5,4},{6,7},{7,6},{8,9},{9,8},{10,11... | collective-permute-start | bytes 589832 | tf_op jit(solution)/shard_map/ppermute | solution.py:38
  89.5 12.5 %collective-permute-start.4 = (f32[384,384]{1,0:T(8,128)S(1)}, f32[384,384]{1,0:T(8,128)S(1)}, u32[]{:S(2)}, u32[]{:S(2)}) collective-permute-start(f32[384,384]{1,0:T(8,128)S(1)} %pad_maximum_fusion.3), channel_id=1, source_target_pairs={{0,1},{1,0},{2,3},{3,2},{4,5},{5,4},{6,7},{7,6},{8,9},{9,8},{10,11... | collective-permute-start | bytes 1769480 | tf_op jit(solution)/shard_map/ppermute | solution.py:38
  91.0 7.4 %collective-permute-start.11 = (f32[384,128]{1,0:T(8,128)S(1)}, f32[384,128]{1,0:T(8,128)S(1)}, u32[]{:S(2)}, u32[]{:S(2)}) collective-permute-start(f32[384,128]{1,0:T(8,128)S(1)} %fusion.41), channel_id=1, source_target_pairs={{0,2},{2,0},{1,3},{3,1},{4,6},{6,4},{5,7},{7,5},{8,10},{10,8},{9,1... | collective-permute-start | bytes 589832 | tf_op jit(solution)/shard_map/ppermute | solution.py:38
  94.1 6.1 %collective-permute-start.7 = (f32[384,128]{1,0:T(8,128)S(1)}, f32[384,128]{1,0:T(8,128)S(1)}, u32[]{:S(2)}, u32[]{:S(2)}) collective-permute-start(f32[384,128]{1,0:T(8,128)S(1)} %pad_maximum_fusion.4), channel_id=1, source_target_pairs={{0,1},{1,0},{2,3},{3,2},{4,5},{5,4},{6,7},{7,6},{8,9},{9,8},{10,11... | collective-permute-start | bytes 589832 | tf_op jit(solution)/shard_map/ppermute | solution.py:38
  98.9 27.7 %collective-permute-start.12 = (bf16[2048,128]{0,1:T(8,128)(2,1)S(1)}, bf16[2048,128]{0,1:T(8,128)(2,1)}, u32[]{:S(2)}, u32[]{:S(2)}) collective-permute-start(bf16[2048,128]{0,1:T(8,128)(2,1)S(1)} %fusion.10), channel_id=1, source_target_pairs={{0,4},{12,8},{1,5},{13,9},{2,6},{14,10},{3,7},{15,11},{16,20},{28,... | collective-permute-start | bytes 1572872 | tf_op jit(solution)/shard_map/ppermute | solution.py:38
  100.3 8.0 %collective-permute-start.8 = (f32[384,128]{1,0:T(8,128)S(1)}, f32[384,128]{1,0:T(8,128)}, u32[]{:S(2)}, u32[]{:S(2)}) collective-permute-start(f32[384,128]{1,0:T(8,128)S(1)} %fusion.42), channel_id=1, source_target_pairs={{0,2},{2,0},{1,3},{3,1},{4,6},{6,4},{5,7},{7,5},{8,10},{10,8},{9,1... | collective-permute-start | bytes 589832 | tf_op jit(solution)/shard_map/ppermute | solution.py:38
  102.0 32.5 %collective-permute-start.5 = (f32[384,384]{1,0:T(8,128)S(1)}, f32[384,384]{1,0:T(8,128)S(1)}, u32[]{:S(2)}, u32[]{:S(2)}) collective-permute-start(f32[384,384]{1,0:T(8,128)S(1)} %fusion.43), channel_id=1, source_target_pairs={{0,2},{2,0},{1,3},{3,1},{4,6},{6,4},{5,7},{7,5},{8,10},{10,8},{9,1... | collective-permute-start | bytes 1769480 | tf_op jit(solution)/shard_map/ppermute | solution.py:38
  128.4 15.0 %collective-permute-start.15 = (bf16[2048,128]{0,1:T(8,128)(2,1)S(1)}, bf16[2048,128]{0,1:T(8,128)(2,1)}, u32[]{:S(2)}, u32[]{:S(2)}) collective-permute-start(bf16[2048,128]{0,1:T(8,128)(2,1)S(1)} %fusion.7), channel_id=1, source_target_pairs={{12,8},{8,4},{13,9},{9,5},{14,10},{10,6},{15,11},{11,7},{28,24},{2... | collective-permute-start | bytes 1572872 | tf_op jit(solution)/shard_map/ppermute | solution.py:38
  129.9 16.8 %collective-permute-start.13 = (bf16[2048,128]{0,1:T(8,128)(2,1)S(1)}, bf16[2048,128]{0,1:T(8,128)(2,1)S(1)}, u32[]{:S(2)}, u32[]{:S(2)}) collective-permute-start(bf16[2048,128]{0,1:T(8,128)(2,1)S(1)} %fusion.7), channel_id=1, source_target_pairs={{0,4},{4,8},{1,5},{5,9},{2,6},{6,10},{3,7},{7,11},{16,20},{20,24},... | collective-permute-start | bytes 1572872 | tf_op jit(solution)/shard_map/ppermute | solution.py:38
  144.8 13.9 %collective-permute-start.16 = (bf16[2048,128]{0,1:T(8,128)(2,1)S(1)}, bf16[2048,128]{0,1:T(8,128)(2,1)S(1)}, u32[]{:S(2)}, u32[]{:S(2)}) collective-permute-start(bf16[2048,128]{0,1:T(8,128)(2,1)S(1)} %fusion.8), channel_id=1, source_target_pairs={{12,8},{8,4},{4,0},{13,9},{9,5},{5,1},{14,10},{10,6},{6,2},{15,11}... | collective-permute-start | bytes 1572872 | tf_op jit(solution)/shard_map/ppermute | solution.py:38
  147.2 13.9 %collective-permute-start.14 = (bf16[2048,128]{0,1:T(8,128)(2,1)S(1)}, bf16[2048,128]{0,1:T(8,128)(2,1)S(1)}, u32[]{:S(2)}, u32[]{:S(2)}) collective-permute-start(bf16[2048,128]{0,1:T(8,128)(2,1)S(1)} %fusion.6), channel_id=1, source_target_pairs={{0,4},{4,8},{8,12},{1,5},{5,9},{9,13},{2,6},{6,10},{10,14},{3,7},{... | collective-permute-start | bytes 1572872 | tf_op jit(solution)/shard_map/ppermute | solution.py:38
Sparse Core Ops, SparseCore 0:
  73.6 53.5 reduce-scatter.1

commit v2 on v1

--- a/solution.py
+++ b/solution.py
@@ -24,6 +24,10 @@
     return jnp.any(hit, axis=1).astype(jnp.float32)
 
 
+def after(value, *others):
+    return lax.optimization_barrier((value,) + others)[0]
+
+
 def shards_line(acts, err_grad, codes, dec_weight, act_ids, act_count):
     z = lax.axis_index("lat")
     x = lax.axis_index("tok")
@@ -37,31 +41,42 @@
     def send(value, axis, pairs):
         return lax.ppermute(value, axis, pairs)
 
-    w_own = lax.dynamic_slice_in_dim(dec_weight.reshape(lat, -1), x * width, width, 1)
-    w_far = send(w_own, "lat", [(0, 3), (3, 0)])
-    w_two = send(w_own, "lat", [(0, 2), (1, 3), (2, 0), (3, 1)])
-    w_prev = send(w_own, "lat", up)
-    w_next = send(w_own, "lat", down)
+    codes_own = lax.all_to_all(
+        codes.reshape(4, rows, lat), "lat", split_axis=0, concat_axis=0, tiled=True
+    )
+    codes_other = send(codes_own, "tok", swap)
+
+    codes_own, weights = lax.optimization_barrier((codes_own, dec_weight.reshape(lat, -1)))
+    w_own = lax.dynamic_slice_in_dim(weights, x * width, width, 1)
+    w_prev = send(w_own, "lat", [(i, (i + 1) % 4) for i in range(4)])
+    w_next = send(w_own, "lat", [(i, (i + 3) % 4) for i in range(4)])
 
     err = err_grad.reshape(rows, -1)
     err_own = lax.dynamic_slice_in_dim(err, x * width, width, 1)
     err_other = send(lax.dynamic_slice_in_dim(err, (1 - x) * width, width, 1), "tok", swap)
 
     ids = valid_ids(act_ids, act_count)
+    far_block = jnp.where(z == 0, 3, 0)
+    two_block = lax.rem(z + 2, 4)
+    hits = [row_hits(ids, z * rows, rows, lax.rem(z + d, 4)) for d in range(4)]
 
-    code_hits = row_hits(lax.dynamic_slice_in_dim(ids, x, 1, 0), 0, codes.shape[1], z)
-    used = codes[0] * code_hits.astype(jnp.bfloat16).T
-    codes_own = lax.all_to_all(used, "lat", split_axis=0, concat_axis=1, tiled=True)
-    codes_other = send(codes_own, "tok", swap)
-    dec_part = dot32(codes_own, err_own, CONTRACT_ROWS) + dot32(codes_other, err_other, CONTRACT_ROWS)
-    grad_dec = lax.psum_scatter(
-        dec_part.astype(jnp.bfloat16), "lat", scatter_dimension=0, tiled=True
+    def masked(value, hit):
+        return value * hit.reshape(2 * rows, 1)
+
+    all_hits = jnp.stack([row_hits(ids, z * rows, rows, block) for block in range(4)])
+    codes_own = codes_own.astype(jnp.float32) * all_hits[:, x, :, None]
+    codes_other = codes_other.astype(jnp.float32) * all_hits[:, 1 - x, :, None]
+    dec_terms = lax.dot_general(
+        codes_own.astype(jnp.bfloat16), err_own, (((1,), (0,)), ((), ())),
+        preferred_element_type=jnp.float32,
+    ) + lax.dot_general(
+        codes_other.astype(jnp.bfloat16), err_other, (((1,), (0,)), ((), ())),
+        preferred_element_type=jnp.float32,
     )
 
     act_rows = acts.reshape(2 * rows, width)
 
-    def enc_terms(weights, blocks):
-        w = jnp.concatenate(weights, axis=0) if len(weights) > 1 else weights[0]
+    def latent_grads(w, hit_list):
         part_own = dot32(err_own, w, CONTRACT_LAST)
         part_other = dot32(err_other, w, CONTRACT_LAST)
         first = jnp.where(x == 0, part_own, part_other)
@@ -69,27 +84,47 @@
         part = jnp.concatenate([first, second], axis=0)
         part = part + send(part, "sub", swap)
         part = part + send(part, "tok", swap)
-        hits = [row_hits(ids, z * rows, rows, block).reshape(2 * rows, 1) for block in blocks]
-        hits = jnp.concatenate([jnp.broadcast_to(h, (2 * rows, lat)) for h in hits], axis=1)
-        dcodes = (part * hits).astype(jnp.bfloat16)
         return [
-            dot32(act_rows, dcodes[:, i * lat : (i + 1) * lat], CONTRACT_ROWS)
-            for i in range(len(blocks))
+            masked(part[:, i * lat : (i + 1) * lat], hit).astype(jnp.bfloat16)
+            for i, hit in enumerate(hit_list)
         ]
 
-    (far,) = enc_terms([w_far], [jnp.where(z == 0, 3, 0)])
-    got_far = send(far.astype(jnp.bfloat16), "lat", [(0, 1), (3, 2)])
-    (two,) = enc_terms([w_two], [lax.rem(z + 2, 4)])
-    two = (two + got_far.astype(jnp.float32)).astype(jnp.bfloat16)
-    two_up = send(two, "lat", [(0, 1), (1, 2)])
-    two_down = send(two, "lat", [(3, 2), (2, 1)])
-    nxt, prev, own = enc_terms([w_next, w_prev, w_own], [z + 1, z - 1, z])
-    nxt = (nxt + two_up.astype(jnp.float32)).astype(jnp.bfloat16)
-    prev = (prev + two_down.astype(jnp.float32)).astype(jnp.bfloat16)
-    from_prev = send(nxt, "lat", up)
-    from_next = send(prev, "lat", down)
-    grad_enc = own + from_prev.astype(jnp.float32) + from_next.astype(jnp.float32)
-    return grad_dec[:, None, :], grad_enc.astype(jnp.bfloat16)[None]
+    def enc_of(dcodes):
+        return dot32(act_rows, dcodes, CONTRACT_ROWS)
+
+    def dec_of(block):
+        return lax.dynamic_index_in_dim(dec_terms, block, 0, keepdims=False)
+
+    def add_send(term, got, pairs):
+        value = term if got is None else term + got.astype(jnp.float32)
+        return send(value.astype(jnp.bfloat16), "lat", pairs)
+
+    far_up_down = [(0, 1), (3, 2)]
+    two_up, two_down = [(0, 1), (1, 2)], [(3, 2), (2, 1)]
+    fwd_up, fwd_down = [(1, 2), (2, 3)], [(2, 1), (1, 0)]
+
+    dec_far = add_send(dec_of(far_block), None, far_up_down)
+    w_next, w_prev = after(w_next, dec_terms), after(w_prev, dec_terms)
+    d_own, d_next, d_prev = latent_grads(
+        jnp.concatenate([w_own, w_next, w_prev], axis=0), [hits[0], hits[1], hits[3]]
+    )
+    enc_far = add_send(enc_of(jnp.where(z == 0, d_prev, d_next)), None, far_up_down)
+    w_two = jnp.where(z < 2, send(w_next, "lat", fwd_down), send(w_prev, "lat", fwd_up))
+
+    dec_two = (dec_of(two_block) + dec_far.astype(jnp.float32)).astype(jnp.bfloat16)
+    dec_up, dec_down = send(dec_two, "lat", two_up), send(dec_two, "lat", two_down)
+    (d_two,) = latent_grads(w_two, hits[2:3])
+    enc_two = (enc_of(d_two) + enc_far.astype(jnp.float32)).astype(jnp.bfloat16)
+    enc_up, enc_down = send(enc_two, "lat", two_up), send(enc_two, "lat", two_down)
+
+    dec_prev = add_send(dec_of(jnp.minimum(z + 1, 3)), dec_up, up)
+    dec_next = add_send(dec_of(jnp.maximum(z - 1, 0)), dec_down, down)
+    enc_prev = add_send(enc_of(d_next), enc_up, up)
+    enc_next = add_send(enc_of(d_prev), enc_down, down)
+
+    grad_dec = dec_of(z) + dec_prev.astype(jnp.float32) + dec_next.astype(jnp.float32)
+    grad_enc = enc_of(d_own) + enc_prev.astype(jnp.float32) + enc_next.astype(jnp.float32)
+    return grad_dec.astype(jnp.bfloat16)[:, None, :], grad_enc.astype(jnp.bfloat16)[None]
 
 
 def shards_any(acts, err_grad, codes, dec_weight, act_ids, act_count):

time: 171 us -> 136 us (0.80)
  waiting for transfers between devices: 92 us -> 50 us
  between operations: 14.4 us -> 0.99 us
  starting transfers between devices: 34.9 us -> 44.6 us
  other arithmetic: 3.57 us -> 10.5 us
  matrix products: 18.4 us -> 20.7 us
    all_to_all x1, waiting for transfers between devices: 34 us -> 0.62 us  [shards_line(): lax.all_to_all(codes.reshape(4, rows, lat), 'lat', split_axis=0, concat_a...]
    ppermute x17 -> x20, waiting for transfers between devices: 58 us -> 49.4 us  [send(): return lax.ppermute(value, axis, pairs)]
    ppermute x17 -> x20, starting transfers between devices: 31.5 us -> 39 us  [send(): return lax.ppermute(value, axis, pairs)]
    dot_general x0 -> x2, matrix products: none -> 5.02 us  [the longest x1 4.05 us: shards_line(): lax.dot_general(codes_other.astype(jnp.bfloat16), err_other, (((1,), (0,)...]
    convert_element_type x2, other arithmetic: 0.09 us -> 5.06 us  [the longest x1 2.93 us: add_send(): return send(value.astype(jnp.bfloat16), 'lat', pairs)]
    dot_general x13 -> x9, matrix products: 18.4 us -> 15.6 us  [dot32(): lax.dot_general(left, right, dims, preferred_element_type=jnp.float32)]
    broadcast_in_dim x0 -> x1, other arithmetic: none -> 2.53 us  [shards_line(): grad_dec.astype(jnp.bfloat16)[:, None, :]]
    all_to_all x1, starting transfers between devices: 3.42 us -> 5.59 us  [shards_line(): lax.all_to_all(codes.reshape(4, rows, lat), 'lat', split_axis=0, concat_a...]
  transfers between devices with their start and end apart: 19 -> 21, of which waited for: 9 -> 13; matrix products, arithmetic and copies ran while one was open for 15% -> 23% of each run, Pallas kernels for 0% -> 0%
where the time goes in v2:
time: 136 us; the launch traced here: 134 us
  waiting for transfers between devices  50 us (37%)
  starting transfers between devices  44.6 us (33%)
  matrix products  20.7 us (15%)
  other arithmetic  10.5 us (8%)
  local copies, waits for them, and re-layouts  7.49 us (6%)
    ppermute x20, waiting for transfers between devices, send(): return lax.ppermute(value, axis, pairs)  49.4 us
    ppermute x20, starting transfers between devices, send(): return lax.ppermute(value, axis, pairs)  39 us
    dot_general x9, matrix products, dot32(): lax.dot_general(left, right, dims, preferred_element_type=jnp.float32)  15.6 us
    all_to_all x1, starting transfers between devices, shards_line(): lax.all_to_all(codes.reshape(4, rows, lat), 'lat', split_axis=0, concat_a...  5.59 us
    dot_general x1, matrix products, shards_line(): lax.dot_general(codes_other.astype(jnp.bfloat16), err_other, (((1,), (0,)...  4.05 us
    convert_element_type x1, other arithmetic, add_send(): return send(value.astype(jnp.bfloat16), 'lat', pairs)  2.93 us
  transfers between devices with their start and end apart: 21, of which 13 were waited for; matrix products, arithmetic and copies ran while one was open for 23% of the time, Pallas kernels for 0%

profile of v2, /device:TPU:12, one launch (start us, length us, event | category | flops | bytes accessed | tf_op | source)
XLA Modules:
  0.0 134.2 jit_solution(18315026080464574200)
XLA Ops:
  0.7 5.6 %all-to-all-start = ((bf16[4,192,128]{2,1,0:T(8,128)(2,1)}), bf16[4,192,128]{2,1,0:T(8,128)(2,1)S(1)}, u32[]{:S(2)}, u32[]{:S(2)}) async-start(bf16[4,192,128]{2,1,0:T(8,128)(2,1)} %bitcast.100), calls=%async_computation | async-start | bytes 393216 | tf_op jit(solution)/shard_map/all_to_all | solution.py:44
  6.3 2.1 %dynamic-slice_bitcast_fusion = bf16[192,2048]{1,0:T(8,128)(2,1)} fusion(bf16[1,192,1,4096]{3,1,2,0:T(8,128)(2,1)} %param.7, s32[]{:T(128)S(6)} %select_n.95), kind=kLoop, calls=%fused_computation.35 | loop fusion | bytes 1572868 | tf_op jit(solution)/shard_map/dynamic_slice | solution.py:56
  17.8 13.7 %collective-permute-done = bf16[4,192,128]{2,1,0:T(8,128)(2,1)S(1)} collective-permute-done((bf16[4,192,128]{2,1,0:T(8,128)(2,1)S(1)}, bf16[4,192,128]{2,1,0:T(8,128)(2,1)S(1)}, u32[]{:S(2)}, u32[]{:S(2)}) %collective-permute-start) | collective-permute-done | bytes 196640 | tf_op jit(solution)/shard_map/ppermute | solution.py:42
  31.5 4.1 %convolution_add_fusion = f32[4,128,2048]{2,1,0:T(8,128)} fusion(f32[4,128,2048]{2,1,0:T(8,128)S(1)} %fusion.16, bf16[192,2048]{1,0:T(8,128)(2,1)} %collective-permute-done.1, bf16[4,192,128]{2,1,0:T(8,128)(2,1)S(1)} %collective-permute-done, f32[4,192]{1,0:T(4,128)S(1)} %bitcast.101), kind=kOutput, calls=%fused_computation | convolution fusion | flops 403996672 | bytes 9374720 | tf_op jit(solution)/shard_map/dot_general | solution.py:72
  35.6 2.1 %collective-permute-done.7 = bf16[128,2048]{1,0:T(8,128)(2,1)} collective-permute-done((bf16[128,2048]{1,0:T(8,128)(2,1)S(1)}, bf16[128,2048]{1,0:T(8,128)(2,1)}, u32[]{:S(2)}, u32[]{:S(2)}) %collective-permute-start.7) | collective-permute-done | bytes 524320 | tf_op jit(solution)/shard_map/ppermute | solution.py:42
  37.7 2.1 %fusion.23 = f32[192,384]{1,0:T(8,128)S(1)} fusion(bf16[192,2048]{1,0:T(8,128)(2,1)} %collective-permute-done.1, bf16[128,2048]{1,0:T(8,128)(2,1)} %collective-permute-done.8, bf16[128,2048]{1,0:T(8,128)(2,1)} %collective-permute-done.7, bf16[128,2048]{1,0:T(8,128)(2,1)S(1)} %constant_dynamic-slice_fusion), kind=kOutput, calls=%fused_computation.36 | convolution fusion | flops 306708480 | bytes 2654208 | tf_op jit(solution)/shard_map/dot_general | solution.py:12
  43.3 2.9 %collective-permute-start.11 = (bf16[128,2048]{1,0:T(8,128)(2,1)}, bf16[128,2048]{1,0:T(8,128)(2,1)}, u32[]{:S(2)}, u32[]{:S(2)}) collective-permute-start(bf16[128,2048]{1,0:T(8,128)(2,1)} %collective-permute-done.7), channel_id=1, source_target_pairs={{8,4},{4,0},{9,5},{5,1},{10,6},{6,2},{11,7},{7,3},{24,20},{20,16},... | collective-permute-start | bytes 1572872 | tf_op jit(solution)/shard_map/ppermute | solution.py:42
  46.1 4.5 %collective-permute-start.12 = (bf16[128,2048]{1,0:T(8,128)(2,1)}, bf16[128,2048]{1,0:T(8,128)(2,1)}, u32[]{:S(2)}, u32[]{:S(2)}) collective-permute-start(bf16[128,2048]{1,0:T(8,128)(2,1)} %collective-permute-done.8), channel_id=1, source_target_pairs={{4,8},{8,12},{5,9},{9,13},{6,10},{10,14},{7,11},{11,15},{20,24},{2... | collective-permute-start | bytes 1572872 | tf_op jit(solution)/shard_map/ppermute | solution.py:42
  56.2 3.6 %collective-permute-done.11 = bf16[128,2048]{1,0:T(8,128)(2,1)} collective-permute-done((bf16[128,2048]{1,0:T(8,128)(2,1)}, bf16[128,2048]{1,0:T(8,128)(2,1)}, u32[]{:S(2)}, u32[]{:S(2)}) %collective-permute-start.11) | collective-permute-done | bytes 524320 | tf_op jit(solution)/shard_map/ppermute | solution.py:42
  59.8 2.0 %collective-permute-done.12 = bf16[128,2048]{1,0:T(8,128)(2,1)} collective-permute-done((bf16[128,2048]{1,0:T(8,128)(2,1)}, bf16[128,2048]{1,0:T(8,128)(2,1)}, u32[]{:S(2)}, u32[]{:S(2)}) %collective-permute-start.12) | collective-permute-done | bytes 524320 | tf_op jit(solution)/shard_map/ppermute | solution.py:42
  64.9 4.9 %collective-permute-done.10 = f32[384,384]{1,0:T(8,128)S(1)} collective-permute-done((f32[384,384]{1,0:T(8,128)S(1)}, f32[384,384]{1,0:T(8,128)S(1)}, u32[]{:S(2)}, u32[]{:S(2)}) %collective-permute-start.10) | collective-permute-done | bytes 589856 | tf_op jit(solution)/shard_map/ppermute | solution.py:42
  72.7 2.1 %fusion.12 = bf16[128,2048]{1,0:T(8,128)(2,1)} fusion(bf16[128,2048]{1,0:T(8,128)(2,1)S(1)} %collective-permute-done.2, f32[4,128,2048]{2,1,0:T(8,128)} %convolution_add_fusion, s32[]{:T(128)S(6)} %select_n.98), kind=kLoop, calls=%fused_computation.21 | loop fusion | flops 786432 | bytes 2097156 | tf_op jit(solution)/shard_map/convert_element_type | solution.py:114
  79.7 4.3 %collective-permute-done.14 = f32[384,128]{1,0:T(8,128)S(1)} collective-permute-done((f32[384,128]{1,0:T(8,128)S(1)}, f32[384,128]{1,0:T(8,128)S(1)}, u32[]{:S(2)}, u32[]{:S(2)}) %collective-permute-start.14) | collective-permute-done | bytes 196640 | tf_op jit(solution)/shard_map/ppermute | solution.py:42
  84.0 4.4 %collective-permute-done.15 = bf16[2048,128]{0,1:T(8,128)(2,1)} collective-permute-done((bf16[2048,128]{0,1:T(8,128)(2,1)}, bf16[2048,128]{0,1:T(8,128)(2,1)}, u32[]{:S(2)}, u32[]{:S(2)}) %collective-permute-start.15) | collective-permute-done | bytes 524320 | tf_op jit(solution)/shard_map/ppermute | solution.py:42
  88.4 2.4 %fusion.7 = bf16[2048,128]{0,1:T(8,128)(2,1)} fusion(bf16[384,2048]{1,0:T(8,128)(2,1)S(1)} %bitcast.96, bf16[2048,128]{0,1:T(8,128)(2,1)} %collective-permute-done.15, f32[384,128]{1,0:T(8,128)S(1)} %fusion.49, f32[384,128]{1,0:T(8,128)S(1)} %collective-permute-done.14, f32[384]{0:T(512)S(1)} %reshape.144), kind=kOutput, calls=%fused_computation.12 | convolution fusion | flops 202260480 | bytes 3016192 | tf_op jit(solution)/shard_map/dot_general | solution.py:12
  92.1 4.6 %collective-permute-start.16 = (bf16[2048,128]{0,1:T(8,128)(2,1)}, bf16[2048,128]{0,1:T(8,128)(2,1)S(1)}, u32[]{:S(2)}, u32[]{:S(2)}) collective-permute-start(bf16[2048,128]{0,1:T(8,128)(2,1)} %fusion.7), channel_id=1, source_target_pairs={{0,4},{4,8},{1,5},{5,9},{2,6},{6,10},{3,7},{7,11},{16,20},{20,24},... | collective-permute-start | bytes 1572872 | tf_op jit(solution)/shard_map/ppermute | solution.py:42
  96.7 2.9 %collective-permute-done.3 = bf16[128,2048]{1,0:T(8,128)(2,1)S(1)} collective-permute-done((bf16[128,2048]{1,0:T(8,128)(2,1)}, bf16[128,2048]{1,0:T(8,128)(2,1)S(1)}, u32[]{:S(2)}, u32[]{:S(2)}) %collective-permute-start.3) | collective-permute-done | bytes 524320 | tf_op jit(solution)/shard_map/ppermute | solution.py:42
  99.5 2.9 %fusion.13 = (bf16[128,2048]{1,0:T(8,128)(2,1)}, bf16[128,2048]{1,0:T(8,128)(2,1)}) fusion(bf16[128,2048]{1,0:T(8,128)(2,1)S(1)} %collective-permute-done.3, f32[4,128,2048]{2,1,0:T(8,128)} %convolution_add_fusion, s32[]{:T(128)S(6)} %select_n.97, bf16[128,2048]{1,0:T(8,128)(2,1)} %collective-permute-done.5, s32[]{:T(128)S(6)} %max.3), kind=kLoop, calls=%fused_computation.23 | loop fusion | flops 1572864 | bytes 4194312 | tf_op jit(solution)/shard_map/convert_element_type | solution.py:100
  104.4 3.9 %collective-permute-start.4 = (bf16[128,2048]{1,0:T(8,128)(2,1)}, bf16[128,2048]{1,0:T(8,128)(2,1)}, u32[]{:S(2)}, u32[]{:S(2)}) collective-permute-start(bf16[128,2048]{1,0:T(8,128)(2,1)} %get-tuple-element.34), channel_id=1, source_target_pairs={{0,4},{4,8},{8,12},{1,5},{5,9},{9,13},{2,6},{6,10},{10,14},{3,7},{... | collective-permute-start | bytes 1572872 | tf_op jit(solution)/shard_map/ppermute | solution.py:42
  109.9 2.7 %collective-permute-start.19 = (bf16[2048,128]{0,1:T(8,128)(2,1)S(1)}, bf16[2048,128]{0,1:T(8,128)(2,1)}, u32[]{:S(2)}, u32[]{:S(2)}) collective-permute-start(bf16[2048,128]{0,1:T(8,128)(2,1)S(1)} %fusion.8), channel_id=1, source_target_pairs={{12,8},{8,4},{4,0},{13,9},{9,5},{5,1},{14,10},{10,6},{6,2},{15,11}... | collective-permute-start | bytes 1572872 | tf_op jit(solution)/shard_map/ppermute | solution.py:42
  114.1 3.2 %collective-permute-start.17 = (bf16[2048,128]{0,1:T(8,128)(2,1)}, bf16[2048,128]{0,1:T(8,128)(2,1)}, u32[]{:S(2)}, u32[]{:S(2)}) collective-permute-start(bf16[2048,128]{0,1:T(8,128)(2,1)} %fusion.6), channel_id=1, source_target_pairs={{0,4},{4,8},{8,12},{1,5},{5,9},{9,13},{2,6},{6,10},{10,14},{3,7},{... | collective-permute-start | bytes 1572872 | tf_op jit(solution)/shard_map/ppermute | solution.py:42
  117.6 4.5 %collective-permute-done.4 = bf16[128,2048]{1,0:T(8,128)(2,1)} collective-permute-done((bf16[128,2048]{1,0:T(8,128)(2,1)}, bf16[128,2048]{1,0:T(8,128)(2,1)}, u32[]{:S(2)}, u32[]{:S(2)}) %collective-permute-start.4) | collective-permute-done | bytes 524320 | tf_op jit(solution)/shard_map/ppermute | solution.py:42
  122.1 2.5 %fusion.28 = bf16[128,1,2048]{2,0,1:T(8,128)(2,1)} fusion(bf16[128,2048]{1,0:T(8,128)(2,1)} %collective-permute-done.6, bf16[128,2048]{1,0:T(8,128)(2,1)} %collective-permute-done.4, f32[4,128,2048]{2,1,0:T(8,128)} %convolution_add_fusion, s32[]{:T(128)S(6)} %select_n.96), kind=kLoop, calls=%fused_computation.42 | loop fusion | flops 1310720 | bytes 2621444 | tf_op jit(solution)/shard_map/broadcast_in_dim | solution.py:127
  125.9 5.5 %collective-permute-done.17 = bf16[2048,128]{0,1:T(8,128)(2,1)} collective-permute-done((bf16[2048,128]{0,1:T(8,128)(2,1)}, bf16[2048,128]{0,1:T(8,128)(2,1)}, u32[]{:S(2)}, u32[]{:S(2)}) %collective-permute-start.17) | collective-permute-done | bytes 524320 | tf_op jit(solution)/shard_map/ppermute | solution.py:42
  (76 shorter events, 39.8 us)
Async XLA Ops:
  0.6 69.3 %copy-start = (bf16[2,192,1,2048]{3,1,2,0:T(8,128)(2,1)S(1)}, bf16[2,192,1,2048]{3,1,2,0:T(8,128)(2,1)}, u32[]{:S(2)}) copy-start(bf16[2,192,1,2048]{3,1,2,0:T(8,128)(2,1)} %param.6) | copy-start | bytes 4718596
  0.7 9.3 %copy-start.3 = (s32[2,3,3]{2,0,1:T(2,128)S(1)}, s32[2,3,3]{2,0,1:T(2,128)}, u32[]{:S(2)}) copy-start(s32[2,3,3]{2,0,1:T(2,128)} %param.10) | copy-start | bytes 220
  0.7 16.2 %copy-start.1 = (bf16[1,192,1,4096]{3,1,2,0:T(8,128)(2,1)S(1)}, bf16[1,192,1,4096]{3,1,2,0:T(8,128)(2,1)}, u32[]{:S(2)}) copy-start(bf16[1,192,1,4096]{3,1,2,0:T(8,128)(2,1)} %param.7) | copy-start | bytes 4718596
  0.7 11.5 %all-to-all-start = ((bf16[4,192,128]{2,1,0:T(8,128)(2,1)}), bf16[4,192,128]{2,1,0:T(8,128)(2,1)S(1)}, u32[]{:S(2)}, u32[]{:S(2)}) async-start(bf16[4,192,128]{2,1,0:T(8,128)(2,1)} %bitcast.100), calls=%async_computation | async-start | bytes 393216 | tf_op jit(solution)/shard_map/all_to_all | solution.py:44
  8.4 23.1 %collective-permute-start.1 = (bf16[192,2048]{1,0:T(8,128)(2,1)}, bf16[192,2048]{1,0:T(8,128)(2,1)}, u32[]{:S(2)}, u32[]{:S(2)}) collective-permute-start(bf16[192,2048]{1,0:T(8,128)(2,1)} %dynamic-slice_bitcast_fusion), channel_id=1, source_target_pairs={{0,2},{2,0},{1,3},{3,1},{4,6},{6,4},{5,7},{7,5},{8,10},{10,8},{9,1... | collective-permute-start | bytes 2359304 | tf_op jit(solution)/shard_map/ppermute | solution.py:42
  13.3 22.3 %collective-permute-start.8 = (bf16[128,2048]{1,0:T(8,128)(2,1)S(1)}, bf16[128,2048]{1,0:T(8,128)(2,1)}, u32[]{:S(2)}, u32[]{:S(2)}) collective-permute-start(bf16[128,2048]{1,0:T(8,128)(2,1)S(1)} %constant_dynamic-slice_fusion), channel_id=1, source_target_pairs={{0,4},{4,8},{8,12},{12,0},{1,5},{5,9},{9,13},{13,1},{2,6},{6,10},{... | collective-permute-start | bytes 1572872 | tf_op jit(solution)/shard_map/ppermute | solution.py:42
  14.2 23.5 %collective-permute-start.7 = (bf16[128,2048]{1,0:T(8,128)(2,1)S(1)}, bf16[128,2048]{1,0:T(8,128)(2,1)}, u32[]{:S(2)}, u32[]{:S(2)}) collective-permute-start(bf16[128,2048]{1,0:T(8,128)(2,1)S(1)} %constant_dynamic-slice_fusion), channel_id=1, source_target_pairs={{0,12},{4,0},{8,4},{12,8},{1,13},{5,1},{9,5},{13,9},{2,14},{6,2},{... | collective-permute-start | bytes 1572872 | tf_op jit(solution)/shard_map/ppermute | solution.py:42
  15.4 16.1 %collective-permute-start = (bf16[4,192,128]{2,1,0:T(8,128)(2,1)S(1)}, bf16[4,192,128]{2,1,0:T(8,128)(2,1)S(1)}, u32[]{:S(2)}, u32[]{:S(2)}) collective-permute-start(bf16[4,192,128]{2,1,0:T(8,128)(2,1)S(1)} %all-to-all-done), channel_id=1, source_target_pairs={{0,2},{2,0},{1,3},{3,1},{4,6},{6,4},{5,7},{7,5},{8,10},{10,8},{9,1... | collective-permute-start | bytes 589832 | tf_op jit(solution)/shard_map/ppermute | solution.py:42
  43.2 10.2 %collective-permute-start.9 = (f32[384,384]{1,0:T(8,128)}, f32[384,384]{1,0:T(8,128)}, u32[]{:S(2)}, u32[]{:S(2)}) collective-permute-start(f32[384,384]{1,0:T(8,128)} %pad_maximum_fusion.3), channel_id=1, source_target_pairs={{0,1},{1,0},{2,3},{3,2},{4,5},{5,4},{6,7},{7,6},{8,9},{9,8},{10,11... | collective-permute-start | bytes 1769480 | tf_op jit(solution)/shard_map/ppermute | solution.py:42
  43.3 16.5 %collective-permute-start.11 = (bf16[128,2048]{1,0:T(8,128)(2,1)}, bf16[128,2048]{1,0:T(8,128)(2,1)}, u32[]{:S(2)}, u32[]{:S(2)}) collective-permute-start(bf16[128,2048]{1,0:T(8,128)(2,1)} %collective-permute-done.7), channel_id=1, source_target_pairs={{8,4},{4,0},{9,5},{5,1},{10,6},{6,2},{11,7},{7,3},{24,20},{20,16},... | collective-permute-start | bytes 1572872 | tf_op jit(solution)/shard_map/ppermute | solution.py:42
  46.1 15.6 %collective-permute-start.12 = (bf16[128,2048]{1,0:T(8,128)(2,1)}, bf16[128,2048]{1,0:T(8,128)(2,1)}, u32[]{:S(2)}, u32[]{:S(2)}) collective-permute-start(bf16[128,2048]{1,0:T(8,128)(2,1)} %collective-permute-done.8), channel_id=1, source_target_pairs={{4,8},{8,12},{5,9},{9,13},{6,10},{10,14},{7,11},{11,15},{20,24},{2... | collective-permute-start | bytes 1572872 | tf_op jit(solution)/shard_map/ppermute | solution.py:42
  52.1 20.5 %collective-permute-start.2 = (bf16[128,2048]{1,0:T(8,128)(2,1)S(1)}, bf16[128,2048]{1,0:T(8,128)(2,1)S(1)}, u32[]{:S(2)}, u32[]{:S(2)}) collective-permute-start(bf16[128,2048]{1,0:T(8,128)(2,1)S(1)} %fusion.27), channel_id=1, source_target_pairs={{0,4},{12,8},{1,5},{13,9},{2,6},{14,10},{3,7},{15,11},{16,20},{28,... | collective-permute-start | bytes 1572872 | tf_op jit(solution)/shard_map/ppermute | solution.py:42
  54.7 15.2 %collective-permute-start.10 = (f32[384,384]{1,0:T(8,128)S(1)}, f32[384,384]{1,0:T(8,128)S(1)}, u32[]{:S(2)}, u32[]{:S(2)}) collective-permute-start(f32[384,384]{1,0:T(8,128)S(1)} %fusion.50), channel_id=1, source_target_pairs={{0,2},{2,0},{1,3},{3,1},{4,6},{6,4},{5,7},{7,5},{8,10},{10,8},{9,1... | collective-permute-start | bytes 1769480 | tf_op jit(solution)/shard_map/ppermute | solution.py:42
  64.9 13.1 %collective-permute-start.13 = (f32[384,128]{1,0:T(8,128)S(1)}, f32[384,128]{1,0:T(8,128)S(1)}, u32[]{:S(2)}, u32[]{:S(2)}) collective-permute-start(f32[384,128]{1,0:T(8,128)S(1)} %pad_maximum_fusion.4), channel_id=1, source_target_pairs={{0,1},{1,0},{2,3},{3,2},{4,5},{5,4},{6,7},{7,6},{8,9},{9,8},{10,11... | collective-permute-start | bytes 589832 | tf_op jit(solution)/shard_map/ppermute | solution.py:42
  71.4 17.1 %collective-permute-start.15 = (bf16[2048,128]{0,1:T(8,128)(2,1)}, bf16[2048,128]{0,1:T(8,128)(2,1)}, u32[]{:S(2)}, u32[]{:S(2)}) collective-permute-start(bf16[2048,128]{0,1:T(8,128)(2,1)} %fusion.10), channel_id=1, source_target_pairs={{0,4},{12,8},{1,5},{13,9},{2,6},{14,10},{3,7},{15,11},{16,20},{28,... | collective-permute-start | bytes 1572872 | tf_op jit(solution)/shard_map/ppermute | solution.py:42
  74.8 24.8 %collective-permute-start.3 = (bf16[128,2048]{1,0:T(8,128)(2,1)}, bf16[128,2048]{1,0:T(8,128)(2,1)S(1)}, u32[]{:S(2)}, u32[]{:S(2)}) collective-permute-start(bf16[128,2048]{1,0:T(8,128)(2,1)} %fusion.12), channel_id=1, source_target_pairs={{0,4},{4,8},{1,5},{5,9},{2,6},{6,10},{3,7},{7,11},{16,20},{20,24},... | collective-permute-start | bytes 1572872 | tf_op jit(solution)/shard_map/ppermute | solution.py:42
  76.7 22.8 %collective-permute-start.5 = (bf16[128,2048]{1,0:T(8,128)(2,1)}, bf16[128,2048]{1,0:T(8,128)(2,1)}, u32[]{:S(2)}, u32[]{:S(2)}) collective-permute-start(bf16[128,2048]{1,0:T(8,128)(2,1)} %fusion.12), channel_id=1, source_target_pairs={{12,8},{8,4},{13,9},{9,5},{14,10},{10,6},{15,11},{11,7},{28,24},{2... | collective-permute-start | bytes 1572872 | tf_op jit(solution)/shard_map/ppermute | solution.py:42
  78.0 5.9 %collective-permute-start.14 = (f32[384,128]{1,0:T(8,128)S(1)}, f32[384,128]{1,0:T(8,128)S(1)}, u32[]{:S(2)}, u32[]{:S(2)}) collective-permute-start(f32[384,128]{1,0:T(8,128)S(1)} %fusion.49), channel_id=1, source_target_pairs={{0,2},{2,0},{1,3},{3,1},{4,6},{6,4},{5,7},{7,5},{8,10},{10,8},{9,1... | collective-permute-start | bytes 589832 | tf_op jit(solution)/shard_map/ppermute | solution.py:42
  90.8 17.5 %collective-permute-start.18 = (bf16[2048,128]{0,1:T(8,128)(2,1)}, bf16[2048,128]{0,1:T(8,128)(2,1)}, u32[]{:S(2)}, u32[]{:S(2)}) collective-permute-start(bf16[2048,128]{0,1:T(8,128)(2,1)} %fusion.7), channel_id=1, source_target_pairs={{12,8},{8,4},{13,9},{9,5},{14,10},{10,6},{15,11},{11,7},{28,24},{2... | collective-permute-start | bytes 1572872 | tf_op jit(solution)/shard_map/ppermute | solution.py:42
  92.1 20.6 %collective-permute-start.16 = (bf16[2048,128]{0,1:T(8,128)(2,1)}, bf16[2048,128]{0,1:T(8,128)(2,1)S(1)}, u32[]{:S(2)}, u32[]{:S(2)}) collective-permute-start(bf16[2048,128]{0,1:T(8,128)(2,1)} %fusion.7), channel_id=1, source_target_pairs={{0,4},{4,8},{1,5},{5,9},{2,6},{6,10},{3,7},{7,11},{16,20},{20,24},... | collective-permute-start | bytes 1572872 | tf_op jit(solution)/shard_map/ppermute | solution.py:42
  102.5 15.1 %collective-permute-start.6 = (bf16[128,2048]{1,0:T(8,128)(2,1)}, bf16[128,2048]{1,0:T(8,128)(2,1)}, u32[]{:S(2)}, u32[]{:S(2)}) collective-permute-start(bf16[128,2048]{1,0:T(8,128)(2,1)} %get-tuple-element.35), channel_id=1, source_target_pairs={{12,8},{8,4},{4,0},{13,9},{9,5},{5,1},{14,10},{10,6},{6,2},{15,11}... | collective-permute-start | bytes 1572872 | tf_op jit(solution)/shard_map/ppermute | solution.py:42
  104.4 17.7 %collective-permute-start.4 = (bf16[128,2048]{1,0:T(8,128)(2,1)}, bf16[128,2048]{1,0:T(8,128)(2,1)}, u32[]{:S(2)}, u32[]{:S(2)}) collective-permute-start(bf16[128,2048]{1,0:T(8,128)(2,1)} %get-tuple-element.34), channel_id=1, source_target_pairs={{0,4},{4,8},{8,12},{1,5},{5,9},{9,13},{2,6},{6,10},{10,14},{3,7},{... | collective-permute-start | bytes 1572872 | tf_op jit(solution)/shard_map/ppermute | solution.py:42
  109.9 16.0 %collective-permute-start.19 = (bf16[2048,128]{0,1:T(8,128)(2,1)S(1)}, bf16[2048,128]{0,1:T(8,128)(2,1)}, u32[]{:S(2)}, u32[]{:S(2)}) collective-permute-start(bf16[2048,128]{0,1:T(8,128)(2,1)S(1)} %fusion.8), channel_id=1, source_target_pairs={{12,8},{8,4},{4,0},{13,9},{9,5},{5,1},{14,10},{10,6},{6,2},{15,11}... | collective-permute-start | bytes 1572872 | tf_op jit(solution)/shard_map/ppermute | solution.py:42
  114.1 17.3 %collective-permute-start.17 = (bf16[2048,128]{0,1:T(8,128)(2,1)}, bf16[2048,128]{0,1:T(8,128)(2,1)}, u32[]{:S(2)}, u32[]{:S(2)}) collective-permute-start(bf16[2048,128]{0,1:T(8,128)(2,1)} %fusion.6), channel_id=1, source_target_pairs={{0,4},{4,8},{8,12},{1,5},{5,9},{9,13},{2,6},{6,10},{10,14},{3,7},{... | collective-permute-start | bytes 1572872 | tf_op jit(solution)/shard_map/ppermute | solution.py:42
  (2 other events, 9.9 us)

commit v3 on v1

v3 whole, which is shorter than its diff:
```python
import functools

import jax
import jax.numpy as jnp
from jax import lax
from jax.experimental import pallas as pl
from jax.experimental.pallas import tpu as pltpu
from jax.sharding import PartitionSpec as P

TBLK = 256
MERGED = False
ORDER = {
    "dec_down": ("enc_two",),
    "dec_far": ("enc_far_in",),
    "dec_up": ("enc_two",),
    "tok_near": ("up", "down",),
    "tok_two": ("dec_two",),
    "w_next": ("dec",),
    "w_next_in": ("codes",),
    "w_prev": ("dec",),
}
CONTRACT_LAST = (((1,), (1,)), ((), ()))
PLAIN = (((1,), (0,)), ((), ()))
CONTRACT_ROWS = (((0,), (0,)), ((), ()))


def dot32(left, right, dims):
    return lax.dot_general(left, right, dims, preferred_element_type=jnp.float32)


def local_call(body, out_shape, scalars, *args):
    vmem = pl.BlockSpec(memory_space=pltpu.VMEM)
    return pl.pallas_call(
        body,
        out_shape=out_shape,
        in_specs=[pl.BlockSpec(memory_space=pltpu.SMEM)] + [vmem] * len(args),
        out_specs=jax.tree.map(lambda _: vmem, out_shape),
        compiler_params=pltpu.CompilerParams(vmem_limit_bytes=32 * 2**20),
        cost_estimate=pl.CostEstimate(flops=0, bytes_accessed=0, transcendentals=0),
    )(jnp.stack(scalars).astype(jnp.int32), *args)


def turned(value):
    return value.astype(jnp.float32).T.astype(jnp.bfloat16)


def dec_body(far_ref, own_ref, other_ref, err_own_ref, err_other_ref, out_ref, first_ref):
    for j in range(out_ref.shape[0]):
        out_ref[j] = dot32(turned(own_ref[j]), err_own_ref[...], PLAIN) + dot32(
            turned(other_ref[j]), err_other_ref[...], PLAIN
        )
    first_ref[...] = out_ref[far_ref[0]].astype(jnp.bfloat16)


def dlat_body(place_ref, own_ref, other_ref, *refs):
    place, out_ref = place_ref[0], refs[-1]
    for i, w_ref in enumerate(refs[:-1]):
        lanes = slice(i * w_ref.shape[0], (i + 1) * w_ref.shape[0])
        out_ref[place, :, lanes] = dot32(own_ref[...], w_ref[...], CONTRACT_LAST)
        out_ref[1 - place, :, lanes] = dot32(other_ref[...], w_ref[...], CONTRACT_LAST)


def enc_body(core_ref, acts_ref, mine_ref, other_ref, out_ref):
    core = core_ref[0]
    total = dot32(turned(mine_ref[...]), acts_ref[core], PLAIN)
    total += dot32(turned(other_ref[...]), acts_ref[1 - core], PLAIN)
    out_ref[...] = total.astype(out_ref.dtype)


def valid_ids(act_ids, act_count):
    slot = jnp.arange(act_ids.shape[2], dtype=jnp.int32)
    return jnp.where(slot[None, None, :] < act_count[:, :, None], act_ids, -1)


def row_hits(ids, first_row, rows, block):
    on = jnp.any(ids == block, axis=2)
    tile = (first_row + jnp.arange(rows, dtype=jnp.int32)) // TBLK
    hit = on[:, :, None] & (tile[None, None, :] == jnp.arange(ids.shape[1])[None, :, None])
    return jnp.any(hit, axis=1).astype(jnp.float32)


def shards_line(acts, err_grad, codes, dec_weight, act_ids, act_count):
    z = lax.axis_index("lat")
    x = lax.axis_index("tok")
    c = lax.axis_index("sub")
    rows = err_grad.shape[1]
    lat = dec_weight.shape[0]
    width = acts.shape[3]
    swap = [(0, 1), (1, 0)]
    ring = [(0, 1), (1, 2), (2, 3), (3, 0)]
    up, down = [(0, 1), (1, 2), (2, 3)], [(3, 2), (2, 1), (1, 0)]
    up_two, down_two = [(0, 1), (1, 2)], [(3, 2), (2, 1)]
    up_on, down_on = [(1, 2), (2, 3)], [(2, 1), (1, 0)]
    inward = [(0, 1), (3, 2)]

    ids = valid_ids(act_ids, act_count)
    far_block = jnp.where(z == 0, 3, 0)
    two_block = lax.rem(z + 2, 4)
    act_rows = acts.reshape(2, rows, width)
    err_rows = err_grad.reshape(rows, -1)
    block = jax.ShapeDtypeStruct((lat, width), jnp.float32)
    block16 = jax.ShapeDtypeStruct((lat, width), jnp.bfloat16)
    steps, done = {}, {}

    def get(name):
        if name not in done:
            value = steps[name]()
            others = [get(other) for other in ORDER.get(name, ())]
            done[name] = lax.optimization_barrier((value, *others))[0] if others else value
        return done[name]

    def step(name, make):
        steps[name] = make

    def send(name, source, axis, pairs):
        step(name + "_in", source)
        step(name, lambda: lax.ppermute(get(name + "_in"), axis, pairs))

    def add32(term, got):
        return (term + got.astype(jnp.float32)).astype(jnp.bfloat16)

    step("weights", lambda: dec_weight.reshape(lat, -1))
    step("w_own", lambda: lax.dynamic_slice_in_dim(get("weights"), x * width, width, 1))
    send("w_prev", lambda: get("w_own"), "lat", ring)
    send("w_next", lambda: get("w_own"), "lat", [(b, a) for a, b in ring])

    step("err_own", lambda: lax.dynamic_slice_in_dim(err_rows, x * width, width, 1))
    send("err", lambda: lax.dynamic_slice_in_dim(err_rows, (1 - x) * width, width, 1), "tok", swap)

    step("codes_in", lambda: codes.reshape(4, rows, lat))
    step("codes", lambda: lax.all_to_all(get("codes_in"), "lat", split_axis=0, concat_axis=0, tiled=True))
    send("codes_other", lambda: get("codes"), "tok", swap)

    def used(value, group):
        all_hits = jnp.stack([row_hits(ids, z * rows, rows, b) for b in range(4)])
        hit = lax.dynamic_index_in_dim(all_hits, group, 1, keepdims=False)
        return value * hit[:, :, None].astype(jnp.bfloat16)

    step("used_own", lambda: used(get("codes"), x))
    step(
        "dec",
        lambda: local_call(
            dec_body,
            (jax.ShapeDtypeStruct((4, lat, width), jnp.float32), block16),
            [far_block], get("used_own"), used(get("codes_other"), 1 - x), get("err_own"), get("err"),
        ),
    )

    def dec_of(b):
        return lax.dynamic_index_in_dim(get("dec")[0], b, 0, keepdims=False)

    if MERGED:
        send("up", lambda: jnp.where(z == 0, get("dec")[1], get("w_prev")), "lat", up)
        send("down", lambda: jnp.where(z == 3, get("dec")[1], get("w_next")), "lat", down)

        def far_term():
            got = jnp.where(z == 1, get("up"), get("down"))
            return jnp.where((z == 1) | (z == 2), got, jnp.zeros((), jnp.bfloat16))

        step("dec_far", far_term)
    else:
        send("up", lambda: get("w_prev"), "lat", up_on)
        send("down", lambda: get("w_next"), "lat", down_on)
        send("dec_far", lambda: get("dec")[1], "lat", inward)
    step("w_two", lambda: jnp.where(z < 2, get("down"), get("up")))

    def latent_grads(tag, names, blocks):
        def part():
            weights = [get(name) for name in names]
            out = jax.ShapeDtypeStruct((2, rows, lat * len(weights)), jnp.float32)
            return local_call(dlat_body, out, [c ^ x], get("err_own"), get("err"), *weights)

        def mine():
            total, cols = get("sums" + tag) + get("tok" + tag), []
            for i, b in enumerate(blocks):
                hit = lax.dynamic_index_in_dim(row_hits(ids, z * rows, rows, b), c, 0, keepdims=False)
                cols.append((total[:, i * lat : (i + 1) * lat] * hit[:, None]).astype(jnp.bfloat16))
            return jnp.concatenate(cols, axis=1)

        step("part" + tag, part)
        send("sub" + tag, lambda: get("part" + tag)[1], "sub", swap)
        step("sums" + tag, lambda: get("part" + tag)[0] + get("sub" + tag))
        send("tok" + tag, lambda: get("sums" + tag), "tok", swap)
        step("mine" + tag, mine)
        send("other" + tag, lambda: get("mine" + tag), "sub", swap)

    latent_grads("_near", ["w_own", "w_next", "w_prev"], [z, lax.rem(z + 1, 4), lax.rem(z + 3, 4)])
    latent_grads("_two", ["w_two"], [two_block])

    def enc_of(tag, pick, out=block):
        return local_call(enc_body, out, [c], act_rows, pick(get("mine" + tag)), pick(get("other" + tag)))

    def near(i):
        return lambda part: part[:, i * lat : (i + 1) * lat]

    send(
        "enc_far",
        lambda: enc_of("_near", lambda part: jnp.where(z == 0, near(2)(part), near(1)(part)), block16),
        "lat", inward,
    )
    step("dec_two", lambda: add32(dec_of(two_block), get("dec_far")))
    step("enc_two", lambda: add32(enc_of("_two", near(0)), get("enc_far")))
    for kind in ("dec", "enc"):
        send(kind + "_up", functools.partial(get, kind + "_two"), "lat", up_two)
        send(kind + "_down", functools.partial(get, kind + "_two"), "lat", down_two)
    send("dec_prev", lambda: add32(dec_of(jnp.minimum(z + 1, 3)), get("dec_up")), "lat", up)
    send("dec_next", lambda: add32(dec_of(jnp.maximum(z - 1, 0)), get("dec_down")), "lat", down)
    send("enc_prev", lambda: add32(enc_of("_near", near(1)), get("enc_up")), "lat", up)
    send("enc_next", lambda: add32(enc_of("_near", near(2)), get("enc_down")), "lat", down)
    step("dec_own", lambda: dec_of(z))
    step("enc_own", lambda: enc_of("_near", near(0)))

    def total(kind):
        value = get(kind + "_own") + get(kind + "_prev").astype(jnp.float32) + get(kind + "_next").astype(jnp.float32)
        return value.astype(jnp.bfloat16)

    return total("dec")[:, None, :], total("enc").T[None]


def shards_any(acts, err_grad, codes, dec_weight, act_ids, act_count):
    z = lax.axis_index("lat")
    x = lax.axis_index("tok")
    rows = err_grad.shape[1]
    lat = dec_weight.shape[0]
    width = acts.shape[3]
    groups = acts.shape[0]
    blocks = lax.axis_size("lat")
    w_own = lax.dynamic_slice_in_dim(dec_weight.reshape(lat, -1), x * width, width, 1)
    w_all = lax.all_gather(w_own, "lat", axis=0, tiled=True)
    err = lax.all_to_all(err_grad, "tok", split_axis=3, concat_axis=0, tiled=True)
    err = err.reshape(groups * rows, width)
    ids = valid_ids(act_ids, act_count)
    code_hits = row_hits(lax.dynamic_slice_in_dim(ids, x, 1, 0), 0, codes.shape[1], z)
    used = codes[0] * code_hits.astype(jnp.bfloat16).T
    used = lax.all_to_all(used, "lat", split_axis=0, concat_axis=1, tiled=True)
    used = lax.all_gather(used, "tok", axis=0, tiled=True)
    dec_part = dot32(used, err, CONTRACT_ROWS)
    grad_dec = lax.psum_scatter(dec_part, "lat", scatter_dimension=0, tiled=True)
    dlat = lax.psum(dot32(err, w_all, CONTRACT_LAST), ("tok", "sub"))
    hits = [row_hits(ids, z * rows, rows, block).reshape(groups * rows, 1) for block in range(blocks)]
    hits = jnp.concatenate([jnp.broadcast_to(h, (groups * rows, lat)) for h in hits], axis=1)
    dcodes = (dlat * hits).astype(jnp.bfloat16)
    enc_part = dot32(acts.reshape(groups * rows, width), dcodes, CONTRACT_ROWS)
    grad_enc = lax.psum_scatter(enc_part, "lat", scatter_dimension=1, tiled=True)
    return grad_dec.astype(jnp.bfloat16)[:, None, :], grad_enc.astype(jnp.bfloat16)[None]


def solution(mesh):
    line = mesh.shape["lat"] == 4 and mesh.shape["tok"] == 2
    return jax.shard_map(
        shards_line if line else shards_any,
        mesh=mesh,
        in_specs=(
            P("groups", "lat", "sub", "tok"),
            P(("groups", "tok"), "lat", "sub", None),
            P(("groups", "tok"), None, "lat"),
            P(("groups", "lat"), "sub", None),
            P("groups", None, None),
            P("groups", None),
        ),
        out_specs=(P(("groups", "lat"), "sub", "tok"), P("sub", "tok", ("groups", "lat"))),
        check_vma=False,
    )
```

time: 171 us -> 127 us (0.74)
  waiting for transfers between devices: 92 us -> 33.4 us
  starting transfers between devices: 34.9 us -> 58.5 us
  matrix products: 18.4 us -> 0 us
  between operations: 14.4 us -> 1.09 us
  other arithmetic: 3.57 us -> 15.8 us
  Pallas kernels: 0 us -> 6.89 us
  local copies, waits for them, and re-layouts: 6.15 us -> 9.06 us
    all_to_all x1, waiting for transfers between devices: 34 us -> 0.1 us  [shards_line(): lax.all_to_all(get('codes_in'), 'lat', split_axis=0, concat_axis=0, tiled...]
    ppermute x17 -> x22, waiting for transfers between devices: 58 us -> 33.3 us  [send(): step(name, lambda: lax.ppermute(get(name + '_in'), axis, pairs))]
    ppermute x17 -> x22, starting transfers between devices: 31.5 us -> 53 us  [send(): step(name, lambda: lax.ppermute(get(name + '_in'), axis, pairs))]
    dot_general x13 -> x0, matrix products: 18.4 us -> none  [dot32(): lax.dot_general(left, right, dims, preferred_element_type=jnp.float32)]
    convert_element_type x2 -> x7, other arithmetic: 0.09 us -> 8.42 us  [the longest x5 8.25 us: add32(): return (term + got.astype(jnp.float32)).astype(jnp.bfloat16)]
    pallas_call x0 -> x8, Pallas kernels: none -> 6.89 us  [local_call(): pl.pallas_call(body, out_shape=out_shape, in_specs=[pl.BlockSpec(memory_s...]
    broadcast_in_dim x0 -> x2, other arithmetic: none -> 3.91 us  [shards_line(): return (total('dec')[:, None, :], total('enc').T[None])]
    unnamed x8 -> x23, local copies, waits for them, and re-layouts: 1.79 us -> 4.99 us
  transfers between devices with their start and end apart: 19 -> 23, of which waited for: 9 -> 12; matrix products, arithmetic and copies ran while one was open for 15% -> 15% of each run, Pallas kernels for 0% -> 6%
where the time goes in v3:
time: 127 us; the launch traced here: 125 us
  starting transfers between devices  58.5 us (46%)
  waiting for transfers between devices  33.4 us (26%)
  other arithmetic  15.8 us (12%)
  local copies, waits for them, and re-layouts  9.06 us (7%)
  Pallas kernels  6.89 us (5%)
    ppermute x22, starting transfers between devices, send(): step(name, lambda: lax.ppermute(get(name + '_in'), axis, pairs))  53 us
    ppermute x22, waiting for transfers between devices, send(): step(name, lambda: lax.ppermute(get(name + '_in'), axis, pairs))  33.3 us
    convert_element_type x5, other arithmetic, add32(): return (term + got.astype(jnp.float32)).astype(jnp.bfloat16)  8.25 us
    pallas_call x8, Pallas kernels, local_call(): pl.pallas_call(body, out_shape=out_shape, in_specs=[pl.BlockSpec(memory_s...  6.89 us
    all_to_all x1, starting transfers between devices, shards_line(): lax.all_to_all(get('codes_in'), 'lat', split_axis=0, concat_axis=0, tiled...  5.46 us
    unnamed x23, local copies, waits for them, and re-layouts  4.99 us
    broadcast_in_dim x2, other arithmetic, shards_line(): return (total('dec')[:, None, :], total('enc').T[None])  3.91 us
  transfers between devices with their start and end apart: 23, of which 12 were waited for; matrix products, arithmetic and copies ran while one was open for 15% of the time, Pallas kernels for 6%

profile of v3, /device:TPU:12, one launch (start us, length us, event | category | flops | bytes accessed | tf_op | source)
XLA Modules:
  0.0 124.7 jit_solution(5815263043281774872)
XLA Ops:
  0.7 5.5 %all-to-all-start = ((bf16[4,192,128]{2,1,0:T(8,128)(2,1)}), bf16[4,192,128]{2,1,0:T(8,128)(2,1)S(1)}, u32[]{:S(2)}, u32[]{:S(2)}) async-start(bf16[4,192,128]{2,1,0:T(8,128)(2,1)} %bitcast.66), calls=%async_computation | async-start | bytes 393216 | tf_op jit(solution)/shard_map/all_to_all | solution.py:131
  7.7 2.4 %dynamic-slice_bitcast_fusion = (bf16[192,2048]{1,0:T(8,128)(2,1)}, bf16[192,2048]{1,0:T(8,128)(2,1)S(1)}) fusion(bf16[1,192,1,4096]{3,1,2,0:T(8,128)(2,1)} %param.7, s32[]{:T(128)S(6)} %select_n.86, s32[]{:T(128)S(6)} %select_n.85), kind=kLoop, calls=%fused_computation.13 | loop fusion | bytes 3145736 | tf_op jit(solution)/shard_map/dynamic_slice | solution.py:128
  13.4 10.5 %collective-permute-start.3 = (bf16[128,2048]{1,0:T(8,128)(2,1)S(1)}, bf16[128,2048]{1,0:T(8,128)(2,1)}, u32[]{:S(2)}, u32[]{:S(2)}) collective-permute-start(bf16[128,2048]{1,0:T(8,128)(2,1)S(1)} %dynamic-slice_bitcast_fusion.2.refs_0_), channel_id=1, source_target_pairs={{4,0},{8,4},{12,8},{0,12},{5,1},{9,5},{13,9},{1,13},{6,2},{10,6},{... | collective-permute-start | bytes 1572872 | tf_op jit(solution)/shard_map/ppermute | solution.py:117
  25.6 7.3 %collective-permute-done = bf16[4,192,128]{2,1,0:T(8,128)(2,1)S(1)} collective-permute-done((bf16[4,192,128]{2,1,0:T(8,128)(2,1)S(1)}, bf16[4,192,128]{2,1,0:T(8,128)(2,1)S(1)}, u32[]{:S(2)}, u32[]{:S(2)}) %collective-permute-start) | collective-permute-done | bytes 196640 | tf_op jit(solution)/shard_map/ppermute | solution.py:117
  34.5 1.9 %copy-done.4 = f32[4,128,2048]{2,1,0:T(8,128)} copy-done((f32[4,128,2048]{2,1,0:T(8,128)}, f32[4,128,2048]{2,1,0:T(8,128)S(1)}, u32[]{:S(2)}) %copy-start.4) | copy-done | bytes 4194328
  36.5 4.2 %collective-permute-start.7 = (bf16[128,2048]{1,0:T(8,128)(2,1)}, bf16[128,2048]{1,0:T(8,128)(2,1)}, u32[]{:S(2)}, u32[]{:S(2)}) collective-permute-start(bf16[128,2048]{1,0:T(8,128)(2,1)} %collective-permute-done.4.refs_2_), channel_id=1, source_target_pairs={{4,8},{8,12},{5,9},{9,13},{6,10},{10,14},{7,11},{11,15},{20,24},{2... | collective-permute-start | bytes 1572872 | tf_op jit(solution)/shard_map/ppermute | solution.py:117
  40.6 1.9 %collective-permute-start.8 = (bf16[128,2048]{1,0:T(8,128)(2,1)}, bf16[128,2048]{1,0:T(8,128)(2,1)}, u32[]{:S(2)}, u32[]{:S(2)}) collective-permute-start(bf16[128,2048]{1,0:T(8,128)(2,1)} %collective-permute-done.3.refs_1_), channel_id=1, source_target_pairs={{8,4},{4,0},{9,5},{5,1},{10,6},{6,2},{11,7},{7,3},{24,20},{20,16},... | collective-permute-start | bytes 1572872 | tf_op jit(solution)/shard_map/ppermute | solution.py:117
  42.5 2.6 %shard_map.78 = f32[2,192,384]{2,1,0:T(8,128)S(1)} custom-call(s32[1]{0:T(128)} %bitcast.13.place_ref, bf16[192,2048]{1,0:T(8,128)(2,1)S(1)} %get-tuple-element.54.err_own_ref.own_ref, bf16[192,2048]{1,0:T(8,128)(2,1)S(1)} %collective-permute-done.1.err_other_ref.other_ref, bf16[128,2048]{1,0:T(8,128)(2,1)S(1)} %dynamic-slice_bitcast_fusion.2.refs_0_, ...), custom_call_target="tpu_custom_call" | custom-call | tf_op jit(solution)/shard_map/pallas_call | solution.py:33
  49.7 1.6 %collective-permute-start.6 = (f32[192,384]{1,0:T(8,128)S(1)}, f32[192,384]{1,0:T(8,128)S(1)}, u32[]{:S(2)}, u32[]{:S(2)}) collective-permute-start(f32[192,384]{1,0:T(8,128)S(1)} %fusion.7), channel_id=1, source_target_pairs={{0,2},{2,0},{1,3},{3,1},{4,6},{6,4},{5,7},{7,5},{8,10},{10,8},{9,1... | collective-permute-start | bytes 884744 | tf_op jit(solution)/shard_map/ppermute | solution.py:117
  51.3 3.3 %collective-permute-done.8 = bf16[128,2048]{1,0:T(8,128)(2,1)} collective-permute-done((bf16[128,2048]{1,0:T(8,128)(2,1)}, bf16[128,2048]{1,0:T(8,128)(2,1)}, u32[]{:S(2)}, u32[]{:S(2)}) %collective-permute-start.8) | collective-permute-done | bytes 524320 | tf_op jit(solution)/shard_map/ppermute | solution.py:117
  63.2 2.1 %fusion.1 = bf16[128,2048]{1,0:T(8,128)(2,1)} fusion(bf16[128,2048]{1,0:T(8,128)(2,1)S(1)} %collective-permute-done.2, f32[4,128,2048]{2,1,0:T(8,128)} %copy-done.4, s32[]{:T(128)S(6)} %select_n.89), kind=kLoop, calls=%fused_computation.3 | loop fusion | flops 786432 | bytes 2097156 | tf_op jit(solution)/shard_map/convert_element_type | solution.py:120
  66.8 5.3 %collective-permute-start.10 = (bf16[128,2048]{1,0:T(8,128)(2,1)}, bf16[128,2048]{1,0:T(8,128)(2,1)}, u32[]{:S(2)}, u32[]{:S(2)}) collective-permute-start(bf16[128,2048]{1,0:T(8,128)(2,1)} %fusion.1), channel_id=1, source_target_pairs={{0,4},{4,8},{1,5},{5,9},{2,6},{6,10},{3,7},{7,11},{16,20},{20,24},... | collective-permute-start | bytes 1572872 | tf_op jit(solution)/shard_map/ppermute | solution.py:117
  72.6 5.3 %collective-permute-done.14 = bf16[128,2048]{1,0:T(8,128)(2,1)S(1)} collective-permute-done((bf16[128,2048]{1,0:T(8,128)(2,1)S(1)}, bf16[128,2048]{1,0:T(8,128)(2,1)S(1)}, u32[]{:S(2)}, u32[]{:S(2)}) %collective-permute-start.14) | collective-permute-done | bytes 524320 | tf_op jit(solution)/shard_map/ppermute | solution.py:117
  78.9 4.7 %collective-permute-start.18 = (bf16[128,2048]{1,0:T(8,128)(2,1)}, bf16[128,2048]{1,0:T(8,128)(2,1)}, u32[]{:S(2)}, u32[]{:S(2)}) collective-permute-start(bf16[128,2048]{1,0:T(8,128)(2,1)} %add_convert_fusion.3), channel_id=1, source_target_pairs={{0,4},{4,8},{1,5},{5,9},{2,6},{6,10},{3,7},{7,11},{16,20},{20,24},... | collective-permute-start | bytes 1572872 | tf_op jit(solution)/shard_map/ppermute | solution.py:117
  86.0 3.3 %collective-permute-done.10 = bf16[128,2048]{1,0:T(8,128)(2,1)} collective-permute-done((bf16[128,2048]{1,0:T(8,128)(2,1)}, bf16[128,2048]{1,0:T(8,128)(2,1)}, u32[]{:S(2)}, u32[]{:S(2)}) %collective-permute-start.10) | collective-permute-done | bytes 524320 | tf_op jit(solution)/shard_map/ppermute | solution.py:117
  89.3 2.3 %fusion.2 = (bf16[128,2048]{1,0:T(8,128)(2,1)}, bf16[128,2048]{1,0:T(8,128)(2,1)S(1)}) fusion(bf16[128,2048]{1,0:T(8,128)(2,1)} %collective-permute-done.10, f32[4,128,2048]{2,1,0:T(8,128)S(1)} %copy-done.5, s32[]{:T(128)S(6)} %select_n.88, bf16[128,2048]{1,0:T(8,128)(2,1)} %collective-permute-done.16, s32[]{:T(128)S(6)} %max.3), kind=kLoop, calls=%fused_computation.5 | loop fusion | flops 1572864 | bytes 4194312 | tf_op jit(solution)/shard_map/convert_element_type | solution.py:120
  91.6 4.7 %collective-permute-start.15 = (bf16[128,2048]{1,0:T(8,128)(2,1)}, bf16[128,2048]{1,0:T(8,128)(2,1)}, u32[]{:S(2)}, u32[]{:S(2)}) collective-permute-start(bf16[128,2048]{1,0:T(8,128)(2,1)} %get-tuple-element.51), channel_id=1, source_target_pairs={{0,4},{4,8},{8,12},{1,5},{5,9},{9,13},{2,6},{6,10},{10,14},{3,7},{... | collective-permute-start | bytes 1572872 | tf_op jit(solution)/shard_map/ppermute | solution.py:117
  96.3 1.9 %collective-permute-start.17 = (bf16[128,2048]{1,0:T(8,128)(2,1)S(1)}, bf16[128,2048]{1,0:T(8,128)(2,1)}, u32[]{:S(2)}, u32[]{:S(2)}) collective-permute-start(bf16[128,2048]{1,0:T(8,128)(2,1)S(1)} %get-tuple-element.52), channel_id=1, source_target_pairs={{12,8},{8,4},{4,0},{13,9},{9,5},{5,1},{14,10},{10,6},{6,2},{15,11}... | collective-permute-start | bytes 1572872 | tf_op jit(solution)/shard_map/ppermute | solution.py:117
  98.2 2.3 %collective-permute-done.18 = bf16[128,2048]{1,0:T(8,128)(2,1)} collective-permute-done((bf16[128,2048]{1,0:T(8,128)(2,1)}, bf16[128,2048]{1,0:T(8,128)(2,1)}, u32[]{:S(2)}, u32[]{:S(2)}) %collective-permute-start.18) | collective-permute-done | bytes 524320 | tf_op jit(solution)/shard_map/ppermute | solution.py:117
  100.5 2.0 %add_convert_fusion.2 = bf16[128,2048]{1,0:T(8,128)(2,1)} fusion(f32[128,2048]{1,0:T(8,128)S(1)} %shard_map.83, bf16[128,2048]{1,0:T(8,128)(2,1)} %collective-permute-done.18), kind=kLoop, calls=%fused_computation.11 | loop fusion | flops 786432 | bytes 2097152 | tf_op jit(solution)/shard_map/convert_element_type | solution.py:120
  102.5 1.9 %collective-permute-start.19 = (bf16[128,2048]{1,0:T(8,128)(2,1)}, bf16[128,2048]{1,0:T(8,128)(2,1)}, u32[]{:S(2)}, u32[]{:S(2)}) collective-permute-start(bf16[128,2048]{1,0:T(8,128)(2,1)} %add_convert_fusion.2), channel_id=1, source_target_pairs={{0,4},{4,8},{8,12},{1,5},{5,9},{9,13},{2,6},{6,10},{10,14},{3,7},{... | collective-permute-start | bytes 1572872 | tf_op jit(solution)/shard_map/ppermute | solution.py:117
  105.4 4.7 %collective-permute-start.21 = (bf16[128,2048]{1,0:T(8,128)(2,1)}, bf16[128,2048]{1,0:T(8,128)(2,1)}, u32[]{:S(2)}, u32[]{:S(2)}) collective-permute-start(bf16[128,2048]{1,0:T(8,128)(2,1)} %add_convert_fusion.1), channel_id=1, source_target_pairs={{12,8},{8,4},{4,0},{13,9},{9,5},{5,1},{14,10},{10,6},{6,2},{15,11}... | collective-permute-start | bytes 1572872 | tf_op jit(solution)/shard_map/ppermute | solution.py:117
  112.1 2.5 %fusion.6 = bf16[128,1,2048]{2,0,1:T(8,128)(2,1)} fusion(bf16[128,2048]{1,0:T(8,128)(2,1)} %collective-permute-done.17, bf16[128,2048]{1,0:T(8,128)(2,1)} %collective-permute-done.15, f32[4,128,2048]{2,1,0:T(8,128)} %copy-done.4, s32[]{:T(128)S(6)} %select_n.87), kind=kLoop, calls=%fused_computation.16 | loop fusion | flops 1310720 | bytes 2621444 | tf_op jit(solution)/shard_map/broadcast_in_dim | solution.py:217
  114.6 7.7 %collective-permute-done.19 = bf16[128,2048]{1,0:T(8,128)(2,1)} collective-permute-done((bf16[128,2048]{1,0:T(8,128)(2,1)}, bf16[128,2048]{1,0:T(8,128)(2,1)}, u32[]{:S(2)}, u32[]{:S(2)}) %collective-permute-start.19) | collective-permute-done | bytes 524320 | tf_op jit(solution)/shard_map/ppermute | solution.py:117
  (92 shorter events, 31.7 us)
Async XLA Ops:
  0.7 12.8 %all-to-all-start = ((bf16[4,192,128]{2,1,0:T(8,128)(2,1)}), bf16[4,192,128]{2,1,0:T(8,128)(2,1)S(1)}, u32[]{:S(2)}, u32[]{:S(2)}) async-start(bf16[4,192,128]{2,1,0:T(8,128)(2,1)} %bitcast.66), calls=%async_computation | async-start | bytes 393216 | tf_op jit(solution)/shard_map/all_to_all | solution.py:131
  6.2 30.3 %collective-permute-start.4 = (bf16[128,2048]{1,0:T(8,128)(2,1)S(1)}, bf16[128,2048]{1,0:T(8,128)(2,1)}, u32[]{:S(2)}, u32[]{:S(2)}) collective-permute-start(bf16[128,2048]{1,0:T(8,128)(2,1)S(1)} %dynamic-slice_bitcast_fusion.2.refs_0_), channel_id=1, source_target_pairs={{0,4},{4,8},{8,12},{12,0},{1,5},{5,9},{9,13},{13,1},{2,6},{6,10},{... | collective-permute-start | bytes 1572872 | tf_op jit(solution)/shard_map/ppermute | solution.py:117
  10.1 23.0 %collective-permute-start.1 = (bf16[192,2048]{1,0:T(8,128)(2,1)}, bf16[192,2048]{1,0:T(8,128)(2,1)S(1)}, u32[]{:S(2)}, u32[]{:S(2)}) collective-permute-start(bf16[192,2048]{1,0:T(8,128)(2,1)} %get-tuple-element.53), channel_id=1, source_target_pairs={{0,2},{2,0},{1,3},{3,1},{4,6},{6,4},{5,7},{7,5},{8,10},{10,8},{9,1... | collective-permute-start | bytes 2359304 | tf_op jit(solution)/shard_map/ppermute | solution.py:117
  13.4 27.2 %collective-permute-start.3 = (bf16[128,2048]{1,0:T(8,128)(2,1)S(1)}, bf16[128,2048]{1,0:T(8,128)(2,1)}, u32[]{:S(2)}, u32[]{:S(2)}) collective-permute-start(bf16[128,2048]{1,0:T(8,128)(2,1)S(1)} %dynamic-slice_bitcast_fusion.2.refs_0_), channel_id=1, source_target_pairs={{4,0},{8,4},{12,8},{0,12},{5,1},{9,5},{13,9},{1,13},{6,2},{10,6},{... | collective-permute-start | bytes 1572872 | tf_op jit(solution)/shard_map/ppermute | solution.py:117
  24.0 9.0 %collective-permute-start = (bf16[4,192,128]{2,1,0:T(8,128)(2,1)S(1)}, bf16[4,192,128]{2,1,0:T(8,128)(2,1)S(1)}, u32[]{:S(2)}, u32[]{:S(2)}) collective-permute-start(bf16[4,192,128]{2,1,0:T(8,128)(2,1)S(1)} %all-to-all-done), channel_id=1, source_target_pairs={{0,2},{2,0},{1,3},{3,1},{4,6},{6,4},{5,7},{7,5},{8,10},{10,8},{9,1... | collective-permute-start | bytes 589832 | tf_op jit(solution)/shard_map/ppermute | solution.py:117
  36.5 14.8 %collective-permute-start.7 = (bf16[128,2048]{1,0:T(8,128)(2,1)}, bf16[128,2048]{1,0:T(8,128)(2,1)}, u32[]{:S(2)}, u32[]{:S(2)}) collective-permute-start(bf16[128,2048]{1,0:T(8,128)(2,1)} %collective-permute-done.4.refs_2_), channel_id=1, source_target_pairs={{4,8},{8,12},{5,9},{9,13},{6,10},{10,14},{7,11},{11,15},{20,24},{2... | collective-permute-start | bytes 1572872 | tf_op jit(solution)/shard_map/ppermute | solution.py:117
  40.6 13.9 %collective-permute-start.8 = (bf16[128,2048]{1,0:T(8,128)(2,1)}, bf16[128,2048]{1,0:T(8,128)(2,1)}, u32[]{:S(2)}, u32[]{:S(2)}) collective-permute-start(bf16[128,2048]{1,0:T(8,128)(2,1)} %collective-permute-done.3.refs_1_), channel_id=1, source_target_pairs={{8,4},{4,0},{9,5},{5,1},{10,6},{6,2},{11,7},{7,3},{24,20},{20,16},... | collective-permute-start | bytes 1572872 | tf_op jit(solution)/shard_map/ppermute | solution.py:117
  46.0 14.8 %copy-start.1 = (bf16[2,192,1,2048]{3,1,2,0:T(8,128)(2,1)S(1)}, bf16[2,192,1,2048]{3,1,2,0:T(8,128)(2,1)}, u32[]{:S(2)}) copy-start(bf16[2,192,1,2048]{3,1,2,0:T(8,128)(2,1)} %param.6) | copy-start | bytes 4718596
  46.7 1.9 %collective-permute-start.5 = (f32[192,384]{1,0:T(8,128)}, f32[192,384]{1,0:T(8,128)}, u32[]{:S(2)}, u32[]{:S(2)}) collective-permute-start(f32[192,384]{1,0:T(8,128)} %slice_bitcast_fusion), channel_id=1, source_target_pairs={{0,1},{1,0},{2,3},{3,2},{4,5},{5,4},{6,7},{7,6},{8,9},{9,8},{10,11... | collective-permute-start | bytes 884744 | tf_op jit(solution)/shard_map/ppermute | solution.py:117
  46.8 16.4 %collective-permute-start.2 = (bf16[128,2048]{1,0:T(8,128)(2,1)}, bf16[128,2048]{1,0:T(8,128)(2,1)S(1)}, u32[]{:S(2)}, u32[]{:S(2)}) collective-permute-start(bf16[128,2048]{1,0:T(8,128)(2,1)} %copy-done.7), channel_id=1, source_target_pairs={{0,4},{12,8},{1,5},{13,9},{2,6},{14,10},{3,7},{15,11},{16,20},{28,... | collective-permute-start | bytes 1572872 | tf_op jit(solution)/shard_map/ppermute | solution.py:117
  49.7 9.1 %collective-permute-start.6 = (f32[192,384]{1,0:T(8,128)S(1)}, f32[192,384]{1,0:T(8,128)S(1)}, u32[]{:S(2)}, u32[]{:S(2)}) collective-permute-start(f32[192,384]{1,0:T(8,128)S(1)} %fusion.7), channel_id=1, source_target_pairs={{0,2},{2,0},{1,3},{3,1},{4,6},{6,4},{5,7},{7,5},{8,10},{10,8},{9,1... | collective-permute-start | bytes 884744 | tf_op jit(solution)/shard_map/ppermute | solution.py:117
  57.4 1.8 %collective-permute-start.11 = (f32[192,128]{1,0:T(8,128)S(1)}, f32[192,128]{1,0:T(8,128)S(1)}, u32[]{:S(2)}, u32[]{:S(2)}) collective-permute-start(f32[192,128]{1,0:T(8,128)S(1)} %slice_bitcast_fusion.2), channel_id=1, source_target_pairs={{0,1},{1,0},{2,3},{3,2},{4,5},{5,4},{6,7},{7,6},{8,9},{9,8},{10,11... | collective-permute-start | bytes 294920 | tf_op jit(solution)/shard_map/ppermute | solution.py:117
  59.1 1.7 %collective-permute-start.9 = (bf16[192,384]{1,0:T(8,128)(2,1)S(1)}, bf16[192,384]{1,0:T(8,128)(2,1)S(1)}, u32[]{:S(2)}, u32[]{:S(2)}) collective-permute-start(bf16[192,384]{1,0:T(8,128)(2,1)S(1)} %pad_maximum_fusion), channel_id=1, source_target_pairs={{0,1},{1,0},{2,3},{3,2},{4,5},{5,4},{6,7},{7,6},{8,9},{9,8},{10,11... | collective-permute-start | bytes 442376 | tf_op jit(solution)/shard_map/ppermute | solution.py:117
  59.2 6.1 %collective-permute-start.12 = (f32[192,128]{1,0:T(8,128)S(1)}, f32[192,128]{1,0:T(8,128)S(1)}, u32[]{:S(2)}, u32[]{:S(2)}) collective-permute-start(f32[192,128]{1,0:T(8,128)S(1)} %fusion.8), channel_id=1, source_target_pairs={{0,2},{2,0},{1,3},{3,1},{4,6},{6,4},{5,7},{7,5},{8,10},{10,8},{9,1... | collective-permute-start | bytes 294920 | tf_op jit(solution)/shard_map/ppermute | solution.py:117
  61.3 16.7 %collective-permute-start.14 = (bf16[128,2048]{1,0:T(8,128)(2,1)S(1)}, bf16[128,2048]{1,0:T(8,128)(2,1)S(1)}, u32[]{:S(2)}, u32[]{:S(2)}) collective-permute-start(bf16[128,2048]{1,0:T(8,128)(2,1)S(1)} %shard_map.79), channel_id=1, source_target_pairs={{0,4},{12,8},{1,5},{13,9},{2,6},{14,10},{3,7},{15,11},{16,20},{28,... | collective-permute-start | bytes 1572872 | tf_op jit(solution)/shard_map/ppermute | solution.py:117
  65.4 6.7 %collective-permute-start.13 = (bf16[192,128]{1,0:T(8,128)(2,1)S(1)}, bf16[192,128]{1,0:T(8,128)(2,1)S(1)}, u32[]{:S(2)}, u32[]{:S(2)}) collective-permute-start(bf16[192,128]{1,0:T(8,128)(2,1)S(1)} %multiply_convert_fusion.mine_ref), channel_id=1, source_target_pairs={{0,1},{1,0},{2,3},{3,2},{4,5},{5,4},{6,7},{7,6},{8,9},{9,8},{10,11... | collective-permute-start | bytes 147464 | tf_op jit(solution)/shard_map/ppermute | solution.py:117
  65.5 20.5 %collective-permute-start.16 = (bf16[128,2048]{1,0:T(8,128)(2,1)}, bf16[128,2048]{1,0:T(8,128)(2,1)}, u32[]{:S(2)}, u32[]{:S(2)}) collective-permute-start(bf16[128,2048]{1,0:T(8,128)(2,1)} %fusion.1), channel_id=1, source_target_pairs={{12,8},{8,4},{13,9},{9,5},{14,10},{10,6},{15,11},{11,7},{28,24},{2... | collective-permute-start | bytes 1572872 | tf_op jit(solution)/shard_map/ppermute | solution.py:117
  66.8 22.5 %collective-permute-start.10 = (bf16[128,2048]{1,0:T(8,128)(2,1)}, bf16[128,2048]{1,0:T(8,128)(2,1)}, u32[]{:S(2)}, u32[]{:S(2)}) collective-permute-start(bf16[128,2048]{1,0:T(8,128)(2,1)} %fusion.1), channel_id=1, source_target_pairs={{0,4},{4,8},{1,5},{5,9},{2,6},{6,10},{3,7},{7,11},{16,20},{20,24},... | collective-permute-start | bytes 1572872 | tf_op jit(solution)/shard_map/ppermute | solution.py:117
  78.9 21.7 %collective-permute-start.18 = (bf16[128,2048]{1,0:T(8,128)(2,1)}, bf16[128,2048]{1,0:T(8,128)(2,1)}, u32[]{:S(2)}, u32[]{:S(2)}) collective-permute-start(bf16[128,2048]{1,0:T(8,128)(2,1)} %add_convert_fusion.3), channel_id=1, source_target_pairs={{0,4},{4,8},{1,5},{5,9},{2,6},{6,10},{3,7},{7,11},{16,20},{20,24},... | collective-permute-start | bytes 1572872 | tf_op jit(solution)/shard_map/ppermute | solution.py:117
  84.6 19.8 %collective-permute-start.20 = (bf16[128,2048]{1,0:T(8,128)(2,1)}, bf16[128,2048]{1,0:T(8,128)(2,1)S(1)}, u32[]{:S(2)}, u32[]{:S(2)}) collective-permute-start(bf16[128,2048]{1,0:T(8,128)(2,1)} %add_convert_fusion.3), channel_id=1, source_target_pairs={{12,8},{8,4},{13,9},{9,5},{14,10},{10,6},{15,11},{11,7},{28,24},{2... | collective-permute-start | bytes 1572872 | tf_op jit(solution)/shard_map/ppermute | solution.py:117
  91.6 20.2 %collective-permute-start.15 = (bf16[128,2048]{1,0:T(8,128)(2,1)}, bf16[128,2048]{1,0:T(8,128)(2,1)}, u32[]{:S(2)}, u32[]{:S(2)}) collective-permute-start(bf16[128,2048]{1,0:T(8,128)(2,1)} %get-tuple-element.51), channel_id=1, source_target_pairs={{0,4},{4,8},{8,12},{1,5},{5,9},{9,13},{2,6},{6,10},{10,14},{3,7},{... | collective-permute-start | bytes 1572872 | tf_op jit(solution)/shard_map/ppermute | solution.py:117
  96.3 15.8 %collective-permute-start.17 = (bf16[128,2048]{1,0:T(8,128)(2,1)S(1)}, bf16[128,2048]{1,0:T(8,128)(2,1)}, u32[]{:S(2)}, u32[]{:S(2)}) collective-permute-start(bf16[128,2048]{1,0:T(8,128)(2,1)S(1)} %get-tuple-element.52), channel_id=1, source_target_pairs={{12,8},{8,4},{4,0},{13,9},{9,5},{5,1},{14,10},{10,6},{6,2},{15,11}... | collective-permute-start | bytes 1572872 | tf_op jit(solution)/shard_map/ppermute | solution.py:117
  102.5 19.8 %collective-permute-start.19 = (bf16[128,2048]{1,0:T(8,128)(2,1)}, bf16[128,2048]{1,0:T(8,128)(2,1)}, u32[]{:S(2)}, u32[]{:S(2)}) collective-permute-start(bf16[128,2048]{1,0:T(8,128)(2,1)} %add_convert_fusion.2), channel_id=1, source_target_pairs={{0,4},{4,8},{8,12},{1,5},{5,9},{9,13},{2,6},{6,10},{10,14},{3,7},{... | collective-permute-start | bytes 1572872 | tf_op jit(solution)/shard_map/ppermute | solution.py:117
  105.4 16.9 %collective-permute-start.21 = (bf16[128,2048]{1,0:T(8,128)(2,1)}, bf16[128,2048]{1,0:T(8,128)(2,1)}, u32[]{:S(2)}, u32[]{:S(2)}) collective-permute-start(bf16[128,2048]{1,0:T(8,128)(2,1)} %add_convert_fusion.1), channel_id=1, source_target_pairs={{12,8},{8,4},{4,0},{13,9},{9,5},{5,1},{14,10},{10,6},{6,2},{15,11}... | collective-permute-start | bytes 1572872 | tf_op jit(solution)/shard_map/ppermute | solution.py:117
  (9 other events, 56.8 us)

commit v4 on v3

--- a/solution.py
+++ b/solution.py
@@ -8,16 +8,13 @@
 from jax.sharding import PartitionSpec as P
 
 TBLK = 256
-MERGED = False
 ORDER = {
-    "dec_down": ("enc_two",),
-    "dec_far": ("enc_far_in",),
-    "dec_up": ("enc_two",),
-    "tok_near": ("up", "down",),
-    "tok_two": ("dec_two",),
-    "w_next": ("dec",),
-    "w_next_in": ("codes",),
-    "w_prev": ("dec",),
+    "w_3": ("dec",),
+    "w_3_in": ("codes",),
+    "sub_near": ("dec_far",),
+    "w_2": ("enc_far_in",),
+    "tok_two": ("dec_pair_in", "dec_last_in",),
+    "enc_mid": ("dec_pair",),
 }
 CONTRACT_LAST = (((1,), (1,)), ((), ()))
 PLAIN = (((1,), (0,)), ((), ()))
@@ -44,12 +41,12 @@
     return value.astype(jnp.float32).T.astype(jnp.bfloat16)
 
 
-def dec_body(far_ref, own_ref, other_ref, err_own_ref, err_other_ref, out_ref, first_ref):
-    for j in range(out_ref.shape[0]):
-        out_ref[j] = dot32(turned(own_ref[j]), err_own_ref[...], PLAIN) + dot32(
-            turned(other_ref[j]), err_other_ref[...], PLAIN
-        )
-    first_ref[...] = out_ref[far_ref[0]].astype(jnp.bfloat16)
+def dec_body(block_ref, own_ref, other_ref, err_own_ref, err_other_ref, *out_refs):
+    block = block_ref[0]
+    total = dot32(turned(own_ref[block]), err_own_ref[...], PLAIN)
+    total += dot32(turned(other_ref[block]), err_other_ref[...], PLAIN)
+    for out_ref in out_refs:
+        out_ref[...] = total.astype(out_ref.dtype)
 
 
 def dlat_body(place_ref, own_ref, other_ref, *refs):
@@ -87,15 +84,11 @@
     lat = dec_weight.shape[0]
     width = acts.shape[3]
     swap = [(0, 1), (1, 0)]
-    ring = [(0, 1), (1, 2), (2, 3), (3, 0)]
-    up, down = [(0, 1), (1, 2), (2, 3)], [(3, 2), (2, 1), (1, 0)]
-    up_two, down_two = [(0, 1), (1, 2)], [(3, 2), (2, 1)]
-    up_on, down_on = [(1, 2), (2, 3)], [(2, 1), (1, 0)]
-    inward = [(0, 1), (3, 2)]
+    pairs = [(0, 1), (1, 0), (2, 3), (3, 2)]
+    inward, outward, across, ends = [(0, 1), (3, 2)], [(1, 0), (2, 3)], [(1, 2), (2, 1)], [(0, 3), (3, 0)]
+    at_end = (z == 0) | (z == 3)
 
     ids = valid_ids(act_ids, act_count)
-    far_block = jnp.where(z == 0, 3, 0)
-    two_block = lax.rem(z + 2, 4)
     act_rows = acts.reshape(2, rows, width)
     err_rows = err_grad.reshape(rows, -1)
     block = jax.ShapeDtypeStruct((lat, width), jnp.float32)
@@ -121,8 +114,8 @@
 
     step("weights", lambda: dec_weight.reshape(lat, -1))
     step("w_own", lambda: lax.dynamic_slice_in_dim(get("weights"), x * width, width, 1))
-    send("w_prev", lambda: get("w_own"), "lat", ring)
-    send("w_next", lambda: get("w_own"), "lat", [(b, a) for a, b in ring])
+    send("w_1", lambda: get("w_own"), "lat", pairs)
+    send("w_3", lambda: get("w_own"), "lat", across + ends)
 
     step("err_own", lambda: lax.dynamic_slice_in_dim(err_rows, x * width, width, 1))
     send("err", lambda: lax.dynamic_slice_in_dim(err_rows, (1 - x) * width, width, 1), "tok", swap)
@@ -137,32 +130,18 @@
         return value * hit[:, :, None].astype(jnp.bfloat16)
 
     step("used_own", lambda: used(get("codes"), x))
-    step(
-        "dec",
-        lambda: local_call(
-            dec_body,
-            (jax.ShapeDtypeStruct((4, lat, width), jnp.float32), block16),
-            [far_block], get("used_own"), used(get("codes_other"), 1 - x), get("err_own"), get("err"),
-        ),
-    )
-
-    def dec_of(b):
-        return lax.dynamic_index_in_dim(get("dec")[0], b, 0, keepdims=False)
-
-    if MERGED:
-        send("up", lambda: jnp.where(z == 0, get("dec")[1], get("w_prev")), "lat", up)
-        send("down", lambda: jnp.where(z == 3, get("dec")[1], get("w_next")), "lat", down)
-
-        def far_term():
-            got = jnp.where(z == 1, get("up"), get("down"))
-            return jnp.where((z == 1) | (z == 2), got, jnp.zeros((), jnp.bfloat16))
-
-        step("dec_far", far_term)
-    else:
-        send("up", lambda: get("w_prev"), "lat", up_on)
-        send("down", lambda: get("w_next"), "lat", down_on)
-        send("dec_far", lambda: get("dec")[1], "lat", inward)
-    step("w_two", lambda: jnp.where(z < 2, get("down"), get("up")))
+    step("used_other", lambda: used(get("codes_other"), 1 - x))
+
+    def dec_of(b, *out):
+        codes_pair = get("used_own"), get("used_other")
+        return local_call(dec_body, out, [b], *codes_pair, get("err_own"), get("err"))
+
+    step("dec", lambda: dec_of(z ^ 3, block16))
+
+    send("w_across", lambda: get("w_1"), "lat", across)
+    send("w_out", lambda: get("w_3"), "lat", outward)
+    send("dec_far", lambda: get("dec")[0], "lat", inward)
+    step("w_2", lambda: jnp.where(at_end, get("w_out"), get("w_across")))
 
     def latent_grads(tag, names, blocks):
         def part():
@@ -184,8 +163,8 @@
         step("mine" + tag, mine)
         send("other" + tag, lambda: get("mine" + tag), "sub", swap)
 
-    latent_grads("_near", ["w_own", "w_next", "w_prev"], [z, lax.rem(z + 1, 4), lax.rem(z + 3, 4)])
-    latent_grads("_two", ["w_two"], [two_block])
+    latent_grads("_near", ["w_own", "w_1", "w_3"], [z, z ^ 1, z ^ 3])
+    latent_grads("_two", ["w_2"], [z ^ 2])
 
     def enc_of(tag, pick, out=block):
         return local_call(enc_body, out, [c], act_rows, pick(get("mine" + tag)), pick(get("other" + tag)))
@@ -193,25 +172,26 @@
     def near(i):
         return lambda part: part[:, i * lat : (i + 1) * lat]
 
-    send(
-        "enc_far",
-        lambda: enc_of("_near", lambda part: jnp.where(z == 0, near(2)(part), near(1)(part)), block16),
-        "lat", inward,
-    )
-    step("dec_two", lambda: add32(dec_of(two_block), get("dec_far")))
-    step("enc_two", lambda: add32(enc_of("_two", near(0)), get("enc_far")))
-    for kind in ("dec", "enc"):
-        send(kind + "_up", functools.partial(get, kind + "_two"), "lat", up_two)
-        send(kind + "_down", functools.partial(get, kind + "_two"), "lat", down_two)
-    send("dec_prev", lambda: add32(dec_of(jnp.minimum(z + 1, 3)), get("dec_up")), "lat", up)
-    send("dec_next", lambda: add32(dec_of(jnp.maximum(z - 1, 0)), get("dec_down")), "lat", down)
-    send("enc_prev", lambda: add32(enc_of("_near", near(1)), get("enc_up")), "lat", up)
-    send("enc_next", lambda: add32(enc_of("_near", near(2)), get("enc_down")), "lat", down)
-    step("dec_own", lambda: dec_of(z))
+    send("enc_far", lambda: enc_of("_near", near(2), block16), "lat", inward)
     step("enc_own", lambda: enc_of("_near", near(0)))
+    step("enc_1", lambda: enc_of("_near", near(1)))
+    step("enc_2", lambda: enc_of("_two", near(0)))
+    step("enc_3", lambda: enc_of("_near", near(2)))
+    for j, name in enumerate(("dec_own", "dec_1", "dec_2", "dec_3")):
+        step(name, lambda j=j: dec_of(z ^ j, block)[0])
+
+    def line_sums(kind):
+        step(kind + "_two", lambda: add32(get(kind + "_2"), get(kind + "_far")))
+        send(kind + "_in", lambda: get(kind + "_two"), "lat", inward)
+        send(kind + "_mid", lambda: get(kind + "_two"), "lat", across)
+        send(kind + "_pair", lambda: add32(get(kind + "_1"), get(kind + "_mid")), "lat", pairs)
+        send(kind + "_last", lambda: add32(get(kind + "_3"), get(kind + "_in")), "lat", across)
+
+    line_sums("dec")
+    line_sums("enc")
 
     def total(kind):
-        value = get(kind + "_own") + get(kind + "_prev").astype(jnp.float32) + get(kind + "_next").astype(jnp.float32)
+        value = get(kind + "_own") + get(kind + "_pair").astype(jnp.float32) + get(kind + "_last").astype(jnp.float32)
         return value.astype(jnp.bfloat16)
 
     return total("dec")[:, None, :], total("enc").T[None]

time: 127 us -> 116 us (0.913); the launches traced: 125 us -> 115 us
  waiting for transfers between devices: 33.4 us -> 62.2 us
  starting transfers between devices: 58.5 us -> 36.1 us
  other arithmetic: 15.8 us -> 3.29 us
  local copies, waits for them, and re-layouts: 9.06 us -> 4.51 us
    ppermute x22, waiting for transfers between devices: 33.3 us -> 62.1 us  [send(): step(name, lambda: lax.ppermute(get(name + '_in'), axis, pairs))]
    ppermute x22, starting transfers between devices: 53 us -> 30.6 us  [send(): step(name, lambda: lax.ppermute(get(name + '_in'), axis, pairs))]
    convert_element_type x5 -> x6, other arithmetic: 8.25 us -> 0.63 us  [add32(): return (term + got.astype(jnp.float32)).astype(jnp.bfloat16)]
    unnamed x23 -> x11, local copies, waits for them, and re-layouts: 4.99 us -> 1.12 us
    broadcast_in_dim x2, other arithmetic: 3.91 us -> 1.17 us  [shards_line(): return (total('dec')[:, None, :], total('enc').T[None])]
    pallas_call x8 -> x12, Pallas kernels: 6.89 us -> 7.97 us  [local_call(): pl.pallas_call(body, out_shape=out_shape, in_specs=[pl.BlockSpec(memory_s...]
  transfers between devices with their start and end apart: 23 -> 23, of which waited for: 12 -> 16; matrix products, arithmetic and copies ran while one was open for 15% -> 6% of each run, Pallas kernels for 6% -> 7%
where the time goes in v4:
time: 116 us; the launch traced here: 115 us
  waiting for transfers between devices  62.2 us (54%)
  starting transfers between devices  36.1 us (31%)
  Pallas kernels  7.97 us (7%)
  local copies, waits for them, and re-layouts  4.51 us (4%)
  other arithmetic  3.29 us (3%)
    ppermute x22, waiting for transfers between devices, send(): step(name, lambda: lax.ppermute(get(name + '_in'), axis, pairs))  62.1 us
    ppermute x22, starting transfers between devices, send(): step(name, lambda: lax.ppermute(get(name + '_in'), axis, pairs))  30.6 us
    pallas_call x12, Pallas kernels, local_call(): pl.pallas_call(body, out_shape=out_shape, in_specs=[pl.BlockSpec(memory_s...  7.97 us
    all_to_all x1, starting transfers between devices, shards_line(): lax.all_to_all(get('codes_in'), 'lat', split_axis=0, concat_axis=0, tiled...  5.46 us
    dynamic_slice x1, local copies, waits for them, and re-layouts, shards_line(): lax.dynamic_slice_in_dim(err_rows, (1 - x) * width, width, 1)  2.41 us
  transfers between devices with their start and end apart: 23, of which 16 were waited for; matrix products, arithmetic and copies ran while one was open for 6% of the time, Pallas kernels for 7%

profile of v4, /device:TPU:12, one launch (start us, length us, event | category | flops | bytes accessed | tf_op | source)
XLA Modules:
  0.0 115.2 jit_solution(415737880835021031)
XLA Ops:
  0.6 5.5 %all-to-all-start = ((bf16[4,192,128]{2,1,0:T(8,128)(2,1)}), bf16[4,192,128]{2,1,0:T(8,128)(2,1)S(1)}, u32[]{:S(2)}, u32[]{:S(2)}) async-start(bf16[4,192,128]{2,1,0:T(8,128)(2,1)} %bitcast.49), calls=%async_computation | async-start | bytes 393216 | tf_op jit(solution)/shard_map/all_to_all | solution.py:124
  6.1 2.4 %dynamic-slice_bitcast_fusion = (bf16[192,2048]{1,0:T(8,128)(2,1)}, bf16[192,2048]{1,0:T(8,128)(2,1)S(1)}) fusion(bf16[1,192,1,4096]{3,1,2,0:T(8,128)(2,1)} %param.7, s32[]{:T(128)S(6)} %select_n.58, s32[]{:T(128)S(6)} %select_n.57), kind=kLoop, calls=%fused_computation.8 | loop fusion | bytes 3145736 | tf_op jit(solution)/shard_map/dynamic_slice | solution.py:121
  8.5 1.5 %collective-permute-start.1 = (bf16[192,2048]{1,0:T(8,128)(2,1)}, bf16[192,2048]{1,0:T(8,128)(2,1)S(1)}, u32[]{:S(2)}, u32[]{:S(2)}) collective-permute-start(bf16[192,2048]{1,0:T(8,128)(2,1)} %get-tuple-element.40), channel_id=1, source_target_pairs={{0,2},{2,0},{1,3},{3,1},{4,6},{6,4},{5,7},{7,5},{8,10},{10,8},{9,1... | collective-permute-start | bytes 2359304 | tf_op jit(solution)/shard_map/ppermute | solution.py:110
  12.1 2.8 %collective-permute-start.8 = (bf16[128,2048]{1,0:T(8,128)(2,1)S(1)}, bf16[128,2048]{1,0:T(8,128)(2,1)}, u32[]{:S(2)}, u32[]{:S(2)}) collective-permute-start(bf16[128,2048]{1,0:T(8,128)(2,1)S(1)} %dynamic-slice_bitcast_fusion.2.refs_0_), channel_id=1, source_target_pairs={{4,8},{8,4},{0,12},{12,0},{5,9},{9,5},{1,13},{13,1},{6,10},{10,6},... | collective-permute-start | bytes 1572872 | tf_op jit(solution)/shard_map/ppermute | solution.py:110
  15.6 16.1 %collective-permute-done = bf16[4,192,128]{2,1,0:T(8,128)(2,1)S(1)} collective-permute-done((bf16[4,192,128]{2,1,0:T(8,128)(2,1)S(1)}, bf16[4,192,128]{2,1,0:T(8,128)(2,1)S(1)}, u32[]{:S(2)}, u32[]{:S(2)}) %collective-permute-start) | collective-permute-done | bytes 196640 | tf_op jit(solution)/shard_map/ppermute | solution.py:110
  33.6 3.4 %collective-permute-done.8.refs_2_ = bf16[128,2048]{1,0:T(8,128)(2,1)} collective-permute-done((bf16[128,2048]{1,0:T(8,128)(2,1)S(1)}, bf16[128,2048]{1,0:T(8,128)(2,1)}, u32[]{:S(2)}, u32[]{:S(2)}) %collective-permute-start.8) | collective-permute-done | bytes 524320 | tf_op jit(solution)/shard_map/ppermute | solution.py:110
  37.0 2.6 %shard_map.82 = f32[2,192,384]{2,1,0:T(8,128)S(1)} custom-call(s32[1]{0:T(128)} %bitcast.14.place_ref, bf16[192,2048]{1,0:T(8,128)(2,1)S(1)} %get-tuple-element.41.err_own_ref.own_ref, bf16[192,2048]{1,0:T(8,128)(2,1)S(1)} %collective-permute-done.1.err_other_ref.other_ref, bf16[128,2048]{1,0:T(8,128)(2,1)S(1)} %dynamic-slice_bitcast_fusion.2.refs_0_, ...), custom_call_target="tpu_custom_call" | custom-call | tf_op jit(solution)/shard_map/pallas_call | solution.py:30
  39.8 3.6 %collective-permute-start.13 = (bf16[128,2048]{1,0:T(8,128)(2,1)}, bf16[128,2048]{1,0:T(8,128)(2,1)S(1)}, u32[]{:S(2)}, u32[]{:S(2)}) collective-permute-start(bf16[128,2048]{1,0:T(8,128)(2,1)} %collective-permute-done.7.refs_1_), channel_id=1, source_target_pairs={{4,8},{8,4},{5,9},{9,5},{6,10},{10,6},{7,11},{11,7},{20,24},{24,20... | collective-permute-start | bytes 1572872 | tf_op jit(solution)/shard_map/ppermute | solution.py:110
  44.9 1.3 %collective-permute-start.12 = (bf16[128,2048]{1,0:T(8,128)(2,1)}, bf16[128,2048]{1,0:T(8,128)(2,1)S(1)}, u32[]{:S(2)}, u32[]{:S(2)}) collective-permute-start(bf16[128,2048]{1,0:T(8,128)(2,1)} %collective-permute-done.8.refs_2_), channel_id=1, source_target_pairs={{4,0},{8,12},{5,1},{9,13},{6,2},{10,14},{7,3},{11,15},{20,16},{24,... | collective-permute-start | bytes 1572872 | tf_op jit(solution)/shard_map/ppermute | solution.py:110
  46.6 1.6 %collective-permute-start.10 = (f32[192,384]{1,0:T(8,128)S(1)}, f32[192,384]{1,0:T(8,128)S(1)}, u32[]{:S(2)}, u32[]{:S(2)}) collective-permute-start(f32[192,384]{1,0:T(8,128)S(1)} %fusion.2), channel_id=1, source_target_pairs={{0,2},{2,0},{1,3},{3,1},{4,6},{6,4},{5,7},{7,5},{8,10},{10,8},{9,1... | collective-permute-start | bytes 884744 | tf_op jit(solution)/shard_map/ppermute | solution.py:110
  48.2 3.5 %collective-permute-start.3 = (bf16[128,2048]{1,0:T(8,128)(2,1)S(1)}, bf16[128,2048]{1,0:T(8,128)(2,1)S(1)}, u32[]{:S(2)}, u32[]{:S(2)}) collective-permute-start(bf16[128,2048]{1,0:T(8,128)(2,1)S(1)} %add_convert_fusion.7), channel_id=1, source_target_pairs={{4,8},{8,4},{5,9},{9,5},{6,10},{10,6},{7,11},{11,7},{20,24},{24,20... | collective-permute-start | bytes 1572872 | tf_op jit(solution)/shard_map/ppermute | solution.py:110
  53.0 2.4 %collective-permute-done.10 = f32[192,384]{1,0:T(8,128)S(1)} collective-permute-done((f32[192,384]{1,0:T(8,128)S(1)}, f32[192,384]{1,0:T(8,128)S(1)}, u32[]{:S(2)}, u32[]{:S(2)}) %collective-permute-start.10) | collective-permute-done | bytes 294944 | tf_op jit(solution)/shard_map/ppermute | solution.py:110
  56.6 1.7 %collective-permute-done.12 = bf16[128,2048]{1,0:T(8,128)(2,1)S(1)} collective-permute-done((bf16[128,2048]{1,0:T(8,128)(2,1)}, bf16[128,2048]{1,0:T(8,128)(2,1)S(1)}, u32[]{:S(2)}, u32[]{:S(2)}) %collective-permute-start.12) | collective-permute-done | bytes 524320 | tf_op jit(solution)/shard_map/ppermute | solution.py:110
  60.9 6.5 %collective-permute-done.3 = bf16[128,2048]{1,0:T(8,128)(2,1)S(1)} collective-permute-done((bf16[128,2048]{1,0:T(8,128)(2,1)S(1)}, bf16[128,2048]{1,0:T(8,128)(2,1)S(1)}, u32[]{:S(2)}, u32[]{:S(2)}) %collective-permute-start.3) | collective-permute-done | bytes 524320 | tf_op jit(solution)/shard_map/ppermute | solution.py:110
  68.3 4.0 %collective-permute-done.15 = f32[192,128]{1,0:T(8,128)S(1)} collective-permute-done((f32[192,128]{1,0:T(8,128)S(1)}, f32[192,128]{1,0:T(8,128)S(1)}, u32[]{:S(2)}, u32[]{:S(2)}) %collective-permute-start.15) | collective-permute-done | bytes 98336 | tf_op jit(solution)/shard_map/ppermute | solution.py:110
  74.1 2.2 %collective-permute-done.17 = bf16[128,2048]{1,0:T(8,128)(2,1)S(1)} collective-permute-done((bf16[128,2048]{1,0:T(8,128)(2,1)S(1)}, bf16[128,2048]{1,0:T(8,128)(2,1)S(1)}, u32[]{:S(2)}, u32[]{:S(2)}) %collective-permute-start.17) | collective-permute-done | bytes 524320 | tf_op jit(solution)/shard_map/ppermute | solution.py:110
  76.4 3.6 %collective-permute-start.18 = (bf16[128,2048]{1,0:T(8,128)(2,1)S(1)}, bf16[128,2048]{1,0:T(8,128)(2,1)S(1)}, u32[]{:S(2)}, u32[]{:S(2)}) collective-permute-start(bf16[128,2048]{1,0:T(8,128)(2,1)S(1)} %add_convert_fusion.3), channel_id=1, source_target_pairs={{4,8},{8,4},{5,9},{9,5},{6,10},{10,6},{7,11},{11,7},{20,24},{24,20... | collective-permute-start | bytes 1572872 | tf_op jit(solution)/shard_map/ppermute | solution.py:110
  82.3 2.2 %collective-permute-start.6 = (bf16[128,2048]{1,0:T(8,128)(2,1)S(1)}, bf16[128,2048]{1,0:T(8,128)(2,1)S(1)}, u32[]{:S(2)}, u32[]{:S(2)}) collective-permute-start(bf16[128,2048]{1,0:T(8,128)(2,1)S(1)} %add_convert_fusion.5), channel_id=1, source_target_pairs={{4,8},{8,4},{5,9},{9,5},{6,10},{10,6},{7,11},{11,7},{20,24},{24,20... | collective-permute-start | bytes 1572872 | tf_op jit(solution)/shard_map/ppermute | solution.py:110
  84.5 3.0 %collective-permute-done.4 = bf16[128,2048]{1,0:T(8,128)(2,1)S(1)} collective-permute-done((bf16[128,2048]{1,0:T(8,128)(2,1)S(1)}, bf16[128,2048]{1,0:T(8,128)(2,1)S(1)}, u32[]{:S(2)}, u32[]{:S(2)}) %collective-permute-start.4) | collective-permute-done | bytes 524320 | tf_op jit(solution)/shard_map/ppermute | solution.py:110
  87.5 5.6 %collective-permute-done.18 = bf16[128,2048]{1,0:T(8,128)(2,1)S(1)} collective-permute-done((bf16[128,2048]{1,0:T(8,128)(2,1)S(1)}, bf16[128,2048]{1,0:T(8,128)(2,1)S(1)}, u32[]{:S(2)}, u32[]{:S(2)}) %collective-permute-start.18) | collective-permute-done | bytes 524320 | tf_op jit(solution)/shard_map/ppermute | solution.py:110
  93.4 5.4 %collective-permute-done.20 = bf16[128,2048]{1,0:T(8,128)(2,1)S(1)} collective-permute-done((bf16[128,2048]{1,0:T(8,128)(2,1)S(1)}, bf16[128,2048]{1,0:T(8,128)(2,1)S(1)}, u32[]{:S(2)}, u32[]{:S(2)}) %collective-permute-start.20) | collective-permute-done | bytes 524320 | tf_op jit(solution)/shard_map/ppermute | solution.py:110
  98.9 3.6 %collective-permute-start.21 = (bf16[128,2048]{1,0:T(8,128)(2,1)S(1)}, bf16[128,2048]{1,0:T(8,128)(2,1)S(1)}, u32[]{:S(2)}, u32[]{:S(2)}) collective-permute-start(bf16[128,2048]{1,0:T(8,128)(2,1)S(1)} %add_convert_fusion.1), channel_id=1, source_target_pairs={{4,8},{8,4},{5,9},{9,5},{6,10},{10,6},{7,11},{11,7},{20,24},{24,20... | collective-permute-start | bytes 1572872 | tf_op jit(solution)/shard_map/ppermute | solution.py:110
  104.5 5.1 %collective-permute-done.19 = bf16[128,2048]{1,0:T(8,128)(2,1)S(1)} collective-permute-done((bf16[128,2048]{1,0:T(8,128)(2,1)S(1)}, bf16[128,2048]{1,0:T(8,128)(2,1)S(1)}, u32[]{:S(2)}, u32[]{:S(2)}) %collective-permute-start.19) | collective-permute-done | bytes 524320 | tf_op jit(solution)/shard_map/ppermute | solution.py:110
  109.7 4.4 %collective-permute-done.21 = bf16[128,2048]{1,0:T(8,128)(2,1)S(1)} collective-permute-done((bf16[128,2048]{1,0:T(8,128)(2,1)S(1)}, bf16[128,2048]{1,0:T(8,128)(2,1)S(1)}, u32[]{:S(2)}, u32[]{:S(2)}) %collective-permute-start.21) | collective-permute-done | bytes 524320 | tf_op jit(solution)/shard_map/ppermute | solution.py:110
  (84 shorter events, 20.0 us)
Async XLA Ops:
  0.6 11.4 %all-to-all-start = ((bf16[4,192,128]{2,1,0:T(8,128)(2,1)}), bf16[4,192,128]{2,1,0:T(8,128)(2,1)S(1)}, u32[]{:S(2)}, u32[]{:S(2)}) async-start(bf16[4,192,128]{2,1,0:T(8,128)(2,1)} %bitcast.49), calls=%async_computation | async-start | bytes 393216 | tf_op jit(solution)/shard_map/all_to_all | solution.py:124
  8.5 23.3 %collective-permute-start.1 = (bf16[192,2048]{1,0:T(8,128)(2,1)}, bf16[192,2048]{1,0:T(8,128)(2,1)S(1)}, u32[]{:S(2)}, u32[]{:S(2)}) collective-permute-start(bf16[192,2048]{1,0:T(8,128)(2,1)} %get-tuple-element.40), channel_id=1, source_target_pairs={{0,2},{2,0},{1,3},{3,1},{4,6},{6,4},{5,7},{7,5},{8,10},{10,8},{9,1... | collective-permute-start | bytes 2359304 | tf_op jit(solution)/shard_map/ppermute | solution.py:110
  10.1 27.0 %collective-permute-start.7 = (bf16[128,2048]{1,0:T(8,128)(2,1)S(1)}, bf16[128,2048]{1,0:T(8,128)(2,1)}, u32[]{:S(2)}, u32[]{:S(2)}) collective-permute-start(bf16[128,2048]{1,0:T(8,128)(2,1)S(1)} %dynamic-slice_bitcast_fusion.2.refs_0_), channel_id=1, source_target_pairs={{0,4},{4,0},{8,12},{12,8},{1,5},{5,1},{9,13},{13,9},{2,6},{6,2},{1... | collective-permute-start | bytes 1572872 | tf_op jit(solution)/shard_map/ppermute | solution.py:110
  12.1 25.0 %collective-permute-start.8 = (bf16[128,2048]{1,0:T(8,128)(2,1)S(1)}, bf16[128,2048]{1,0:T(8,128)(2,1)}, u32[]{:S(2)}, u32[]{:S(2)}) collective-permute-start(bf16[128,2048]{1,0:T(8,128)(2,1)S(1)} %dynamic-slice_bitcast_fusion.2.refs_0_), channel_id=1, source_target_pairs={{4,8},{8,4},{0,12},{12,0},{5,9},{9,5},{1,13},{13,1},{6,10},{10,6},... | collective-permute-start | bytes 1572872 | tf_op jit(solution)/shard_map/ppermute | solution.py:110
  14.9 16.8 %collective-permute-start = (bf16[4,192,128]{2,1,0:T(8,128)(2,1)S(1)}, bf16[4,192,128]{2,1,0:T(8,128)(2,1)S(1)}, u32[]{:S(2)}, u32[]{:S(2)}) collective-permute-start(bf16[4,192,128]{2,1,0:T(8,128)(2,1)S(1)} %all-to-all-done), channel_id=1, source_target_pairs={{0,2},{2,0},{1,3},{3,1},{4,6},{6,4},{5,7},{7,5},{8,10},{10,8},{9,1... | collective-permute-start | bytes 589832 | tf_op jit(solution)/shard_map/ppermute | solution.py:110
  32.3 14.2 %collective-permute-start.2 = (bf16[128,2048]{1,0:T(8,128)(2,1)S(1)}, bf16[128,2048]{1,0:T(8,128)(2,1)S(1)}, u32[]{:S(2)}, u32[]{:S(2)}) collective-permute-start(bf16[128,2048]{1,0:T(8,128)(2,1)S(1)} %shard_map.80), channel_id=1, source_target_pairs={{0,4},{12,8},{1,5},{13,9},{2,6},{14,10},{3,7},{15,11},{16,20},{28,... | collective-permute-start | bytes 1572872 | tf_op jit(solution)/shard_map/ppermute | solution.py:110
  39.6 6.6 %collective-permute-start.9 = (f32[192,384]{1,0:T(8,128)S(1)}, f32[192,384]{1,0:T(8,128)S(1)}, u32[]{:S(2)}, u32[]{:S(2)}) collective-permute-start(f32[192,384]{1,0:T(8,128)S(1)} %slice_bitcast_fusion), channel_id=1, source_target_pairs={{0,1},{1,0},{2,3},{3,2},{4,5},{5,4},{6,7},{7,6},{8,9},{9,8},{10,11... | collective-permute-start | bytes 884744 | tf_op jit(solution)/shard_map/ppermute | solution.py:110
  39.8 16.8 %collective-permute-start.13 = (bf16[128,2048]{1,0:T(8,128)(2,1)}, bf16[128,2048]{1,0:T(8,128)(2,1)S(1)}, u32[]{:S(2)}, u32[]{:S(2)}) collective-permute-start(bf16[128,2048]{1,0:T(8,128)(2,1)} %collective-permute-done.7.refs_1_), channel_id=1, source_target_pairs={{4,8},{8,4},{5,9},{9,5},{6,10},{10,6},{7,11},{11,7},{20,24},{24,20... | collective-permute-start | bytes 1572872 | tf_op jit(solution)/shard_map/ppermute | solution.py:110
  44.9 13.4 %collective-permute-start.12 = (bf16[128,2048]{1,0:T(8,128)(2,1)}, bf16[128,2048]{1,0:T(8,128)(2,1)S(1)}, u32[]{:S(2)}, u32[]{:S(2)}) collective-permute-start(bf16[128,2048]{1,0:T(8,128)(2,1)} %collective-permute-done.8.refs_2_), channel_id=1, source_target_pairs={{4,0},{8,12},{5,1},{9,13},{6,2},{10,14},{7,3},{11,15},{20,16},{24,... | collective-permute-start | bytes 1572872 | tf_op jit(solution)/shard_map/ppermute | solution.py:110
  46.6 8.9 %collective-permute-start.10 = (f32[192,384]{1,0:T(8,128)S(1)}, f32[192,384]{1,0:T(8,128)S(1)}, u32[]{:S(2)}, u32[]{:S(2)}) collective-permute-start(f32[192,384]{1,0:T(8,128)S(1)} %fusion.2), channel_id=1, source_target_pairs={{0,2},{2,0},{1,3},{3,1},{4,6},{6,4},{5,7},{7,5},{8,10},{10,8},{9,1... | collective-permute-start | bytes 884744 | tf_op jit(solution)/shard_map/ppermute | solution.py:110
  48.2 10.2 %copy-start.1 = (bf16[2,192,1,2048]{3,1,2,0:T(8,128)(2,1)S(1)}, bf16[2,192,1,2048]{3,1,2,0:T(8,128)(2,1)}, u32[]{:S(2)}) copy-start(bf16[2,192,1,2048]{3,1,2,0:T(8,128)(2,1)} %param.6) | copy-start | bytes 4718596
  48.2 19.2 %collective-permute-start.3 = (bf16[128,2048]{1,0:T(8,128)(2,1)S(1)}, bf16[128,2048]{1,0:T(8,128)(2,1)S(1)}, u32[]{:S(2)}, u32[]{:S(2)}) collective-permute-start(bf16[128,2048]{1,0:T(8,128)(2,1)S(1)} %add_convert_fusion.7), channel_id=1, source_target_pairs={{4,8},{8,4},{5,9},{9,5},{6,10},{10,6},{7,11},{11,7},{20,24},{24,20... | collective-permute-start | bytes 1572872 | tf_op jit(solution)/shard_map/ppermute | solution.py:110
  51.7 16.4 %collective-permute-start.5 = (bf16[128,2048]{1,0:T(8,128)(2,1)S(1)}, bf16[128,2048]{1,0:T(8,128)(2,1)S(1)}, u32[]{:S(2)}, u32[]{:S(2)}) collective-permute-start(bf16[128,2048]{1,0:T(8,128)(2,1)S(1)} %add_convert_fusion.7), channel_id=1, source_target_pairs={{0,4},{12,8},{1,5},{13,9},{2,6},{14,10},{3,7},{15,11},{16,20},{28,... | collective-permute-start | bytes 1572872 | tf_op jit(solution)/shard_map/ppermute | solution.py:110
  55.7 2.7 %collective-permute-start.11 = (bf16[192,384]{1,0:T(8,128)(2,1)S(1)}, bf16[192,384]{1,0:T(8,128)(2,1)S(1)}, u32[]{:S(2)}, u32[]{:S(2)}) collective-permute-start(bf16[192,384]{1,0:T(8,128)(2,1)S(1)} %pad_maximum_fusion), channel_id=1, source_target_pairs={{0,1},{1,0},{2,3},{3,2},{4,5},{5,4},{6,7},{7,6},{8,9},{9,8},{10,11... | collective-permute-start | bytes 442376 | tf_op jit(solution)/shard_map/ppermute | solution.py:110
  58.9 17.4 %collective-permute-start.17 = (bf16[128,2048]{1,0:T(8,128)(2,1)S(1)}, bf16[128,2048]{1,0:T(8,128)(2,1)S(1)}, u32[]{:S(2)}, u32[]{:S(2)}) collective-permute-start(bf16[128,2048]{1,0:T(8,128)(2,1)S(1)} %shard_map.85), channel_id=1, source_target_pairs={{0,4},{12,8},{1,5},{13,9},{2,6},{14,10},{3,7},{15,11},{16,20},{28,... | collective-permute-start | bytes 1572872 | tf_op jit(solution)/shard_map/ppermute | solution.py:110
  60.8 6.7 %collective-permute-start.14 = (f32[192,128]{1,0:T(8,128)S(1)}, f32[192,128]{1,0:T(8,128)S(1)}, u32[]{:S(2)}, u32[]{:S(2)}) collective-permute-start(f32[192,128]{1,0:T(8,128)S(1)} %slice_bitcast_fusion.2), channel_id=1, source_target_pairs={{0,1},{1,0},{2,3},{3,2},{4,5},{5,4},{6,7},{7,6},{8,9},{9,8},{10,11... | collective-permute-start | bytes 294920 | tf_op jit(solution)/shard_map/ppermute | solution.py:110
  67.6 4.7 %collective-permute-start.15 = (f32[192,128]{1,0:T(8,128)S(1)}, f32[192,128]{1,0:T(8,128)S(1)}, u32[]{:S(2)}, u32[]{:S(2)}) collective-permute-start(f32[192,128]{1,0:T(8,128)S(1)} %fusion.3), channel_id=1, source_target_pairs={{0,2},{2,0},{1,3},{3,1},{4,6},{6,4},{5,7},{7,5},{8,10},{10,8},{9,1... | collective-permute-start | bytes 294920 | tf_op jit(solution)/shard_map/ppermute | solution.py:110
  72.3 1.3 %collective-permute-start.16 = (bf16[192,128]{1,0:T(8,128)(2,1)S(1)}, bf16[192,128]{1,0:T(8,128)(2,1)S(1)}, u32[]{:S(2)}, u32[]{:S(2)}) collective-permute-start(bf16[192,128]{1,0:T(8,128)(2,1)S(1)} %multiply_convert_fusion.mine_ref), channel_id=1, source_target_pairs={{0,1},{1,0},{2,3},{3,2},{4,5},{5,4},{6,7},{7,6},{8,9},{9,8},{10,11... | collective-permute-start | bytes 147464 | tf_op jit(solution)/shard_map/ppermute | solution.py:110
  72.4 15.1 %collective-permute-start.4 = (bf16[128,2048]{1,0:T(8,128)(2,1)S(1)}, bf16[128,2048]{1,0:T(8,128)(2,1)S(1)}, u32[]{:S(2)}, u32[]{:S(2)}) collective-permute-start(bf16[128,2048]{1,0:T(8,128)(2,1)S(1)} %add_convert_fusion.6), channel_id=1, source_target_pairs={{0,4},{4,0},{8,12},{12,8},{1,5},{5,1},{9,13},{13,9},{2,6},{6,2},{1... | collective-permute-start | bytes 1572872 | tf_op jit(solution)/shard_map/ppermute | solution.py:110
  76.4 16.8 %collective-permute-start.18 = (bf16[128,2048]{1,0:T(8,128)(2,1)S(1)}, bf16[128,2048]{1,0:T(8,128)(2,1)S(1)}, u32[]{:S(2)}, u32[]{:S(2)}) collective-permute-start(bf16[128,2048]{1,0:T(8,128)(2,1)S(1)} %add_convert_fusion.3), channel_id=1, source_target_pairs={{4,8},{8,4},{5,9},{9,5},{6,10},{10,6},{7,11},{11,7},{20,24},{24,20... | collective-permute-start | bytes 1572872 | tf_op jit(solution)/shard_map/ppermute | solution.py:110
  80.1 18.7 %collective-permute-start.20 = (bf16[128,2048]{1,0:T(8,128)(2,1)S(1)}, bf16[128,2048]{1,0:T(8,128)(2,1)S(1)}, u32[]{:S(2)}, u32[]{:S(2)}) collective-permute-start(bf16[128,2048]{1,0:T(8,128)(2,1)S(1)} %add_convert_fusion.3), channel_id=1, source_target_pairs={{0,4},{12,8},{1,5},{13,9},{2,6},{14,10},{3,7},{15,11},{16,20},{28,... | collective-permute-start | bytes 1572872 | tf_op jit(solution)/shard_map/ppermute | solution.py:110
  82.3 21.2 %collective-permute-start.6 = (bf16[128,2048]{1,0:T(8,128)(2,1)S(1)}, bf16[128,2048]{1,0:T(8,128)(2,1)S(1)}, u32[]{:S(2)}, u32[]{:S(2)}) collective-permute-start(bf16[128,2048]{1,0:T(8,128)(2,1)S(1)} %add_convert_fusion.5), channel_id=1, source_target_pairs={{4,8},{8,4},{5,9},{9,5},{6,10},{10,6},{7,11},{11,7},{20,24},{24,20... | collective-permute-start | bytes 1572872 | tf_op jit(solution)/shard_map/ppermute | solution.py:110
  93.3 16.4 %collective-permute-start.19 = (bf16[128,2048]{1,0:T(8,128)(2,1)S(1)}, bf16[128,2048]{1,0:T(8,128)(2,1)S(1)}, u32[]{:S(2)}, u32[]{:S(2)}) collective-permute-start(bf16[128,2048]{1,0:T(8,128)(2,1)S(1)} %add_convert_fusion.2), channel_id=1, source_target_pairs={{0,4},{4,0},{8,12},{12,8},{1,5},{5,1},{9,13},{13,9},{2,6},{6,2},{1... | collective-permute-start | bytes 1572872 | tf_op jit(solution)/shard_map/ppermute | solution.py:110
  98.9 15.1 %collective-permute-start.21 = (bf16[128,2048]{1,0:T(8,128)(2,1)S(1)}, bf16[128,2048]{1,0:T(8,128)(2,1)S(1)}, u32[]{:S(2)}, u32[]{:S(2)}) collective-permute-start(bf16[128,2048]{1,0:T(8,128)(2,1)S(1)} %add_convert_fusion.1), channel_id=1, source_target_pairs={{4,8},{8,4},{5,9},{9,5},{6,10},{10,6},{7,11},{11,7},{20,24},{24,20... | collective-permute-start | bytes 1572872 | tf_op jit(solution)/shard_map/ppermute | solution.py:110
  (3 other events, 17.6 us)

commit v5 on v4

--- a/solution.py
+++ b/solution.py
@@ -9,11 +9,13 @@
 
 TBLK = 256
 ORDER = {
-    "w_3": ("dec",),
-    "w_3_in": ("codes",),
+    "w_far_in": ("codes",),
+    "w_mid_in": ("codes",),
+    "w_far": ("dec",),
     "sub_near": ("dec_far",),
+    "tok_near_in": ("dec_far",),
     "w_2": ("enc_far_in",),
-    "tok_two": ("dec_pair_in", "dec_last_in",),
+    "tok_rest": ("dec_pair_in", "dec_last_in",),
     "enc_mid": ("dec_pair",),
 }
 CONTRACT_LAST = (((1,), (1,)), ((), ()))
@@ -115,7 +117,8 @@
     step("weights", lambda: dec_weight.reshape(lat, -1))
     step("w_own", lambda: lax.dynamic_slice_in_dim(get("weights"), x * width, width, 1))
     send("w_1", lambda: get("w_own"), "lat", pairs)
-    send("w_3", lambda: get("w_own"), "lat", across + ends)
+    send("w_far", lambda: get("w_own"), "lat", ends)
+    send("w_mid", lambda: get("w_own"), "lat", across)
 
     step("err_own", lambda: lax.dynamic_slice_in_dim(err_rows, x * width, width, 1))
     send("err", lambda: lax.dynamic_slice_in_dim(err_rows, (1 - x) * width, width, 1), "tok", swap)
@@ -139,7 +142,7 @@
     step("dec", lambda: dec_of(z ^ 3, block16))
 
     send("w_across", lambda: get("w_1"), "lat", across)
-    send("w_out", lambda: get("w_3"), "lat", outward)
+    send("w_out", lambda: get("w_mid"), "lat", outward)
     send("dec_far", lambda: get("dec")[0], "lat", inward)
     step("w_2", lambda: jnp.where(at_end, get("w_out"), get("w_across")))
 
@@ -163,20 +166,20 @@
         step("mine" + tag, mine)
         send("other" + tag, lambda: get("mine" + tag), "sub", swap)
 
-    latent_grads("_near", ["w_own", "w_1", "w_3"], [z, z ^ 1, z ^ 3])
-    latent_grads("_two", ["w_2"], [z ^ 2])
+    latent_grads("_near", ["w_own", "w_far"], [z, z ^ 3])
+    latent_grads("_rest", ["w_2", "w_mid", "w_1"], [z ^ 2, z ^ 3, z ^ 1])
 
     def enc_of(tag, pick, out=block):
         return local_call(enc_body, out, [c], act_rows, pick(get("mine" + tag)), pick(get("other" + tag)))
 
-    def near(i):
+    def cols_of(i):
         return lambda part: part[:, i * lat : (i + 1) * lat]
 
-    send("enc_far", lambda: enc_of("_near", near(2), block16), "lat", inward)
-    step("enc_own", lambda: enc_of("_near", near(0)))
-    step("enc_1", lambda: enc_of("_near", near(1)))
-    step("enc_2", lambda: enc_of("_two", near(0)))
-    step("enc_3", lambda: enc_of("_near", near(2)))
+    send("enc_far", lambda: enc_of("_near", cols_of(1), block16), "lat", inward)
+    step("enc_own", lambda: enc_of("_near", cols_of(0)))
+    step("enc_1", lambda: enc_of("_rest", cols_of(2)))
+    step("enc_2", lambda: enc_of("_rest", cols_of(0)))
+    step("enc_3", lambda: enc_of("_rest", cols_of(1)))
     for j, name in enumerate(("dec_own", "dec_1", "dec_2", "dec_3")):
         step(name, lambda j=j: dec_of(z ^ j, block)[0])
 

time: 116 us -> 114 us (0.983)
  waiting for transfers between devices: 62.2 us -> 54.9 us
  starting transfers between devices: 36.1 us -> 41.5 us
    ppermute x22 -> x23, waiting for transfers between devices: 62.1 us -> 54.8 us  [send(): step(name, lambda: lax.ppermute(get(name + '_in'), axis, pairs))]
    ppermute x22 -> x23, starting transfers between devices: 30.6 us -> 36 us  [send(): step(name, lambda: lax.ppermute(get(name + '_in'), axis, pairs))]
  transfers between devices with their start and end apart: 23 -> 24, of which waited for: 16 -> 14; matrix products, arithmetic and copies ran while one was open for 6% -> 6% of each run, Pallas kernels for 7% -> 7%
where the time goes in v5:
time: 114 us
  waiting for transfers between devices  54.9 us (48%)
  starting transfers between devices  41.5 us (36%)
  Pallas kernels  8.21 us (7%)
  local copies, waits for them, and re-layouts  4.56 us (4%)
  other arithmetic  3.35 us (3%)
  between operations  1.17 us (1%)
    ppermute x23, waiting for transfers between devices, send(): step(name, lambda: lax.ppermute(get(name + '_in'), axis, pairs))  54.8 us
    ppermute x23, starting transfers between devices, send(): step(name, lambda: lax.ppermute(get(name + '_in'), axis, pairs))  36 us
    pallas_call x12, Pallas kernels, local_call(): pl.pallas_call(body, out_shape=out_shape, in_specs=[pl.BlockSpec(memory_s...  8.21 us
    all_to_all x1, starting transfers between devices, shards_line(): lax.all_to_all(get('codes_in'), 'lat', split_axis=0, concat_axis=0, tiled...  5.46 us
    dynamic_slice x1, local copies, waits for them, and re-layouts, shards_line(): lax.dynamic_slice_in_dim(err_rows, (1 - x) * width, width, 1)  2.45 us
  transfers between devices with their start and end apart: 24, of which 14 were waited for; matrix products, arithmetic and copies ran while one was open for 6% of the time, Pallas kernels for 7%

profile of v5, /device:TPU:12, one launch (start us, length us, event | category | flops | bytes accessed | tf_op | source)
XLA Modules:
  0.0 113.6 jit_solution(15717245339298420540)
XLA Ops:
  0.6 5.5 %all-to-all-start = ((bf16[4,192,128]{2,1,0:T(8,128)(2,1)}), bf16[4,192,128]{2,1,0:T(8,128)(2,1)S(1)}, u32[]{:S(2)}, u32[]{:S(2)}) async-start(bf16[4,192,128]{2,1,0:T(8,128)(2,1)} %bitcast.49), calls=%async_computation | async-start | bytes 393216 | tf_op jit(solution)/shard_map/all_to_all | solution.py:127
  6.1 2.4 %dynamic-slice_bitcast_fusion = (bf16[192,2048]{1,0:T(8,128)(2,1)}, bf16[192,2048]{1,0:T(8,128)(2,1)S(1)}) fusion(bf16[1,192,1,4096]{3,1,2,0:T(8,128)(2,1)} %param.7, s32[]{:T(128)S(6)} %select_n.60, s32[]{:T(128)S(6)} %select_n.59), kind=kLoop, calls=%fused_computation.8 | loop fusion | bytes 3145736 | tf_op jit(solution)/shard_map/dynamic_slice | solution.py:124
  8.6 1.5 %collective-permute-start.1 = (bf16[192,2048]{1,0:T(8,128)(2,1)}, bf16[192,2048]{1,0:T(8,128)(2,1)S(1)}, u32[]{:S(2)}, u32[]{:S(2)}) collective-permute-start(bf16[192,2048]{1,0:T(8,128)(2,1)} %get-tuple-element.42), channel_id=1, source_target_pairs={{0,2},{2,0},{1,3},{3,1},{4,6},{6,4},{5,7},{7,5},{8,10},{10,8},{9,1... | collective-permute-start | bytes 2359304 | tf_op jit(solution)/shard_map/ppermute | solution.py:112
  12.8 4.7 %collective-permute-start.11 = (bf16[128,2048]{1,0:T(8,128)(2,1)S(1)}, bf16[128,2048]{1,0:T(8,128)(2,1)S(1)}, u32[]{:S(2)}, u32[]{:S(2)}) collective-permute-start(bf16[128,2048]{1,0:T(8,128)(2,1)S(1)} %dynamic-slice_bitcast_fusion.2.refs_0_), channel_id=1, source_target_pairs={{4,8},{8,4},{5,9},{9,5},{6,10},{10,6},{7,11},{11,7},{20,24},{24,20... | collective-permute-start | bytes 1572872 | tf_op jit(solution)/shard_map/ppermute | solution.py:112
  18.2 13.5 %collective-permute-done = bf16[4,192,128]{2,1,0:T(8,128)(2,1)S(1)} collective-permute-done((bf16[4,192,128]{2,1,0:T(8,128)(2,1)S(1)}, bf16[4,192,128]{2,1,0:T(8,128)(2,1)S(1)}, u32[]{:S(2)}, u32[]{:S(2)}) %collective-permute-start) | collective-permute-done | bytes 196640 | tf_op jit(solution)/shard_map/ppermute | solution.py:112
  34.8 3.4 %collective-permute-start.14 = (bf16[128,2048]{1,0:T(8,128)(2,1)}, bf16[128,2048]{1,0:T(8,128)(2,1)S(1)}, u32[]{:S(2)}, u32[]{:S(2)}) collective-permute-start(bf16[128,2048]{1,0:T(8,128)(2,1)} %collective-permute-done.13.refs_2_), channel_id=1, source_target_pairs={{4,8},{8,4},{5,9},{9,5},{6,10},{10,6},{7,11},{11,7},{20,24},{24,20... | collective-permute-start | bytes 1572872 | tf_op jit(solution)/shard_map/ppermute | solution.py:112
  39.7 2.2 %collective-permute-start.12 = (bf16[128,2048]{1,0:T(8,128)(2,1)S(1)}, bf16[128,2048]{1,0:T(8,128)(2,1)S(1)}, u32[]{:S(2)}, u32[]{:S(2)}) collective-permute-start(bf16[128,2048]{1,0:T(8,128)(2,1)S(1)} %collective-permute-done.11.refs_1_), channel_id=1, source_target_pairs={{4,0},{8,12},{5,1},{9,13},{6,2},{10,14},{7,3},{11,15},{20,16},{24,... | collective-permute-start | bytes 1572872 | tf_op jit(solution)/shard_map/ppermute | solution.py:112
  42.0 4.5 %collective-permute-done.2 = bf16[128,2048]{1,0:T(8,128)(2,1)S(1)} collective-permute-done((bf16[128,2048]{1,0:T(8,128)(2,1)S(1)}, bf16[128,2048]{1,0:T(8,128)(2,1)S(1)}, u32[]{:S(2)}, u32[]{:S(2)}) %collective-permute-start.2) | collective-permute-done | bytes 524320 | tf_op jit(solution)/shard_map/ppermute | solution.py:112
  46.5 1.6 %collective-permute-start.9 = (f32[192,256]{1,0:T(8,128)S(1)}, f32[192,256]{1,0:T(8,128)S(1)}, u32[]{:S(2)}, u32[]{:S(2)}) collective-permute-start(f32[192,256]{1,0:T(8,128)S(1)} %fusion.3), channel_id=1, source_target_pairs={{0,2},{2,0},{1,3},{3,1},{4,6},{6,4},{5,7},{7,5},{8,10},{10,8},{9,1... | collective-permute-start | bytes 589832 | tf_op jit(solution)/shard_map/ppermute | solution.py:112
  48.2 3.5 %collective-permute-start.3 = (bf16[128,2048]{1,0:T(8,128)(2,1)S(1)}, bf16[128,2048]{1,0:T(8,128)(2,1)S(1)}, u32[]{:S(2)}, u32[]{:S(2)}) collective-permute-start(bf16[128,2048]{1,0:T(8,128)(2,1)S(1)} %add_convert_fusion.7), channel_id=1, source_target_pairs={{4,8},{8,4},{5,9},{9,5},{6,10},{10,6},{7,11},{11,7},{20,24},{24,20... | collective-permute-start | bytes 1572872 | tf_op jit(solution)/shard_map/ppermute | solution.py:112
  56.3 2.4 %shard_map.85 = f32[2,192,384]{2,1,0:T(8,128)S(1)} custom-call(s32[1]{0:T(128)} %bitcast.14.place_ref, bf16[192,2048]{1,0:T(8,128)(2,1)S(1)} %get-tuple-element.43.err_own_ref.own_ref, bf16[192,2048]{1,0:T(8,128)(2,1)S(1)} %collective-permute-done.1.err_other_ref.other_ref, bf16[128,2048]{1,0:T(8,128)(2,1)S(1)} %broadcast_select_fusion.refs_0_, ...), custom_call_target="tpu_custom_call" | custom-call | tf_op jit(solution)/shard_map/pallas_call | solution.py:32
  59.0 3.5 %collective-permute-done.3 = bf16[128,2048]{1,0:T(8,128)(2,1)S(1)} collective-permute-done((bf16[128,2048]{1,0:T(8,128)(2,1)S(1)}, bf16[128,2048]{1,0:T(8,128)(2,1)S(1)}, u32[]{:S(2)}, u32[]{:S(2)}) %collective-permute-start.3) | collective-permute-done | bytes 524320 | tf_op jit(solution)/shard_map/ppermute | solution.py:112
  62.7 1.6 %collective-permute-start.16 = (f32[192,384]{1,0:T(8,128)S(1)}, f32[192,384]{1,0:T(8,128)S(1)}, u32[]{:S(2)}, u32[]{:S(2)}) collective-permute-start(f32[192,384]{1,0:T(8,128)S(1)} %fusion.2), channel_id=1, source_target_pairs={{0,2},{2,0},{1,3},{3,1},{4,6},{6,4},{5,7},{7,5},{8,10},{10,8},{9,1... | collective-permute-start | bytes 884744 | tf_op jit(solution)/shard_map/ppermute | solution.py:112
  64.2 4.2 %collective-permute-done.5 = bf16[128,2048]{1,0:T(8,128)(2,1)S(1)} collective-permute-done((bf16[128,2048]{1,0:T(8,128)(2,1)S(1)}, bf16[128,2048]{1,0:T(8,128)(2,1)S(1)}, u32[]{:S(2)}, u32[]{:S(2)}) %collective-permute-start.5) | collective-permute-done | bytes 524320 | tf_op jit(solution)/shard_map/ppermute | solution.py:112
  70.2 2.5 %collective-permute-start.4 = (bf16[128,2048]{1,0:T(8,128)(2,1)S(1)}, bf16[128,2048]{1,0:T(8,128)(2,1)S(1)}, u32[]{:S(2)}, u32[]{:S(2)}) collective-permute-start(bf16[128,2048]{1,0:T(8,128)(2,1)S(1)} %add_convert_fusion.6), channel_id=1, source_target_pairs={{0,4},{4,0},{8,12},{12,8},{1,5},{5,1},{9,13},{13,9},{2,6},{6,2},{1... | collective-permute-start | bytes 1572872 | tf_op jit(solution)/shard_map/ppermute | solution.py:112
  73.2 3.8 %collective-permute-done.18 = bf16[128,2048]{1,0:T(8,128)(2,1)S(1)} collective-permute-done((bf16[128,2048]{1,0:T(8,128)(2,1)S(1)}, bf16[128,2048]{1,0:T(8,128)(2,1)S(1)}, u32[]{:S(2)}, u32[]{:S(2)}) %collective-permute-start.18) | collective-permute-done | bytes 524320 | tf_op jit(solution)/shard_map/ppermute | solution.py:112
  77.1 2.2 %collective-permute-start.19 = (bf16[128,2048]{1,0:T(8,128)(2,1)S(1)}, bf16[128,2048]{1,0:T(8,128)(2,1)S(1)}, u32[]{:S(2)}, u32[]{:S(2)}) collective-permute-start(bf16[128,2048]{1,0:T(8,128)(2,1)S(1)} %add_convert_fusion.3), channel_id=1, source_target_pairs={{4,8},{8,4},{5,9},{9,5},{6,10},{10,6},{7,11},{11,7},{20,24},{24,20... | collective-permute-start | bytes 1572872 | tf_op jit(solution)/shard_map/ppermute | solution.py:112
  80.6 3.6 %collective-permute-start.6 = (bf16[128,2048]{1,0:T(8,128)(2,1)S(1)}, bf16[128,2048]{1,0:T(8,128)(2,1)S(1)}, u32[]{:S(2)}, u32[]{:S(2)}) collective-permute-start(bf16[128,2048]{1,0:T(8,128)(2,1)S(1)} %add_convert_fusion.5), channel_id=1, source_target_pairs={{4,8},{8,4},{5,9},{9,5},{6,10},{10,6},{7,11},{11,7},{20,24},{24,20... | collective-permute-start | bytes 1572872 | tf_op jit(solution)/shard_map/ppermute | solution.py:112
  85.2 3.0 %collective-permute-done.4 = bf16[128,2048]{1,0:T(8,128)(2,1)S(1)} collective-permute-done((bf16[128,2048]{1,0:T(8,128)(2,1)S(1)}, bf16[128,2048]{1,0:T(8,128)(2,1)S(1)}, u32[]{:S(2)}, u32[]{:S(2)}) %collective-permute-start.4) | collective-permute-done | bytes 524320 | tf_op jit(solution)/shard_map/ppermute | solution.py:112
  88.2 5.6 %collective-permute-done.19 = bf16[128,2048]{1,0:T(8,128)(2,1)S(1)} collective-permute-done((bf16[128,2048]{1,0:T(8,128)(2,1)S(1)}, bf16[128,2048]{1,0:T(8,128)(2,1)S(1)}, u32[]{:S(2)}, u32[]{:S(2)}) %collective-permute-start.19) | collective-permute-done | bytes 524320 | tf_op jit(solution)/shard_map/ppermute | solution.py:112
  94.0 5.4 %collective-permute-done.21 = bf16[128,2048]{1,0:T(8,128)(2,1)S(1)} collective-permute-done((bf16[128,2048]{1,0:T(8,128)(2,1)S(1)}, bf16[128,2048]{1,0:T(8,128)(2,1)S(1)}, u32[]{:S(2)}, u32[]{:S(2)}) %collective-permute-start.21) | collective-permute-done | bytes 524320 | tf_op jit(solution)/shard_map/ppermute | solution.py:112
  99.5 2.2 %collective-permute-start.22 = (bf16[128,2048]{1,0:T(8,128)(2,1)S(1)}, bf16[128,2048]{1,0:T(8,128)(2,1)S(1)}, u32[]{:S(2)}, u32[]{:S(2)}) collective-permute-start(bf16[128,2048]{1,0:T(8,128)(2,1)S(1)} %add_convert_fusion.1), channel_id=1, source_target_pairs={{4,8},{8,4},{5,9},{9,5},{6,10},{10,6},{7,11},{11,7},{20,24},{24,20... | collective-permute-start | bytes 1572872 | tf_op jit(solution)/shard_map/ppermute | solution.py:112
  103.8 5.4 %collective-permute-done.20 = bf16[128,2048]{1,0:T(8,128)(2,1)S(1)} collective-permute-done((bf16[128,2048]{1,0:T(8,128)(2,1)S(1)}, bf16[128,2048]{1,0:T(8,128)(2,1)S(1)}, u32[]{:S(2)}, u32[]{:S(2)}) %collective-permute-start.20) | collective-permute-done | bytes 524320 | tf_op jit(solution)/shard_map/ppermute | solution.py:112
  109.2 3.2 %collective-permute-done.22 = bf16[128,2048]{1,0:T(8,128)(2,1)S(1)} collective-permute-done((bf16[128,2048]{1,0:T(8,128)(2,1)S(1)}, bf16[128,2048]{1,0:T(8,128)(2,1)S(1)}, u32[]{:S(2)}, u32[]{:S(2)}) %collective-permute-start.22) | collective-permute-done | bytes 524320 | tf_op jit(solution)/shard_map/ppermute | solution.py:112
  (89 shorter events, 21.0 us)
Async XLA Ops:
  0.6 11.4 %all-to-all-start = ((bf16[4,192,128]{2,1,0:T(8,128)(2,1)}), bf16[4,192,128]{2,1,0:T(8,128)(2,1)S(1)}, u32[]{:S(2)}, u32[]{:S(2)}) async-start(bf16[4,192,128]{2,1,0:T(8,128)(2,1)} %bitcast.49), calls=%async_computation | async-start | bytes 393216 | tf_op jit(solution)/shard_map/all_to_all | solution.py:127
  8.6 23.3 %collective-permute-start.1 = (bf16[192,2048]{1,0:T(8,128)(2,1)}, bf16[192,2048]{1,0:T(8,128)(2,1)S(1)}, u32[]{:S(2)}, u32[]{:S(2)}) collective-permute-start(bf16[192,2048]{1,0:T(8,128)(2,1)} %get-tuple-element.42), channel_id=1, source_target_pairs={{0,2},{2,0},{1,3},{3,1},{4,6},{6,4},{5,7},{7,5},{8,10},{10,8},{9,1... | collective-permute-start | bytes 2359304 | tf_op jit(solution)/shard_map/ppermute | solution.py:112
  10.1 24.7 %collective-permute-start.13 = (bf16[128,2048]{1,0:T(8,128)(2,1)S(1)}, bf16[128,2048]{1,0:T(8,128)(2,1)}, u32[]{:S(2)}, u32[]{:S(2)}) collective-permute-start(bf16[128,2048]{1,0:T(8,128)(2,1)S(1)} %dynamic-slice_bitcast_fusion.2.refs_0_), channel_id=1, source_target_pairs={{0,4},{4,0},{8,12},{12,8},{1,5},{5,1},{9,13},{13,9},{2,6},{6,2},{1... | collective-permute-start | bytes 1572872 | tf_op jit(solution)/shard_map/ppermute | solution.py:112
  12.1 21.6 %collective-permute-start.7 = (bf16[128,2048]{1,0:T(8,128)(2,1)S(1)}, bf16[128,2048]{1,0:T(8,128)(2,1)S(1)}, u32[]{:S(2)}, u32[]{:S(2)}) collective-permute-start(bf16[128,2048]{1,0:T(8,128)(2,1)S(1)} %dynamic-slice_bitcast_fusion.2.refs_0_), channel_id=1, source_target_pairs={{0,12},{12,0},{1,13},{13,1},{2,14},{14,2},{3,15},{15,3},{16,28},{2... | collective-permute-start | bytes 1572872 | tf_op jit(solution)/shard_map/ppermute | solution.py:112
  12.8 26.9 %collective-permute-start.11 = (bf16[128,2048]{1,0:T(8,128)(2,1)S(1)}, bf16[128,2048]{1,0:T(8,128)(2,1)S(1)}, u32[]{:S(2)}, u32[]{:S(2)}) collective-permute-start(bf16[128,2048]{1,0:T(8,128)(2,1)S(1)} %dynamic-slice_bitcast_fusion.2.refs_0_), channel_id=1, source_target_pairs={{4,8},{8,4},{5,9},{9,5},{6,10},{10,6},{7,11},{11,7},{20,24},{24,20... | collective-permute-start | bytes 1572872 | tf_op jit(solution)/shard_map/ppermute | solution.py:112
  17.5 14.2 %collective-permute-start = (bf16[4,192,128]{2,1,0:T(8,128)(2,1)S(1)}, bf16[4,192,128]{2,1,0:T(8,128)(2,1)S(1)}, u32[]{:S(2)}, u32[]{:S(2)}) collective-permute-start(bf16[4,192,128]{2,1,0:T(8,128)(2,1)S(1)} %all-to-all-done), channel_id=1, source_target_pairs={{0,2},{2,0},{1,3},{3,1},{4,6},{6,4},{5,7},{7,5},{8,10},{10,8},{9,1... | collective-permute-start | bytes 589832 | tf_op jit(solution)/shard_map/ppermute | solution.py:112
  32.4 14.1 %collective-permute-start.2 = (bf16[128,2048]{1,0:T(8,128)(2,1)S(1)}, bf16[128,2048]{1,0:T(8,128)(2,1)S(1)}, u32[]{:S(2)}, u32[]{:S(2)}) collective-permute-start(bf16[128,2048]{1,0:T(8,128)(2,1)S(1)} %shard_map.80), channel_id=1, source_target_pairs={{0,4},{12,8},{1,5},{13,9},{2,6},{14,10},{3,7},{15,11},{16,20},{28,... | collective-permute-start | bytes 1572872 | tf_op jit(solution)/shard_map/ppermute | solution.py:112
  34.7 7.2 %collective-permute-start.8 = (f32[192,256]{1,0:T(8,128)S(1)}, f32[192,256]{1,0:T(8,128)S(1)}, u32[]{:S(2)}, u32[]{:S(2)}) collective-permute-start(f32[192,256]{1,0:T(8,128)S(1)} %slice_bitcast_fusion.2), channel_id=1, source_target_pairs={{0,1},{1,0},{2,3},{3,2},{4,5},{5,4},{6,7},{7,6},{8,9},{9,8},{10,11... | collective-permute-start | bytes 589832 | tf_op jit(solution)/shard_map/ppermute | solution.py:112
  34.8 18.4 %collective-permute-start.14 = (bf16[128,2048]{1,0:T(8,128)(2,1)}, bf16[128,2048]{1,0:T(8,128)(2,1)S(1)}, u32[]{:S(2)}, u32[]{:S(2)}) collective-permute-start(bf16[128,2048]{1,0:T(8,128)(2,1)} %collective-permute-done.13.refs_2_), channel_id=1, source_target_pairs={{4,8},{8,4},{5,9},{9,5},{6,10},{10,6},{7,11},{11,7},{20,24},{24,20... | collective-permute-start | bytes 1572872 | tf_op jit(solution)/shard_map/ppermute | solution.py:112
  39.7 14.0 %collective-permute-start.12 = (bf16[128,2048]{1,0:T(8,128)(2,1)S(1)}, bf16[128,2048]{1,0:T(8,128)(2,1)S(1)}, u32[]{:S(2)}, u32[]{:S(2)}) collective-permute-start(bf16[128,2048]{1,0:T(8,128)(2,1)S(1)} %collective-permute-done.11.refs_1_), channel_id=1, source_target_pairs={{4,0},{8,12},{5,1},{9,13},{6,2},{10,14},{7,3},{11,15},{20,16},{24,... | collective-permute-start | bytes 1572872 | tf_op jit(solution)/shard_map/ppermute | solution.py:112
  46.5 6.5 %collective-permute-start.9 = (f32[192,256]{1,0:T(8,128)S(1)}, f32[192,256]{1,0:T(8,128)S(1)}, u32[]{:S(2)}, u32[]{:S(2)}) collective-permute-start(f32[192,256]{1,0:T(8,128)S(1)} %fusion.3), channel_id=1, source_target_pairs={{0,2},{2,0},{1,3},{3,1},{4,6},{6,4},{5,7},{7,5},{8,10},{10,8},{9,1... | collective-permute-start | bytes 589832 | tf_op jit(solution)/shard_map/ppermute | solution.py:112
  48.2 14.3 %collective-permute-start.3 = (bf16[128,2048]{1,0:T(8,128)(2,1)S(1)}, bf16[128,2048]{1,0:T(8,128)(2,1)S(1)}, u32[]{:S(2)}, u32[]{:S(2)}) collective-permute-start(bf16[128,2048]{1,0:T(8,128)(2,1)S(1)} %add_convert_fusion.7), channel_id=1, source_target_pairs={{4,8},{8,4},{5,9},{9,5},{6,10},{10,6},{7,11},{11,7},{20,24},{24,20... | collective-permute-start | bytes 1572872 | tf_op jit(solution)/shard_map/ppermute | solution.py:112
  51.7 16.8 %collective-permute-start.5 = (bf16[128,2048]{1,0:T(8,128)(2,1)S(1)}, bf16[128,2048]{1,0:T(8,128)(2,1)S(1)}, u32[]{:S(2)}, u32[]{:S(2)}) collective-permute-start(bf16[128,2048]{1,0:T(8,128)(2,1)S(1)} %add_convert_fusion.7), channel_id=1, source_target_pairs={{0,4},{12,8},{1,5},{13,9},{2,6},{14,10},{3,7},{15,11},{16,20},{28,... | collective-permute-start | bytes 1572872 | tf_op jit(solution)/shard_map/ppermute | solution.py:112
  53.2 1.4 %collective-permute-start.10 = (bf16[192,256]{1,0:T(8,128)(2,1)S(1)}, bf16[192,256]{1,0:T(8,128)(2,1)S(1)}, u32[]{:S(2)}, u32[]{:S(2)}) collective-permute-start(bf16[192,256]{1,0:T(8,128)(2,1)S(1)} %pad_maximum_fusion.1), channel_id=1, source_target_pairs={{0,1},{1,0},{2,3},{3,2},{4,5},{5,4},{6,7},{7,6},{8,9},{9,8},{10,11... | collective-permute-start | bytes 294920 | tf_op jit(solution)/shard_map/ppermute | solution.py:112
  55.0 21.9 %collective-permute-start.18 = (bf16[128,2048]{1,0:T(8,128)(2,1)S(1)}, bf16[128,2048]{1,0:T(8,128)(2,1)S(1)}, u32[]{:S(2)}, u32[]{:S(2)}) collective-permute-start(bf16[128,2048]{1,0:T(8,128)(2,1)S(1)} %shard_map.84), channel_id=1, source_target_pairs={{0,4},{12,8},{1,5},{13,9},{2,6},{14,10},{3,7},{15,11},{16,20},{28,... | collective-permute-start | bytes 1572872 | tf_op jit(solution)/shard_map/ppermute | solution.py:112
  58.8 3.8 %collective-permute-start.15 = (f32[192,384]{1,0:T(8,128)S(1)}, f32[192,384]{1,0:T(8,128)S(1)}, u32[]{:S(2)}, u32[]{:S(2)}) collective-permute-start(f32[192,384]{1,0:T(8,128)S(1)} %slice_bitcast_fusion), channel_id=1, source_target_pairs={{0,1},{1,0},{2,3},{3,2},{4,5},{5,4},{6,7},{7,6},{8,9},{9,8},{10,11... | collective-permute-start | bytes 884744 | tf_op jit(solution)/shard_map/ppermute | solution.py:112
  62.7 7.2 %collective-permute-start.16 = (f32[192,384]{1,0:T(8,128)S(1)}, f32[192,384]{1,0:T(8,128)S(1)}, u32[]{:S(2)}, u32[]{:S(2)}) collective-permute-start(f32[192,384]{1,0:T(8,128)S(1)} %fusion.2), channel_id=1, source_target_pairs={{0,2},{2,0},{1,3},{3,1},{4,6},{6,4},{5,7},{7,5},{8,10},{10,8},{9,1... | collective-permute-start | bytes 884744 | tf_op jit(solution)/shard_map/ppermute | solution.py:112
  70.1 2.6 %collective-permute-start.17 = (bf16[192,384]{1,0:T(8,128)(2,1)S(1)}, bf16[192,384]{1,0:T(8,128)(2,1)S(1)}, u32[]{:S(2)}, u32[]{:S(2)}) collective-permute-start(bf16[192,384]{1,0:T(8,128)(2,1)S(1)} %pad_maximum_fusion), channel_id=1, source_target_pairs={{0,1},{1,0},{2,3},{3,2},{4,5},{5,4},{6,7},{7,6},{8,9},{9,8},{10,11... | collective-permute-start | bytes 442376 | tf_op jit(solution)/shard_map/ppermute | solution.py:112
  70.2 18.0 %collective-permute-start.4 = (bf16[128,2048]{1,0:T(8,128)(2,1)S(1)}, bf16[128,2048]{1,0:T(8,128)(2,1)S(1)}, u32[]{:S(2)}, u32[]{:S(2)}) collective-permute-start(bf16[128,2048]{1,0:T(8,128)(2,1)S(1)} %add_convert_fusion.6), channel_id=1, source_target_pairs={{0,4},{4,0},{8,12},{12,8},{1,5},{5,1},{9,13},{13,9},{2,6},{6,2},{1... | collective-permute-start | bytes 1572872 | tf_op jit(solution)/shard_map/ppermute | solution.py:112
  77.1 16.8 %collective-permute-start.19 = (bf16[128,2048]{1,0:T(8,128)(2,1)S(1)}, bf16[128,2048]{1,0:T(8,128)(2,1)S(1)}, u32[]{:S(2)}, u32[]{:S(2)}) collective-permute-start(bf16[128,2048]{1,0:T(8,128)(2,1)S(1)} %add_convert_fusion.3), channel_id=1, source_target_pairs={{4,8},{8,4},{5,9},{9,5},{6,10},{10,6},{7,11},{11,7},{20,24},{24,20... | collective-permute-start | bytes 1572872 | tf_op jit(solution)/shard_map/ppermute | solution.py:112
  79.3 20.1 %collective-permute-start.21 = (bf16[128,2048]{1,0:T(8,128)(2,1)S(1)}, bf16[128,2048]{1,0:T(8,128)(2,1)S(1)}, u32[]{:S(2)}, u32[]{:S(2)}) collective-permute-start(bf16[128,2048]{1,0:T(8,128)(2,1)S(1)} %add_convert_fusion.3), channel_id=1, source_target_pairs={{0,4},{12,8},{1,5},{13,9},{2,6},{14,10},{3,7},{15,11},{16,20},{28,... | collective-permute-start | bytes 1572872 | tf_op jit(solution)/shard_map/ppermute | solution.py:112
  80.6 22.1 %collective-permute-start.6 = (bf16[128,2048]{1,0:T(8,128)(2,1)S(1)}, bf16[128,2048]{1,0:T(8,128)(2,1)S(1)}, u32[]{:S(2)}, u32[]{:S(2)}) collective-permute-start(bf16[128,2048]{1,0:T(8,128)(2,1)S(1)} %add_convert_fusion.5), channel_id=1, source_target_pairs={{4,8},{8,4},{5,9},{9,5},{6,10},{10,6},{7,11},{11,7},{20,24},{24,20... | collective-permute-start | bytes 1572872 | tf_op jit(solution)/shard_map/ppermute | solution.py:112
  93.9 15.3 %collective-permute-start.20 = (bf16[128,2048]{1,0:T(8,128)(2,1)S(1)}, bf16[128,2048]{1,0:T(8,128)(2,1)S(1)}, u32[]{:S(2)}, u32[]{:S(2)}) collective-permute-start(bf16[128,2048]{1,0:T(8,128)(2,1)S(1)} %add_convert_fusion.2), channel_id=1, source_target_pairs={{0,4},{4,0},{8,12},{12,8},{1,5},{5,1},{9,13},{13,9},{2,6},{6,2},{1... | collective-permute-start | bytes 1572872 | tf_op jit(solution)/shard_map/ppermute | solution.py:112
  99.5 12.9 %collective-permute-start.22 = (bf16[128,2048]{1,0:T(8,128)(2,1)S(1)}, bf16[128,2048]{1,0:T(8,128)(2,1)S(1)}, u32[]{:S(2)}, u32[]{:S(2)}) collective-permute-start(bf16[128,2048]{1,0:T(8,128)(2,1)S(1)} %add_convert_fusion.1), channel_id=1, source_target_pairs={{4,8},{8,4},{5,9},{9,5},{6,10},{10,6},{7,11},{11,7},{20,24},{24,20... | collective-permute-start | bytes 1572872 | tf_op jit(solution)/shard_map/ppermute | solution.py:112
  (4 other events, 24.1 us)

commit v6 on v5

--- a/solution.py
+++ b/solution.py
@@ -17,6 +17,8 @@
     "w_2": ("enc_far_in",),
     "tok_rest": ("dec_pair_in", "dec_last_in",),
     "enc_mid": ("dec_pair",),
+    "sub_rest": ("dec_two",),
+    "w_across": ("tok_near", "w_out",),
 }
 CONTRACT_LAST = (((1,), (1,)), ((), ()))
 PLAIN = (((1,), (0,)), ((), ()))
@@ -34,7 +36,7 @@
         out_shape=out_shape,
         in_specs=[pl.BlockSpec(memory_space=pltpu.SMEM)] + [vmem] * len(args),
         out_specs=jax.tree.map(lambda _: vmem, out_shape),
-        compiler_params=pltpu.CompilerParams(vmem_limit_bytes=32 * 2**20),
+        compiler_params=pltpu.CompilerParams(vmem_limit_bytes=12 * 2**20),
         cost_estimate=pl.CostEstimate(flops=0, bytes_accessed=0, transcendentals=0),
     )(jnp.stack(scalars).astype(jnp.int32), *args)
 
@@ -185,7 +187,7 @@
 
     def line_sums(kind):
         step(kind + "_two", lambda: add32(get(kind + "_2"), get(kind + "_far")))
-        send(kind + "_in", lambda: get(kind + "_two"), "lat", inward)
+        send(kind + "_in", lambda: get(kind + "_2").astype(jnp.bfloat16), "lat", inward)
         send(kind + "_mid", lambda: get(kind + "_two"), "lat", across)
         send(kind + "_pair", lambda: add32(get(kind + "_1"), get(kind + "_mid")), "lat", pairs)
         send(kind + "_last", lambda: add32(get(kind + "_3"), get(kind + "_in")), "lat", across)

time: 114 us -> 114 us (level)
  no operation moved by 1% of the time
where the time goes in v6:
time: 114 us
  waiting for transfers between devices  54.6 us (48%)
  starting transfers between devices  41.7 us (37%)
  Pallas kernels  8.22 us (7%)
  local copies, waits for them, and re-layouts  4.56 us (4%)
  other arithmetic  3.45 us (3%)
  between operations  1.17 us (1%)
    ppermute x23, waiting for transfers between devices, send(): step(name, lambda: lax.ppermute(get(name + '_in'), axis, pairs))  54.5 us
    ppermute x23, starting transfers between devices, send(): step(name, lambda: lax.ppermute(get(name + '_in'), axis, pairs))  36.2 us
    pallas_call x12, Pallas kernels, local_call(): pl.pallas_call(body, out_shape=out_shape, in_specs=[pl.BlockSpec(memory_s...  8.22 us
    all_to_all x1, starting transfers between devices, shards_line(): lax.all_to_all(get('codes_in'), 'lat', split_axis=0, concat_axis=0, tiled...  5.46 us
    dynamic_slice x1, local copies, waits for them, and re-layouts, shards_line(): lax.dynamic_slice_in_dim(err_rows, (1 - x) * width, width, 1)  2.45 us
  transfers between devices with their start and end apart: 24, of which 14 were waited for; matrix products, arithmetic and copies ran while one was open for 6% of the time, Pallas kernels for 7%

profile of v6, /device:TPU:12, one launch (start us, length us, event | category | flops | bytes accessed | tf_op | source)
XLA Modules:
  0.0 113.7 jit_solution(1626366504418832416)
XLA Ops:
  0.6 5.5 %all-to-all-start = ((bf16[4,192,128]{2,1,0:T(8,128)(2,1)}), bf16[4,192,128]{2,1,0:T(8,128)(2,1)S(1)}, u32[]{:S(2)}, u32[]{:S(2)}) async-start(bf16[4,192,128]{2,1,0:T(8,128)(2,1)} %bitcast.49), calls=%async_computation | async-start | bytes 393216 | tf_op jit(solution)/shard_map/all_to_all | solution.py:129
  6.1 2.4 %dynamic-slice_bitcast_fusion = (bf16[192,2048]{1,0:T(8,128)(2,1)}, bf16[192,2048]{1,0:T(8,128)(2,1)S(1)}) fusion(bf16[1,192,1,4096]{3,1,2,0:T(8,128)(2,1)} %param.7, s32[]{:T(128)S(6)} %select_n.60, s32[]{:T(128)S(6)} %select_n.59), kind=kLoop, calls=%fused_computation.8 | loop fusion | bytes 3145736 | tf_op jit(solution)/shard_map/dynamic_slice | solution.py:126
  8.6 1.5 %collective-permute-start.1 = (bf16[192,2048]{1,0:T(8,128)(2,1)}, bf16[192,2048]{1,0:T(8,128)(2,1)S(1)}, u32[]{:S(2)}, u32[]{:S(2)}) collective-permute-start(bf16[192,2048]{1,0:T(8,128)(2,1)} %get-tuple-element.46), channel_id=1, source_target_pairs={{0,2},{2,0},{1,3},{3,1},{4,6},{6,4},{5,7},{7,5},{8,10},{10,8},{9,1... | collective-permute-start | bytes 2359304 | tf_op jit(solution)/shard_map/ppermute | solution.py:114
  12.8 4.7 %collective-permute-start.11 = (bf16[128,2048]{1,0:T(8,128)(2,1)S(1)}, bf16[128,2048]{1,0:T(8,128)(2,1)S(1)}, u32[]{:S(2)}, u32[]{:S(2)}) collective-permute-start(bf16[128,2048]{1,0:T(8,128)(2,1)S(1)} %dynamic-slice_bitcast_fusion.2.refs_0_), channel_id=1, source_target_pairs={{4,8},{8,4},{5,9},{9,5},{6,10},{10,6},{7,11},{11,7},{20,24},{24,20... | collective-permute-start | bytes 1572872 | tf_op jit(solution)/shard_map/ppermute | solution.py:114
  18.2 13.5 %collective-permute-done = bf16[4,192,128]{2,1,0:T(8,128)(2,1)S(1)} collective-permute-done((bf16[4,192,128]{2,1,0:T(8,128)(2,1)S(1)}, bf16[4,192,128]{2,1,0:T(8,128)(2,1)S(1)}, u32[]{:S(2)}, u32[]{:S(2)}) %collective-permute-start) | collective-permute-done | bytes 196640 | tf_op jit(solution)/shard_map/ppermute | solution.py:114
  34.8 3.4 %collective-permute-start.14 = (bf16[128,2048]{1,0:T(8,128)(2,1)}, bf16[128,2048]{1,0:T(8,128)(2,1)S(1)}, u32[]{:S(2)}, u32[]{:S(2)}) collective-permute-start(bf16[128,2048]{1,0:T(8,128)(2,1)} %collective-permute-done.13.refs_2_), channel_id=1, source_target_pairs={{4,8},{8,4},{5,9},{9,5},{6,10},{10,6},{7,11},{11,7},{20,24},{24,20... | collective-permute-start | bytes 1572872 | tf_op jit(solution)/shard_map/ppermute | solution.py:114
  39.7 2.2 %collective-permute-start.12 = (bf16[128,2048]{1,0:T(8,128)(2,1)S(1)}, bf16[128,2048]{1,0:T(8,128)(2,1)S(1)}, u32[]{:S(2)}, u32[]{:S(2)}) collective-permute-start(bf16[128,2048]{1,0:T(8,128)(2,1)S(1)} %collective-permute-done.11.refs_1_), channel_id=1, source_target_pairs={{4,0},{8,12},{5,1},{9,13},{6,2},{10,14},{7,3},{11,15},{20,16},{24,... | collective-permute-start | bytes 1572872 | tf_op jit(solution)/shard_map/ppermute | solution.py:114
  41.9 4.5 %collective-permute-done.2 = bf16[128,2048]{1,0:T(8,128)(2,1)S(1)} collective-permute-done((bf16[128,2048]{1,0:T(8,128)(2,1)S(1)}, bf16[128,2048]{1,0:T(8,128)(2,1)S(1)}, u32[]{:S(2)}, u32[]{:S(2)}) %collective-permute-start.2) | collective-permute-done | bytes 524320 | tf_op jit(solution)/shard_map/ppermute | solution.py:114
  46.5 1.6 %collective-permute-start.9 = (f32[192,256]{1,0:T(8,128)S(1)}, f32[192,256]{1,0:T(8,128)S(1)}, u32[]{:S(2)}, u32[]{:S(2)}) collective-permute-start(f32[192,256]{1,0:T(8,128)S(1)} %fusion.3), channel_id=1, source_target_pairs={{0,2},{2,0},{1,3},{3,1},{4,6},{6,4},{5,7},{7,5},{8,10},{10,8},{9,1... | collective-permute-start | bytes 589832 | tf_op jit(solution)/shard_map/ppermute | solution.py:114
  48.2 3.5 %collective-permute-start.3 = (bf16[128,2048]{1,0:T(8,128)(2,1)S(1)}, bf16[128,2048]{1,0:T(8,128)(2,1)S(1)}, u32[]{:S(2)}, u32[]{:S(2)}) collective-permute-start(bf16[128,2048]{1,0:T(8,128)(2,1)S(1)} %get-tuple-element.50), channel_id=1, source_target_pairs={{4,8},{8,4},{5,9},{9,5},{6,10},{10,6},{7,11},{11,7},{20,24},{24,20... | collective-permute-start | bytes 1572872 | tf_op jit(solution)/shard_map/ppermute | solution.py:114
  56.4 2.4 %shard_map.85 = f32[2,192,384]{2,1,0:T(8,128)S(1)} custom-call(s32[1]{0:T(128)} %bitcast.14.place_ref, bf16[192,2048]{1,0:T(8,128)(2,1)S(1)} %get-tuple-element.47.err_own_ref.own_ref, bf16[192,2048]{1,0:T(8,128)(2,1)S(1)} %collective-permute-done.1.err_other_ref.other_ref, bf16[128,2048]{1,0:T(8,128)(2,1)S(1)} %broadcast_select_fusion.refs_0_, ...), custom_call_target="tpu_custom_call" | custom-call | tf_op jit(solution)/shard_map/pallas_call | solution.py:34
  59.1 3.4 %collective-permute-done.3 = bf16[128,2048]{1,0:T(8,128)(2,1)S(1)} collective-permute-done((bf16[128,2048]{1,0:T(8,128)(2,1)S(1)}, bf16[128,2048]{1,0:T(8,128)(2,1)S(1)}, u32[]{:S(2)}, u32[]{:S(2)}) %collective-permute-start.3) | collective-permute-done | bytes 524320 | tf_op jit(solution)/shard_map/ppermute | solution.py:114
  62.7 1.6 %collective-permute-start.16 = (f32[192,384]{1,0:T(8,128)S(1)}, f32[192,384]{1,0:T(8,128)S(1)}, u32[]{:S(2)}, u32[]{:S(2)}) collective-permute-start(f32[192,384]{1,0:T(8,128)S(1)} %fusion.2), channel_id=1, source_target_pairs={{0,2},{2,0},{1,3},{3,1},{4,6},{6,4},{5,7},{7,5},{8,10},{10,8},{9,1... | collective-permute-start | bytes 884744 | tf_op jit(solution)/shard_map/ppermute | solution.py:114
  64.2 4.3 %collective-permute-done.5 = bf16[128,2048]{1,0:T(8,128)(2,1)S(1)} collective-permute-done((bf16[128,2048]{1,0:T(8,128)(2,1)S(1)}, bf16[128,2048]{1,0:T(8,128)(2,1)S(1)}, u32[]{:S(2)}, u32[]{:S(2)}) %collective-permute-start.5) | collective-permute-done | bytes 524320 | tf_op jit(solution)/shard_map/ppermute | solution.py:114
  70.1 2.6 %collective-permute-start.4 = (bf16[128,2048]{1,0:T(8,128)(2,1)S(1)}, bf16[128,2048]{1,0:T(8,128)(2,1)S(1)}, u32[]{:S(2)}, u32[]{:S(2)}) collective-permute-start(bf16[128,2048]{1,0:T(8,128)(2,1)S(1)} %add_convert_fusion.6), channel_id=1, source_target_pairs={{0,4},{4,0},{8,12},{12,8},{1,5},{5,1},{9,13},{13,9},{2,6},{6,2},{1... | collective-permute-start | bytes 1572872 | tf_op jit(solution)/shard_map/ppermute | solution.py:114
  73.2 3.8 %collective-permute-done.18 = bf16[128,2048]{1,0:T(8,128)(2,1)S(1)} collective-permute-done((bf16[128,2048]{1,0:T(8,128)(2,1)S(1)}, bf16[128,2048]{1,0:T(8,128)(2,1)S(1)}, u32[]{:S(2)}, u32[]{:S(2)}) %collective-permute-start.18) | collective-permute-done | bytes 524320 | tf_op jit(solution)/shard_map/ppermute | solution.py:114
  77.2 2.3 %collective-permute-start.19 = (bf16[128,2048]{1,0:T(8,128)(2,1)S(1)}, bf16[128,2048]{1,0:T(8,128)(2,1)S(1)}, u32[]{:S(2)}, u32[]{:S(2)}) collective-permute-start(bf16[128,2048]{1,0:T(8,128)(2,1)S(1)} %get-tuple-element.48), channel_id=1, source_target_pairs={{4,8},{8,4},{5,9},{9,5},{6,10},{10,6},{7,11},{11,7},{20,24},{24,20... | collective-permute-start | bytes 1572872 | tf_op jit(solution)/shard_map/ppermute | solution.py:114
  80.8 3.5 %collective-permute-start.6 = (bf16[128,2048]{1,0:T(8,128)(2,1)S(1)}, bf16[128,2048]{1,0:T(8,128)(2,1)S(1)}, u32[]{:S(2)}, u32[]{:S(2)}) collective-permute-start(bf16[128,2048]{1,0:T(8,128)(2,1)S(1)} %add_convert_fusion.5), channel_id=1, source_target_pairs={{4,8},{8,4},{5,9},{9,5},{6,10},{10,6},{7,11},{11,7},{20,24},{24,20... | collective-permute-start | bytes 1572872 | tf_op jit(solution)/shard_map/ppermute | solution.py:114
  85.3 3.0 %collective-permute-done.4 = bf16[128,2048]{1,0:T(8,128)(2,1)S(1)} collective-permute-done((bf16[128,2048]{1,0:T(8,128)(2,1)S(1)}, bf16[128,2048]{1,0:T(8,128)(2,1)S(1)}, u32[]{:S(2)}, u32[]{:S(2)}) %collective-permute-start.4) | collective-permute-done | bytes 524320 | tf_op jit(solution)/shard_map/ppermute | solution.py:114
  88.3 5.7 %collective-permute-done.19 = bf16[128,2048]{1,0:T(8,128)(2,1)S(1)} collective-permute-done((bf16[128,2048]{1,0:T(8,128)(2,1)S(1)}, bf16[128,2048]{1,0:T(8,128)(2,1)S(1)}, u32[]{:S(2)}, u32[]{:S(2)}) %collective-permute-start.19) | collective-permute-done | bytes 524320 | tf_op jit(solution)/shard_map/ppermute | solution.py:114
  94.1 5.4 %collective-permute-done.21 = bf16[128,2048]{1,0:T(8,128)(2,1)S(1)} collective-permute-done((bf16[128,2048]{1,0:T(8,128)(2,1)S(1)}, bf16[128,2048]{1,0:T(8,128)(2,1)S(1)}, u32[]{:S(2)}, u32[]{:S(2)}) %collective-permute-start.21) | collective-permute-done | bytes 524320 | tf_op jit(solution)/shard_map/ppermute | solution.py:114
  99.6 2.3 %collective-permute-start.22 = (bf16[128,2048]{1,0:T(8,128)(2,1)S(1)}, bf16[128,2048]{1,0:T(8,128)(2,1)S(1)}, u32[]{:S(2)}, u32[]{:S(2)}) collective-permute-start(bf16[128,2048]{1,0:T(8,128)(2,1)S(1)} %add_convert_fusion.1), channel_id=1, source_target_pairs={{4,8},{8,4},{5,9},{9,5},{6,10},{10,6},{7,11},{11,7},{20,24},{24,20... | collective-permute-start | bytes 1572872 | tf_op jit(solution)/shard_map/ppermute | solution.py:114
  103.9 5.3 %collective-permute-done.20 = bf16[128,2048]{1,0:T(8,128)(2,1)S(1)} collective-permute-done((bf16[128,2048]{1,0:T(8,128)(2,1)S(1)}, bf16[128,2048]{1,0:T(8,128)(2,1)S(1)}, u32[]{:S(2)}, u32[]{:S(2)}) %collective-permute-start.20) | collective-permute-done | bytes 524320 | tf_op jit(solution)/shard_map/ppermute | solution.py:114
  109.3 3.2 %collective-permute-done.22 = bf16[128,2048]{1,0:T(8,128)(2,1)S(1)} collective-permute-done((bf16[128,2048]{1,0:T(8,128)(2,1)S(1)}, bf16[128,2048]{1,0:T(8,128)(2,1)S(1)}, u32[]{:S(2)}, u32[]{:S(2)}) %collective-permute-start.22) | collective-permute-done | bytes 524320 | tf_op jit(solution)/shard_map/ppermute | solution.py:114
  (89 shorter events, 21.0 us)
Async XLA Ops:
  0.6 11.4 %all-to-all-start = ((bf16[4,192,128]{2,1,0:T(8,128)(2,1)}), bf16[4,192,128]{2,1,0:T(8,128)(2,1)S(1)}, u32[]{:S(2)}, u32[]{:S(2)}) async-start(bf16[4,192,128]{2,1,0:T(8,128)(2,1)} %bitcast.49), calls=%async_computation | async-start | bytes 393216 | tf_op jit(solution)/shard_map/all_to_all | solution.py:129
  8.6 23.3 %collective-permute-start.1 = (bf16[192,2048]{1,0:T(8,128)(2,1)}, bf16[192,2048]{1,0:T(8,128)(2,1)S(1)}, u32[]{:S(2)}, u32[]{:S(2)}) collective-permute-start(bf16[192,2048]{1,0:T(8,128)(2,1)} %get-tuple-element.46), channel_id=1, source_target_pairs={{0,2},{2,0},{1,3},{3,1},{4,6},{6,4},{5,7},{7,5},{8,10},{10,8},{9,1... | collective-permute-start | bytes 2359304 | tf_op jit(solution)/shard_map/ppermute | solution.py:114
  10.1 24.7 %collective-permute-start.13 = (bf16[128,2048]{1,0:T(8,128)(2,1)S(1)}, bf16[128,2048]{1,0:T(8,128)(2,1)}, u32[]{:S(2)}, u32[]{:S(2)}) collective-permute-start(bf16[128,2048]{1,0:T(8,128)(2,1)S(1)} %dynamic-slice_bitcast_fusion.2.refs_0_), channel_id=1, source_target_pairs={{0,4},{4,0},{8,12},{12,8},{1,5},{5,1},{9,13},{13,9},{2,6},{6,2},{1... | collective-permute-start | bytes 1572872 | tf_op jit(solution)/shard_map/ppermute | solution.py:114
  12.1 21.6 %collective-permute-start.7 = (bf16[128,2048]{1,0:T(8,128)(2,1)S(1)}, bf16[128,2048]{1,0:T(8,128)(2,1)S(1)}, u32[]{:S(2)}, u32[]{:S(2)}) collective-permute-start(bf16[128,2048]{1,0:T(8,128)(2,1)S(1)} %dynamic-slice_bitcast_fusion.2.refs_0_), channel_id=1, source_target_pairs={{0,12},{12,0},{1,13},{13,1},{2,14},{14,2},{3,15},{15,3},{16,28},{2... | collective-permute-start | bytes 1572872 | tf_op jit(solution)/shard_map/ppermute | solution.py:114
  12.8 26.9 %collective-permute-start.11 = (bf16[128,2048]{1,0:T(8,128)(2,1)S(1)}, bf16[128,2048]{1,0:T(8,128)(2,1)S(1)}, u32[]{:S(2)}, u32[]{:S(2)}) collective-permute-start(bf16[128,2048]{1,0:T(8,128)(2,1)S(1)} %dynamic-slice_bitcast_fusion.2.refs_0_), channel_id=1, source_target_pairs={{4,8},{8,4},{5,9},{9,5},{6,10},{10,6},{7,11},{11,7},{20,24},{24,20... | collective-permute-start | bytes 1572872 | tf_op jit(solution)/shard_map/ppermute | solution.py:114
  17.5 14.2 %collective-permute-start = (bf16[4,192,128]{2,1,0:T(8,128)(2,1)S(1)}, bf16[4,192,128]{2,1,0:T(8,128)(2,1)S(1)}, u32[]{:S(2)}, u32[]{:S(2)}) collective-permute-start(bf16[4,192,128]{2,1,0:T(8,128)(2,1)S(1)} %all-to-all-done), channel_id=1, source_target_pairs={{0,2},{2,0},{1,3},{3,1},{4,6},{6,4},{5,7},{7,5},{8,10},{10,8},{9,1... | collective-permute-start | bytes 589832 | tf_op jit(solution)/shard_map/ppermute | solution.py:114
  32.4 14.1 %collective-permute-start.2 = (bf16[128,2048]{1,0:T(8,128)(2,1)S(1)}, bf16[128,2048]{1,0:T(8,128)(2,1)S(1)}, u32[]{:S(2)}, u32[]{:S(2)}) collective-permute-start(bf16[128,2048]{1,0:T(8,128)(2,1)S(1)} %shard_map.80), channel_id=1, source_target_pairs={{0,4},{12,8},{1,5},{13,9},{2,6},{14,10},{3,7},{15,11},{16,20},{28,... | collective-permute-start | bytes 1572872 | tf_op jit(solution)/shard_map/ppermute | solution.py:114
  34.7 7.2 %collective-permute-start.8 = (f32[192,256]{1,0:T(8,128)S(1)}, f32[192,256]{1,0:T(8,128)S(1)}, u32[]{:S(2)}, u32[]{:S(2)}) collective-permute-start(f32[192,256]{1,0:T(8,128)S(1)} %slice_bitcast_fusion.2), channel_id=1, source_target_pairs={{0,1},{1,0},{2,3},{3,2},{4,5},{5,4},{6,7},{7,6},{8,9},{9,8},{10,11... | collective-permute-start | bytes 589832 | tf_op jit(solution)/shard_map/ppermute | solution.py:114
  34.8 18.4 %collective-permute-start.14 = (bf16[128,2048]{1,0:T(8,128)(2,1)}, bf16[128,2048]{1,0:T(8,128)(2,1)S(1)}, u32[]{:S(2)}, u32[]{:S(2)}) collective-permute-start(bf16[128,2048]{1,0:T(8,128)(2,1)} %collective-permute-done.13.refs_2_), channel_id=1, source_target_pairs={{4,8},{8,4},{5,9},{9,5},{6,10},{10,6},{7,11},{11,7},{20,24},{24,20... | collective-permute-start | bytes 1572872 | tf_op jit(solution)/shard_map/ppermute | solution.py:114
  39.7 14.0 %collective-permute-start.12 = (bf16[128,2048]{1,0:T(8,128)(2,1)S(1)}, bf16[128,2048]{1,0:T(8,128)(2,1)S(1)}, u32[]{:S(2)}, u32[]{:S(2)}) collective-permute-start(bf16[128,2048]{1,0:T(8,128)(2,1)S(1)} %collective-permute-done.11.refs_1_), channel_id=1, source_target_pairs={{4,0},{8,12},{5,1},{9,13},{6,2},{10,14},{7,3},{11,15},{20,16},{24,... | collective-permute-start | bytes 1572872 | tf_op jit(solution)/shard_map/ppermute | solution.py:114
  46.5 6.5 %collective-permute-start.9 = (f32[192,256]{1,0:T(8,128)S(1)}, f32[192,256]{1,0:T(8,128)S(1)}, u32[]{:S(2)}, u32[]{:S(2)}) collective-permute-start(f32[192,256]{1,0:T(8,128)S(1)} %fusion.3), channel_id=1, source_target_pairs={{0,2},{2,0},{1,3},{3,1},{4,6},{6,4},{5,7},{7,5},{8,10},{10,8},{9,1... | collective-permute-start | bytes 589832 | tf_op jit(solution)/shard_map/ppermute | solution.py:114
  48.2 14.3 %collective-permute-start.3 = (bf16[128,2048]{1,0:T(8,128)(2,1)S(1)}, bf16[128,2048]{1,0:T(8,128)(2,1)S(1)}, u32[]{:S(2)}, u32[]{:S(2)}) collective-permute-start(bf16[128,2048]{1,0:T(8,128)(2,1)S(1)} %get-tuple-element.50), channel_id=1, source_target_pairs={{4,8},{8,4},{5,9},{9,5},{6,10},{10,6},{7,11},{11,7},{20,24},{24,20... | collective-permute-start | bytes 1572872 | tf_op jit(solution)/shard_map/ppermute | solution.py:114
  51.7 16.8 %collective-permute-start.5 = (bf16[128,2048]{1,0:T(8,128)(2,1)S(1)}, bf16[128,2048]{1,0:T(8,128)(2,1)S(1)}, u32[]{:S(2)}, u32[]{:S(2)}) collective-permute-start(bf16[128,2048]{1,0:T(8,128)(2,1)S(1)} %get-tuple-element.51), channel_id=1, source_target_pairs={{0,4},{12,8},{1,5},{13,9},{2,6},{14,10},{3,7},{15,11},{16,20},{28,... | collective-permute-start | bytes 1572872 | tf_op jit(solution)/shard_map/ppermute | solution.py:114
  53.2 1.4 %collective-permute-start.10 = (bf16[192,256]{1,0:T(8,128)(2,1)S(1)}, bf16[192,256]{1,0:T(8,128)(2,1)S(1)}, u32[]{:S(2)}, u32[]{:S(2)}) collective-permute-start(bf16[192,256]{1,0:T(8,128)(2,1)S(1)} %pad_maximum_fusion.1), channel_id=1, source_target_pairs={{0,1},{1,0},{2,3},{3,2},{4,5},{5,4},{6,7},{7,6},{8,9},{9,8},{10,11... | collective-permute-start | bytes 294920 | tf_op jit(solution)/shard_map/ppermute | solution.py:114
  55.1 21.9 %collective-permute-start.18 = (bf16[128,2048]{1,0:T(8,128)(2,1)S(1)}, bf16[128,2048]{1,0:T(8,128)(2,1)S(1)}, u32[]{:S(2)}, u32[]{:S(2)}) collective-permute-start(bf16[128,2048]{1,0:T(8,128)(2,1)S(1)} %shard_map.84), channel_id=1, source_target_pairs={{0,4},{12,8},{1,5},{13,9},{2,6},{14,10},{3,7},{15,11},{16,20},{28,... | collective-permute-start | bytes 1572872 | tf_op jit(solution)/shard_map/ppermute | solution.py:114
  58.8 3.8 %collective-permute-start.15 = (f32[192,384]{1,0:T(8,128)S(1)}, f32[192,384]{1,0:T(8,128)S(1)}, u32[]{:S(2)}, u32[]{:S(2)}) collective-permute-start(f32[192,384]{1,0:T(8,128)S(1)} %slice_bitcast_fusion), channel_id=1, source_target_pairs={{0,1},{1,0},{2,3},{3,2},{4,5},{5,4},{6,7},{7,6},{8,9},{9,8},{10,11... | collective-permute-start | bytes 884744 | tf_op jit(solution)/shard_map/ppermute | solution.py:114
  62.7 7.2 %collective-permute-start.16 = (f32[192,384]{1,0:T(8,128)S(1)}, f32[192,384]{1,0:T(8,128)S(1)}, u32[]{:S(2)}, u32[]{:S(2)}) collective-permute-start(f32[192,384]{1,0:T(8,128)S(1)} %fusion.2), channel_id=1, source_target_pairs={{0,2},{2,0},{1,3},{3,1},{4,6},{6,4},{5,7},{7,5},{8,10},{10,8},{9,1... | collective-permute-start | bytes 884744 | tf_op jit(solution)/shard_map/ppermute | solution.py:114
  70.1 2.7 %collective-permute-start.17 = (bf16[192,384]{1,0:T(8,128)(2,1)S(1)}, bf16[192,384]{1,0:T(8,128)(2,1)S(1)}, u32[]{:S(2)}, u32[]{:S(2)}) collective-permute-start(bf16[192,384]{1,0:T(8,128)(2,1)S(1)} %pad_maximum_fusion), channel_id=1, source_target_pairs={{0,1},{1,0},{2,3},{3,2},{4,5},{5,4},{6,7},{7,6},{8,9},{9,8},{10,11... | collective-permute-start | bytes 442376 | tf_op jit(solution)/shard_map/ppermute | solution.py:114
  70.1 18.1 %collective-permute-start.4 = (bf16[128,2048]{1,0:T(8,128)(2,1)S(1)}, bf16[128,2048]{1,0:T(8,128)(2,1)S(1)}, u32[]{:S(2)}, u32[]{:S(2)}) collective-permute-start(bf16[128,2048]{1,0:T(8,128)(2,1)S(1)} %add_convert_fusion.6), channel_id=1, source_target_pairs={{0,4},{4,0},{8,12},{12,8},{1,5},{5,1},{9,13},{13,9},{2,6},{6,2},{1... | collective-permute-start | bytes 1572872 | tf_op jit(solution)/shard_map/ppermute | solution.py:114
  77.2 16.8 %collective-permute-start.19 = (bf16[128,2048]{1,0:T(8,128)(2,1)S(1)}, bf16[128,2048]{1,0:T(8,128)(2,1)S(1)}, u32[]{:S(2)}, u32[]{:S(2)}) collective-permute-start(bf16[128,2048]{1,0:T(8,128)(2,1)S(1)} %get-tuple-element.48), channel_id=1, source_target_pairs={{4,8},{8,4},{5,9},{9,5},{6,10},{10,6},{7,11},{11,7},{20,24},{24,20... | collective-permute-start | bytes 1572872 | tf_op jit(solution)/shard_map/ppermute | solution.py:114
  79.5 20.0 %collective-permute-start.21 = (bf16[128,2048]{1,0:T(8,128)(2,1)S(1)}, bf16[128,2048]{1,0:T(8,128)(2,1)S(1)}, u32[]{:S(2)}, u32[]{:S(2)}) collective-permute-start(bf16[128,2048]{1,0:T(8,128)(2,1)S(1)} %get-tuple-element.49), channel_id=1, source_target_pairs={{0,4},{12,8},{1,5},{13,9},{2,6},{14,10},{3,7},{15,11},{16,20},{28,... | collective-permute-start | bytes 1572872 | tf_op jit(solution)/shard_map/ppermute | solution.py:114
  80.8 22.1 %collective-permute-start.6 = (bf16[128,2048]{1,0:T(8,128)(2,1)S(1)}, bf16[128,2048]{1,0:T(8,128)(2,1)S(1)}, u32[]{:S(2)}, u32[]{:S(2)}) collective-permute-start(bf16[128,2048]{1,0:T(8,128)(2,1)S(1)} %add_convert_fusion.5), channel_id=1, source_target_pairs={{4,8},{8,4},{5,9},{9,5},{6,10},{10,6},{7,11},{11,7},{20,24},{24,20... | collective-permute-start | bytes 1572872 | tf_op jit(solution)/shard_map/ppermute | solution.py:114
  94.0 15.2 %collective-permute-start.20 = (bf16[128,2048]{1,0:T(8,128)(2,1)S(1)}, bf16[128,2048]{1,0:T(8,128)(2,1)S(1)}, u32[]{:S(2)}, u32[]{:S(2)}) collective-permute-start(bf16[128,2048]{1,0:T(8,128)(2,1)S(1)} %add_convert_fusion.2), channel_id=1, source_target_pairs={{0,4},{4,0},{8,12},{12,8},{1,5},{5,1},{9,13},{13,9},{2,6},{6,2},{1... | collective-permute-start | bytes 1572872 | tf_op jit(solution)/shard_map/ppermute | solution.py:114
  99.6 12.9 %collective-permute-start.22 = (bf16[128,2048]{1,0:T(8,128)(2,1)S(1)}, bf16[128,2048]{1,0:T(8,128)(2,1)S(1)}, u32[]{:S(2)}, u32[]{:S(2)}) collective-permute-start(bf16[128,2048]{1,0:T(8,128)(2,1)S(1)} %add_convert_fusion.1), channel_id=1, source_target_pairs={{4,8},{8,4},{5,9},{9,5},{6,10},{10,6},{7,11},{11,7},{20,24},{24,20... | collective-permute-start | bytes 1572872 | tf_op jit(solution)/shard_map/ppermute | solution.py:114
  (4 other events, 24.1 us)

commit v7 on v5

--- a/solution.py
+++ b/solution.py
@@ -34,7 +34,7 @@
         out_shape=out_shape,
         in_specs=[pl.BlockSpec(memory_space=pltpu.SMEM)] + [vmem] * len(args),
         out_specs=jax.tree.map(lambda _: vmem, out_shape),
-        compiler_params=pltpu.CompilerParams(vmem_limit_bytes=32 * 2**20),
+        compiler_params=pltpu.CompilerParams(vmem_limit_bytes=12 * 2**20),
         cost_estimate=pl.CostEstimate(flops=0, bytes_accessed=0, transcendentals=0),
     )(jnp.stack(scalars).astype(jnp.int32), *args)
 

time: 114 us -> 114 us (level)
  no operation moved by 1% of the time
where the time goes in v7:
time: 114 us
  waiting for transfers between devices  54.9 us (48%)
  starting transfers between devices  41.5 us (36%)
  Pallas kernels  8.21 us (7%)
  local copies, waits for them, and re-layouts  4.56 us (4%)
  other arithmetic  3.35 us (3%)
  between operations  1.17 us (1%)
    ppermute x23, waiting for transfers between devices, send(): step(name, lambda: lax.ppermute(get(name + '_in'), axis, pairs))  54.8 us
    ppermute x23, starting transfers between devices, send(): step(name, lambda: lax.ppermute(get(name + '_in'), axis, pairs))  36 us
    pallas_call x12, Pallas kernels, local_call(): pl.pallas_call(body, out_shape=out_shape, in_specs=[pl.BlockSpec(memory_s...  8.21 us
    all_to_all x1, starting transfers between devices, shards_line(): lax.all_to_all(get('codes_in'), 'lat', split_axis=0, concat_axis=0, tiled...  5.46 us
    dynamic_slice x1, local copies, waits for them, and re-layouts, shards_line(): lax.dynamic_slice_in_dim(err_rows, (1 - x) * width, width, 1)  2.45 us
  transfers between devices with their start and end apart: 24, of which 14 were waited for; matrix products, arithmetic and copies ran while one was open for 6% of the time, Pallas kernels for 7%

profile of v7, /device:TPU:12, one launch (start us, length us, event | category | flops | bytes accessed | tf_op | source)
XLA Modules:
  0.0 113.6 jit_solution(14389950155663109257)
XLA Ops:
  0.6 5.5 %all-to-all-start = ((bf16[4,192,128]{2,1,0:T(8,128)(2,1)}), bf16[4,192,128]{2,1,0:T(8,128)(2,1)S(1)}, u32[]{:S(2)}, u32[]{:S(2)}) async-start(bf16[4,192,128]{2,1,0:T(8,128)(2,1)} %bitcast.49), calls=%async_computation | async-start | bytes 393216 | tf_op jit(solution)/shard_map/all_to_all | solution.py:127
  6.1 2.4 %dynamic-slice_bitcast_fusion = (bf16[192,2048]{1,0:T(8,128)(2,1)}, bf16[192,2048]{1,0:T(8,128)(2,1)S(1)}) fusion(bf16[1,192,1,4096]{3,1,2,0:T(8,128)(2,1)} %param.7, s32[]{:T(128)S(6)} %select_n.60, s32[]{:T(128)S(6)} %select_n.59), kind=kLoop, calls=%fused_computation.8 | loop fusion | bytes 3145736 | tf_op jit(solution)/shard_map/dynamic_slice | solution.py:124
  8.6 1.5 %collective-permute-start.1 = (bf16[192,2048]{1,0:T(8,128)(2,1)}, bf16[192,2048]{1,0:T(8,128)(2,1)S(1)}, u32[]{:S(2)}, u32[]{:S(2)}) collective-permute-start(bf16[192,2048]{1,0:T(8,128)(2,1)} %get-tuple-element.42), channel_id=1, source_target_pairs={{0,2},{2,0},{1,3},{3,1},{4,6},{6,4},{5,7},{7,5},{8,10},{10,8},{9,1... | collective-permute-start | bytes 2359304 | tf_op jit(solution)/shard_map/ppermute | solution.py:112
  12.8 4.7 %collective-permute-start.11 = (bf16[128,2048]{1,0:T(8,128)(2,1)S(1)}, bf16[128,2048]{1,0:T(8,128)(2,1)S(1)}, u32[]{:S(2)}, u32[]{:S(2)}) collective-permute-start(bf16[128,2048]{1,0:T(8,128)(2,1)S(1)} %dynamic-slice_bitcast_fusion.2.refs_0_), channel_id=1, source_target_pairs={{4,8},{8,4},{5,9},{9,5},{6,10},{10,6},{7,11},{11,7},{20,24},{24,20... | collective-permute-start | bytes 1572872 | tf_op jit(solution)/shard_map/ppermute | solution.py:112
  18.2 13.5 %collective-permute-done = bf16[4,192,128]{2,1,0:T(8,128)(2,1)S(1)} collective-permute-done((bf16[4,192,128]{2,1,0:T(8,128)(2,1)S(1)}, bf16[4,192,128]{2,1,0:T(8,128)(2,1)S(1)}, u32[]{:S(2)}, u32[]{:S(2)}) %collective-permute-start) | collective-permute-done | bytes 196640 | tf_op jit(solution)/shard_map/ppermute | solution.py:112
  34.8 3.4 %collective-permute-start.14 = (bf16[128,2048]{1,0:T(8,128)(2,1)}, bf16[128,2048]{1,0:T(8,128)(2,1)S(1)}, u32[]{:S(2)}, u32[]{:S(2)}) collective-permute-start(bf16[128,2048]{1,0:T(8,128)(2,1)} %collective-permute-done.13.refs_2_), channel_id=1, source_target_pairs={{4,8},{8,4},{5,9},{9,5},{6,10},{10,6},{7,11},{11,7},{20,24},{24,20... | collective-permute-start | bytes 1572872 | tf_op jit(solution)/shard_map/ppermute | solution.py:112
  39.7 2.2 %collective-permute-start.12 = (bf16[128,2048]{1,0:T(8,128)(2,1)S(1)}, bf16[128,2048]{1,0:T(8,128)(2,1)S(1)}, u32[]{:S(2)}, u32[]{:S(2)}) collective-permute-start(bf16[128,2048]{1,0:T(8,128)(2,1)S(1)} %collective-permute-done.11.refs_1_), channel_id=1, source_target_pairs={{4,0},{8,12},{5,1},{9,13},{6,2},{10,14},{7,3},{11,15},{20,16},{24,... | collective-permute-start | bytes 1572872 | tf_op jit(solution)/shard_map/ppermute | solution.py:112
  41.9 4.5 %collective-permute-done.2 = bf16[128,2048]{1,0:T(8,128)(2,1)S(1)} collective-permute-done((bf16[128,2048]{1,0:T(8,128)(2,1)S(1)}, bf16[128,2048]{1,0:T(8,128)(2,1)S(1)}, u32[]{:S(2)}, u32[]{:S(2)}) %collective-permute-start.2) | collective-permute-done | bytes 524320 | tf_op jit(solution)/shard_map/ppermute | solution.py:112
  46.5 1.6 %collective-permute-start.9 = (f32[192,256]{1,0:T(8,128)S(1)}, f32[192,256]{1,0:T(8,128)S(1)}, u32[]{:S(2)}, u32[]{:S(2)}) collective-permute-start(f32[192,256]{1,0:T(8,128)S(1)} %fusion.3), channel_id=1, source_target_pairs={{0,2},{2,0},{1,3},{3,1},{4,6},{6,4},{5,7},{7,5},{8,10},{10,8},{9,1... | collective-permute-start | bytes 589832 | tf_op jit(solution)/shard_map/ppermute | solution.py:112
  48.2 3.5 %collective-permute-start.3 = (bf16[128,2048]{1,0:T(8,128)(2,1)S(1)}, bf16[128,2048]{1,0:T(8,128)(2,1)S(1)}, u32[]{:S(2)}, u32[]{:S(2)}) collective-permute-start(bf16[128,2048]{1,0:T(8,128)(2,1)S(1)} %add_convert_fusion.7), channel_id=1, source_target_pairs={{4,8},{8,4},{5,9},{9,5},{6,10},{10,6},{7,11},{11,7},{20,24},{24,20... | collective-permute-start | bytes 1572872 | tf_op jit(solution)/shard_map/ppermute | solution.py:112
  56.3 2.4 %shard_map.85 = f32[2,192,384]{2,1,0:T(8,128)S(1)} custom-call(s32[1]{0:T(128)} %bitcast.14.place_ref, bf16[192,2048]{1,0:T(8,128)(2,1)S(1)} %get-tuple-element.43.err_own_ref.own_ref, bf16[192,2048]{1,0:T(8,128)(2,1)S(1)} %collective-permute-done.1.err_other_ref.other_ref, bf16[128,2048]{1,0:T(8,128)(2,1)S(1)} %broadcast_select_fusion.refs_0_, ...), custom_call_target="tpu_custom_call" | custom-call | tf_op jit(solution)/shard_map/pallas_call | solution.py:32
  59.0 3.5 %collective-permute-done.3 = bf16[128,2048]{1,0:T(8,128)(2,1)S(1)} collective-permute-done((bf16[128,2048]{1,0:T(8,128)(2,1)S(1)}, bf16[128,2048]{1,0:T(8,128)(2,1)S(1)}, u32[]{:S(2)}, u32[]{:S(2)}) %collective-permute-start.3) | collective-permute-done | bytes 524320 | tf_op jit(solution)/shard_map/ppermute | solution.py:112
  62.7 1.6 %collective-permute-start.16 = (f32[192,384]{1,0:T(8,128)S(1)}, f32[192,384]{1,0:T(8,128)S(1)}, u32[]{:S(2)}, u32[]{:S(2)}) collective-permute-start(f32[192,384]{1,0:T(8,128)S(1)} %fusion.2), channel_id=1, source_target_pairs={{0,2},{2,0},{1,3},{3,1},{4,6},{6,4},{5,7},{7,5},{8,10},{10,8},{9,1... | collective-permute-start | bytes 884744 | tf_op jit(solution)/shard_map/ppermute | solution.py:112
  64.2 4.2 %collective-permute-done.5 = bf16[128,2048]{1,0:T(8,128)(2,1)S(1)} collective-permute-done((bf16[128,2048]{1,0:T(8,128)(2,1)S(1)}, bf16[128,2048]{1,0:T(8,128)(2,1)S(1)}, u32[]{:S(2)}, u32[]{:S(2)}) %collective-permute-start.5) | collective-permute-done | bytes 524320 | tf_op jit(solution)/shard_map/ppermute | solution.py:112
  70.2 2.5 %collective-permute-start.4 = (bf16[128,2048]{1,0:T(8,128)(2,1)S(1)}, bf16[128,2048]{1,0:T(8,128)(2,1)S(1)}, u32[]{:S(2)}, u32[]{:S(2)}) collective-permute-start(bf16[128,2048]{1,0:T(8,128)(2,1)S(1)} %add_convert_fusion.6), channel_id=1, source_target_pairs={{0,4},{4,0},{8,12},{12,8},{1,5},{5,1},{9,13},{13,9},{2,6},{6,2},{1... | collective-permute-start | bytes 1572872 | tf_op jit(solution)/shard_map/ppermute | solution.py:112
  73.2 3.8 %collective-permute-done.18 = bf16[128,2048]{1,0:T(8,128)(2,1)S(1)} collective-permute-done((bf16[128,2048]{1,0:T(8,128)(2,1)S(1)}, bf16[128,2048]{1,0:T(8,128)(2,1)S(1)}, u32[]{:S(2)}, u32[]{:S(2)}) %collective-permute-start.18) | collective-permute-done | bytes 524320 | tf_op jit(solution)/shard_map/ppermute | solution.py:112
  77.1 2.2 %collective-permute-start.19 = (bf16[128,2048]{1,0:T(8,128)(2,1)S(1)}, bf16[128,2048]{1,0:T(8,128)(2,1)S(1)}, u32[]{:S(2)}, u32[]{:S(2)}) collective-permute-start(bf16[128,2048]{1,0:T(8,128)(2,1)S(1)} %add_convert_fusion.3), channel_id=1, source_target_pairs={{4,8},{8,4},{5,9},{9,5},{6,10},{10,6},{7,11},{11,7},{20,24},{24,20... | collective-permute-start | bytes 1572872 | tf_op jit(solution)/shard_map/ppermute | solution.py:112
  80.6 3.6 %collective-permute-start.6 = (bf16[128,2048]{1,0:T(8,128)(2,1)S(1)}, bf16[128,2048]{1,0:T(8,128)(2,1)S(1)}, u32[]{:S(2)}, u32[]{:S(2)}) collective-permute-start(bf16[128,2048]{1,0:T(8,128)(2,1)S(1)} %add_convert_fusion.5), channel_id=1, source_target_pairs={{4,8},{8,4},{5,9},{9,5},{6,10},{10,6},{7,11},{11,7},{20,24},{24,20... | collective-permute-start | bytes 1572872 | tf_op jit(solution)/shard_map/ppermute | solution.py:112
  85.2 3.0 %collective-permute-done.4 = bf16[128,2048]{1,0:T(8,128)(2,1)S(1)} collective-permute-done((bf16[128,2048]{1,0:T(8,128)(2,1)S(1)}, bf16[128,2048]{1,0:T(8,128)(2,1)S(1)}, u32[]{:S(2)}, u32[]{:S(2)}) %collective-permute-start.4) | collective-permute-done | bytes 524320 | tf_op jit(solution)/shard_map/ppermute | solution.py:112
  88.2 5.6 %collective-permute-done.19 = bf16[128,2048]{1,0:T(8,128)(2,1)S(1)} collective-permute-done((bf16[128,2048]{1,0:T(8,128)(2,1)S(1)}, bf16[128,2048]{1,0:T(8,128)(2,1)S(1)}, u32[]{:S(2)}, u32[]{:S(2)}) %collective-permute-start.19) | collective-permute-done | bytes 524320 | tf_op jit(solution)/shard_map/ppermute | solution.py:112
  94.0 5.4 %collective-permute-done.21 = bf16[128,2048]{1,0:T(8,128)(2,1)S(1)} collective-permute-done((bf16[128,2048]{1,0:T(8,128)(2,1)S(1)}, bf16[128,2048]{1,0:T(8,128)(2,1)S(1)}, u32[]{:S(2)}, u32[]{:S(2)}) %collective-permute-start.21) | collective-permute-done | bytes 524320 | tf_op jit(solution)/shard_map/ppermute | solution.py:112
  99.5 2.2 %collective-permute-start.22 = (bf16[128,2048]{1,0:T(8,128)(2,1)S(1)}, bf16[128,2048]{1,0:T(8,128)(2,1)S(1)}, u32[]{:S(2)}, u32[]{:S(2)}) collective-permute-start(bf16[128,2048]{1,0:T(8,128)(2,1)S(1)} %add_convert_fusion.1), channel_id=1, source_target_pairs={{4,8},{8,4},{5,9},{9,5},{6,10},{10,6},{7,11},{11,7},{20,24},{24,20... | collective-permute-start | bytes 1572872 | tf_op jit(solution)/shard_map/ppermute | solution.py:112
  103.8 5.4 %collective-permute-done.20 = bf16[128,2048]{1,0:T(8,128)(2,1)S(1)} collective-permute-done((bf16[128,2048]{1,0:T(8,128)(2,1)S(1)}, bf16[128,2048]{1,0:T(8,128)(2,1)S(1)}, u32[]{:S(2)}, u32[]{:S(2)}) %collective-permute-start.20) | collective-permute-done | bytes 524320 | tf_op jit(solution)/shard_map/ppermute | solution.py:112
  109.2 3.2 %collective-permute-done.22 = bf16[128,2048]{1,0:T(8,128)(2,1)S(1)} collective-permute-done((bf16[128,2048]{1,0:T(8,128)(2,1)S(1)}, bf16[128,2048]{1,0:T(8,128)(2,1)S(1)}, u32[]{:S(2)}, u32[]{:S(2)}) %collective-permute-start.22) | collective-permute-done | bytes 524320 | tf_op jit(solution)/shard_map/ppermute | solution.py:112
  (89 shorter events, 21.0 us)
Async XLA Ops:
  0.6 11.4 %all-to-all-start = ((bf16[4,192,128]{2,1,0:T(8,128)(2,1)}), bf16[4,192,128]{2,1,0:T(8,128)(2,1)S(1)}, u32[]{:S(2)}, u32[]{:S(2)}) async-start(bf16[4,192,128]{2,1,0:T(8,128)(2,1)} %bitcast.49), calls=%async_computation | async-start | bytes 393216 | tf_op jit(solution)/shard_map/all_to_all | solution.py:127
  8.6 23.3 %collective-permute-start.1 = (bf16[192,2048]{1,0:T(8,128)(2,1)}, bf16[192,2048]{1,0:T(8,128)(2,1)S(1)}, u32[]{:S(2)}, u32[]{:S(2)}) collective-permute-start(bf16[192,2048]{1,0:T(8,128)(2,1)} %get-tuple-element.42), channel_id=1, source_target_pairs={{0,2},{2,0},{1,3},{3,1},{4,6},{6,4},{5,7},{7,5},{8,10},{10,8},{9,1... | collective-permute-start | bytes 2359304 | tf_op jit(solution)/shard_map/ppermute | solution.py:112
  10.1 24.7 %collective-permute-start.13 = (bf16[128,2048]{1,0:T(8,128)(2,1)S(1)}, bf16[128,2048]{1,0:T(8,128)(2,1)}, u32[]{:S(2)}, u32[]{:S(2)}) collective-permute-start(bf16[128,2048]{1,0:T(8,128)(2,1)S(1)} %dynamic-slice_bitcast_fusion.2.refs_0_), channel_id=1, source_target_pairs={{0,4},{4,0},{8,12},{12,8},{1,5},{5,1},{9,13},{13,9},{2,6},{6,2},{1... | collective-permute-start | bytes 1572872 | tf_op jit(solution)/shard_map/ppermute | solution.py:112
  12.1 21.6 %collective-permute-start.7 = (bf16[128,2048]{1,0:T(8,128)(2,1)S(1)}, bf16[128,2048]{1,0:T(8,128)(2,1)S(1)}, u32[]{:S(2)}, u32[]{:S(2)}) collective-permute-start(bf16[128,2048]{1,0:T(8,128)(2,1)S(1)} %dynamic-slice_bitcast_fusion.2.refs_0_), channel_id=1, source_target_pairs={{0,12},{12,0},{1,13},{13,1},{2,14},{14,2},{3,15},{15,3},{16,28},{2... | collective-permute-start | bytes 1572872 | tf_op jit(solution)/shard_map/ppermute | solution.py:112
  12.8 26.9 %collective-permute-start.11 = (bf16[128,2048]{1,0:T(8,128)(2,1)S(1)}, bf16[128,2048]{1,0:T(8,128)(2,1)S(1)}, u32[]{:S(2)}, u32[]{:S(2)}) collective-permute-start(bf16[128,2048]{1,0:T(8,128)(2,1)S(1)} %dynamic-slice_bitcast_fusion.2.refs_0_), channel_id=1, source_target_pairs={{4,8},{8,4},{5,9},{9,5},{6,10},{10,6},{7,11},{11,7},{20,24},{24,20... | collective-permute-start | bytes 1572872 | tf_op jit(solution)/shard_map/ppermute | solution.py:112
  17.5 14.2 %collective-permute-start = (bf16[4,192,128]{2,1,0:T(8,128)(2,1)S(1)}, bf16[4,192,128]{2,1,0:T(8,128)(2,1)S(1)}, u32[]{:S(2)}, u32[]{:S(2)}) collective-permute-start(bf16[4,192,128]{2,1,0:T(8,128)(2,1)S(1)} %all-to-all-done), channel_id=1, source_target_pairs={{0,2},{2,0},{1,3},{3,1},{4,6},{6,4},{5,7},{7,5},{8,10},{10,8},{9,1... | collective-permute-start | bytes 589832 | tf_op jit(solution)/shard_map/ppermute | solution.py:112
  32.4 14.1 %collective-permute-start.2 = (bf16[128,2048]{1,0:T(8,128)(2,1)S(1)}, bf16[128,2048]{1,0:T(8,128)(2,1)S(1)}, u32[]{:S(2)}, u32[]{:S(2)}) collective-permute-start(bf16[128,2048]{1,0:T(8,128)(2,1)S(1)} %shard_map.80), channel_id=1, source_target_pairs={{0,4},{12,8},{1,5},{13,9},{2,6},{14,10},{3,7},{15,11},{16,20},{28,... | collective-permute-start | bytes 1572872 | tf_op jit(solution)/shard_map/ppermute | solution.py:112
  34.7 7.2 %collective-permute-start.8 = (f32[192,256]{1,0:T(8,128)S(1)}, f32[192,256]{1,0:T(8,128)S(1)}, u32[]{:S(2)}, u32[]{:S(2)}) collective-permute-start(f32[192,256]{1,0:T(8,128)S(1)} %slice_bitcast_fusion.2), channel_id=1, source_target_pairs={{0,1},{1,0},{2,3},{3,2},{4,5},{5,4},{6,7},{7,6},{8,9},{9,8},{10,11... | collective-permute-start | bytes 589832 | tf_op jit(solution)/shard_map/ppermute | solution.py:112
  34.8 18.4 %collective-permute-start.14 = (bf16[128,2048]{1,0:T(8,128)(2,1)}, bf16[128,2048]{1,0:T(8,128)(2,1)S(1)}, u32[]{:S(2)}, u32[]{:S(2)}) collective-permute-start(bf16[128,2048]{1,0:T(8,128)(2,1)} %collective-permute-done.13.refs_2_), channel_id=1, source_target_pairs={{4,8},{8,4},{5,9},{9,5},{6,10},{10,6},{7,11},{11,7},{20,24},{24,20... | collective-permute-start | bytes 1572872 | tf_op jit(solution)/shard_map/ppermute | solution.py:112
  39.7 14.0 %collective-permute-start.12 = (bf16[128,2048]{1,0:T(8,128)(2,1)S(1)}, bf16[128,2048]{1,0:T(8,128)(2,1)S(1)}, u32[]{:S(2)}, u32[]{:S(2)}) collective-permute-start(bf16[128,2048]{1,0:T(8,128)(2,1)S(1)} %collective-permute-done.11.refs_1_), channel_id=1, source_target_pairs={{4,0},{8,12},{5,1},{9,13},{6,2},{10,14},{7,3},{11,15},{20,16},{24,... | collective-permute-start | bytes 1572872 | tf_op jit(solution)/shard_map/ppermute | solution.py:112
  46.5 6.5 %collective-permute-start.9 = (f32[192,256]{1,0:T(8,128)S(1)}, f32[192,256]{1,0:T(8,128)S(1)}, u32[]{:S(2)}, u32[]{:S(2)}) collective-permute-start(f32[192,256]{1,0:T(8,128)S(1)} %fusion.3), channel_id=1, source_target_pairs={{0,2},{2,0},{1,3},{3,1},{4,6},{6,4},{5,7},{7,5},{8,10},{10,8},{9,1... | collective-permute-start | bytes 589832 | tf_op jit(solution)/shard_map/ppermute | solution.py:112
  48.2 14.3 %collective-permute-start.3 = (bf16[128,2048]{1,0:T(8,128)(2,1)S(1)}, bf16[128,2048]{1,0:T(8,128)(2,1)S(1)}, u32[]{:S(2)}, u32[]{:S(2)}) collective-permute-start(bf16[128,2048]{1,0:T(8,128)(2,1)S(1)} %add_convert_fusion.7), channel_id=1, source_target_pairs={{4,8},{8,4},{5,9},{9,5},{6,10},{10,6},{7,11},{11,7},{20,24},{24,20... | collective-permute-start | bytes 1572872 | tf_op jit(solution)/shard_map/ppermute | solution.py:112
  51.7 16.8 %collective-permute-start.5 = (bf16[128,2048]{1,0:T(8,128)(2,1)S(1)}, bf16[128,2048]{1,0:T(8,128)(2,1)S(1)}, u32[]{:S(2)}, u32[]{:S(2)}) collective-permute-start(bf16[128,2048]{1,0:T(8,128)(2,1)S(1)} %add_convert_fusion.7), channel_id=1, source_target_pairs={{0,4},{12,8},{1,5},{13,9},{2,6},{14,10},{3,7},{15,11},{16,20},{28,... | collective-permute-start | bytes 1572872 | tf_op jit(solution)/shard_map/ppermute | solution.py:112
  53.2 1.4 %collective-permute-start.10 = (bf16[192,256]{1,0:T(8,128)(2,1)S(1)}, bf16[192,256]{1,0:T(8,128)(2,1)S(1)}, u32[]{:S(2)}, u32[]{:S(2)}) collective-permute-start(bf16[192,256]{1,0:T(8,128)(2,1)S(1)} %pad_maximum_fusion.1), channel_id=1, source_target_pairs={{0,1},{1,0},{2,3},{3,2},{4,5},{5,4},{6,7},{7,6},{8,9},{9,8},{10,11... | collective-permute-start | bytes 294920 | tf_op jit(solution)/shard_map/ppermute | solution.py:112
  55.0 21.9 %collective-permute-start.18 = (bf16[128,2048]{1,0:T(8,128)(2,1)S(1)}, bf16[128,2048]{1,0:T(8,128)(2,1)S(1)}, u32[]{:S(2)}, u32[]{:S(2)}) collective-permute-start(bf16[128,2048]{1,0:T(8,128)(2,1)S(1)} %shard_map.84), channel_id=1, source_target_pairs={{0,4},{12,8},{1,5},{13,9},{2,6},{14,10},{3,7},{15,11},{16,20},{28,... | collective-permute-start | bytes 1572872 | tf_op jit(solution)/shard_map/ppermute | solution.py:112
  58.8 3.8 %collective-permute-start.15 = (f32[192,384]{1,0:T(8,128)S(1)}, f32[192,384]{1,0:T(8,128)S(1)}, u32[]{:S(2)}, u32[]{:S(2)}) collective-permute-start(f32[192,384]{1,0:T(8,128)S(1)} %slice_bitcast_fusion), channel_id=1, source_target_pairs={{0,1},{1,0},{2,3},{3,2},{4,5},{5,4},{6,7},{7,6},{8,9},{9,8},{10,11... | collective-permute-start | bytes 884744 | tf_op jit(solution)/shard_map/ppermute | solution.py:112
  62.7 7.2 %collective-permute-start.16 = (f32[192,384]{1,0:T(8,128)S(1)}, f32[192,384]{1,0:T(8,128)S(1)}, u32[]{:S(2)}, u32[]{:S(2)}) collective-permute-start(f32[192,384]{1,0:T(8,128)S(1)} %fusion.2), channel_id=1, source_target_pairs={{0,2},{2,0},{1,3},{3,1},{4,6},{6,4},{5,7},{7,5},{8,10},{10,8},{9,1... | collective-permute-start | bytes 884744 | tf_op jit(solution)/shard_map/ppermute | solution.py:112
  70.1 2.6 %collective-permute-start.17 = (bf16[192,384]{1,0:T(8,128)(2,1)S(1)}, bf16[192,384]{1,0:T(8,128)(2,1)S(1)}, u32[]{:S(2)}, u32[]{:S(2)}) collective-permute-start(bf16[192,384]{1,0:T(8,128)(2,1)S(1)} %pad_maximum_fusion), channel_id=1, source_target_pairs={{0,1},{1,0},{2,3},{3,2},{4,5},{5,4},{6,7},{7,6},{8,9},{9,8},{10,11... | collective-permute-start | bytes 442376 | tf_op jit(solution)/shard_map/ppermute | solution.py:112
  70.2 18.0 %collective-permute-start.4 = (bf16[128,2048]{1,0:T(8,128)(2,1)S(1)}, bf16[128,2048]{1,0:T(8,128)(2,1)S(1)}, u32[]{:S(2)}, u32[]{:S(2)}) collective-permute-start(bf16[128,2048]{1,0:T(8,128)(2,1)S(1)} %add_convert_fusion.6), channel_id=1, source_target_pairs={{0,4},{4,0},{8,12},{12,8},{1,5},{5,1},{9,13},{13,9},{2,6},{6,2},{1... | collective-permute-start | bytes 1572872 | tf_op jit(solution)/shard_map/ppermute | solution.py:112
  77.1 16.8 %collective-permute-start.19 = (bf16[128,2048]{1,0:T(8,128)(2,1)S(1)}, bf16[128,2048]{1,0:T(8,128)(2,1)S(1)}, u32[]{:S(2)}, u32[]{:S(2)}) collective-permute-start(bf16[128,2048]{1,0:T(8,128)(2,1)S(1)} %add_convert_fusion.3), channel_id=1, source_target_pairs={{4,8},{8,4},{5,9},{9,5},{6,10},{10,6},{7,11},{11,7},{20,24},{24,20... | collective-permute-start | bytes 1572872 | tf_op jit(solution)/shard_map/ppermute | solution.py:112
  79.3 20.1 %collective-permute-start.21 = (bf16[128,2048]{1,0:T(8,128)(2,1)S(1)}, bf16[128,2048]{1,0:T(8,128)(2,1)S(1)}, u32[]{:S(2)}, u32[]{:S(2)}) collective-permute-start(bf16[128,2048]{1,0:T(8,128)(2,1)S(1)} %add_convert_fusion.3), channel_id=1, source_target_pairs={{0,4},{12,8},{1,5},{13,9},{2,6},{14,10},{3,7},{15,11},{16,20},{28,... | collective-permute-start | bytes 1572872 | tf_op jit(solution)/shard_map/ppermute | solution.py:112
  80.6 22.1 %collective-permute-start.6 = (bf16[128,2048]{1,0:T(8,128)(2,1)S(1)}, bf16[128,2048]{1,0:T(8,128)(2,1)S(1)}, u32[]{:S(2)}, u32[]{:S(2)}) collective-permute-start(bf16[128,2048]{1,0:T(8,128)(2,1)S(1)} %add_convert_fusion.5), channel_id=1, source_target_pairs={{4,8},{8,4},{5,9},{9,5},{6,10},{10,6},{7,11},{11,7},{20,24},{24,20... | collective-permute-start | bytes 1572872 | tf_op jit(solution)/shard_map/ppermute | solution.py:112
  93.9 15.3 %collective-permute-start.20 = (bf16[128,2048]{1,0:T(8,128)(2,1)S(1)}, bf16[128,2048]{1,0:T(8,128)(2,1)S(1)}, u32[]{:S(2)}, u32[]{:S(2)}) collective-permute-start(bf16[128,2048]{1,0:T(8,128)(2,1)S(1)} %add_convert_fusion.2), channel_id=1, source_target_pairs={{0,4},{4,0},{8,12},{12,8},{1,5},{5,1},{9,13},{13,9},{2,6},{6,2},{1... | collective-permute-start | bytes 1572872 | tf_op jit(solution)/shard_map/ppermute | solution.py:112
  99.5 12.9 %collective-permute-start.22 = (bf16[128,2048]{1,0:T(8,128)(2,1)S(1)}, bf16[128,2048]{1,0:T(8,128)(2,1)S(1)}, u32[]{:S(2)}, u32[]{:S(2)}) collective-permute-start(bf16[128,2048]{1,0:T(8,128)(2,1)S(1)} %add_convert_fusion.1), channel_id=1, source_target_pairs={{4,8},{8,4},{5,9},{9,5},{6,10},{10,6},{7,11},{11,7},{20,24},{24,20... | collective-permute-start | bytes 1572872 | tf_op jit(solution)/shard_map/ppermute | solution.py:112
  (4 other events, 24.1 us)

commit v8 on v7

--- a/solution.py
+++ b/solution.py
@@ -14,6 +14,7 @@
     "w_far": ("dec",),
     "sub_near": ("dec_far",),
     "tok_near_in": ("dec_far",),
+    "w_across": ("tok_near", "w_out",),
     "w_2": ("enc_far_in",),
     "tok_rest": ("dec_pair_in", "dec_last_in",),
     "enc_mid": ("dec_pair",),

time: 114 us -> 114 us (level)
  no operation moved by 1% of the time
where the time goes in v8:
time: 114 us
  waiting for transfers between devices  54.9 us (48%)
  starting transfers between devices  41.5 us (36%)
  Pallas kernels  8.21 us (7%)
  local copies, waits for them, and re-layouts  4.56 us (4%)
  other arithmetic  3.35 us (3%)
  between operations  1.17 us (1%)
    ppermute x23, waiting for transfers between devices, send(): step(name, lambda: lax.ppermute(get(name + '_in'), axis, pairs))  54.8 us
    ppermute x23, starting transfers between devices, send(): step(name, lambda: lax.ppermute(get(name + '_in'), axis, pairs))  36 us
    pallas_call x12, Pallas kernels, local_call(): pl.pallas_call(body, out_shape=out_shape, in_specs=[pl.BlockSpec(memory_s...  8.21 us
    all_to_all x1, starting transfers between devices, shards_line(): lax.all_to_all(get('codes_in'), 'lat', split_axis=0, concat_axis=0, tiled...  5.46 us
    dynamic_slice x1, local copies, waits for them, and re-layouts, shards_line(): lax.dynamic_slice_in_dim(err_rows, (1 - x) * width, width, 1)  2.45 us
  transfers between devices with their start and end apart: 24, of which 14 were waited for; matrix products, arithmetic and copies ran while one was open for 6% of the time, Pallas kernels for 7%

profile of v8, /device:TPU:12, one launch (start us, length us, event | category | flops | bytes accessed | tf_op | source)
XLA Modules:
  0.0 113.6 jit_solution(14389950155663109257)
XLA Ops:
  0.6 5.5 %all-to-all-start = ((bf16[4,192,128]{2,1,0:T(8,128)(2,1)}), bf16[4,192,128]{2,1,0:T(8,128)(2,1)S(1)}, u32[]{:S(2)}, u32[]{:S(2)}) async-start(bf16[4,192,128]{2,1,0:T(8,128)(2,1)} %bitcast.49), calls=%async_computation | async-start | bytes 393216 | tf_op jit(solution)/shard_map/all_to_all | solution.py:128
  6.1 2.4 %dynamic-slice_bitcast_fusion = (bf16[192,2048]{1,0:T(8,128)(2,1)}, bf16[192,2048]{1,0:T(8,128)(2,1)S(1)}) fusion(bf16[1,192,1,4096]{3,1,2,0:T(8,128)(2,1)} %param.7, s32[]{:T(128)S(6)} %select_n.60, s32[]{:T(128)S(6)} %select_n.59), kind=kLoop, calls=%fused_computation.8 | loop fusion | bytes 3145736 | tf_op jit(solution)/shard_map/dynamic_slice | solution.py:125
  8.6 1.5 %collective-permute-start.1 = (bf16[192,2048]{1,0:T(8,128)(2,1)}, bf16[192,2048]{1,0:T(8,128)(2,1)S(1)}, u32[]{:S(2)}, u32[]{:S(2)}) collective-permute-start(bf16[192,2048]{1,0:T(8,128)(2,1)} %get-tuple-element.44), channel_id=1, source_target_pairs={{0,2},{2,0},{1,3},{3,1},{4,6},{6,4},{5,7},{7,5},{8,10},{10,8},{9,1... | collective-permute-start | bytes 2359304 | tf_op jit(solution)/shard_map/ppermute | solution.py:113
  12.8 4.7 %collective-permute-start.11 = (bf16[128,2048]{1,0:T(8,128)(2,1)S(1)}, bf16[128,2048]{1,0:T(8,128)(2,1)S(1)}, u32[]{:S(2)}, u32[]{:S(2)}) collective-permute-start(bf16[128,2048]{1,0:T(8,128)(2,1)S(1)} %dynamic-slice_bitcast_fusion.2.refs_0_), channel_id=1, source_target_pairs={{4,8},{8,4},{5,9},{9,5},{6,10},{10,6},{7,11},{11,7},{20,24},{24,20... | collective-permute-start | bytes 1572872 | tf_op jit(solution)/shard_map/ppermute | solution.py:113
  18.2 13.5 %collective-permute-done = bf16[4,192,128]{2,1,0:T(8,128)(2,1)S(1)} collective-permute-done((bf16[4,192,128]{2,1,0:T(8,128)(2,1)S(1)}, bf16[4,192,128]{2,1,0:T(8,128)(2,1)S(1)}, u32[]{:S(2)}, u32[]{:S(2)}) %collective-permute-start) | collective-permute-done | bytes 196640 | tf_op jit(solution)/shard_map/ppermute | solution.py:113
  34.8 3.4 %collective-permute-start.14 = (bf16[128,2048]{1,0:T(8,128)(2,1)}, bf16[128,2048]{1,0:T(8,128)(2,1)S(1)}, u32[]{:S(2)}, u32[]{:S(2)}) collective-permute-start(bf16[128,2048]{1,0:T(8,128)(2,1)} %collective-permute-done.13.refs_2_), channel_id=1, source_target_pairs={{4,8},{8,4},{5,9},{9,5},{6,10},{10,6},{7,11},{11,7},{20,24},{24,20... | collective-permute-start | bytes 1572872 | tf_op jit(solution)/shard_map/ppermute | solution.py:113
  39.7 2.2 %collective-permute-start.12 = (bf16[128,2048]{1,0:T(8,128)(2,1)S(1)}, bf16[128,2048]{1,0:T(8,128)(2,1)S(1)}, u32[]{:S(2)}, u32[]{:S(2)}) collective-permute-start(bf16[128,2048]{1,0:T(8,128)(2,1)S(1)} %collective-permute-done.11.refs_1_), channel_id=1, source_target_pairs={{4,0},{8,12},{5,1},{9,13},{6,2},{10,14},{7,3},{11,15},{20,16},{24,... | collective-permute-start | bytes 1572872 | tf_op jit(solution)/shard_map/ppermute | solution.py:113
  41.9 4.5 %collective-permute-done.2 = bf16[128,2048]{1,0:T(8,128)(2,1)S(1)} collective-permute-done((bf16[128,2048]{1,0:T(8,128)(2,1)S(1)}, bf16[128,2048]{1,0:T(8,128)(2,1)S(1)}, u32[]{:S(2)}, u32[]{:S(2)}) %collective-permute-start.2) | collective-permute-done | bytes 524320 | tf_op jit(solution)/shard_map/ppermute | solution.py:113
  46.5 1.6 %collective-permute-start.9 = (f32[192,256]{1,0:T(8,128)S(1)}, f32[192,256]{1,0:T(8,128)S(1)}, u32[]{:S(2)}, u32[]{:S(2)}) collective-permute-start(f32[192,256]{1,0:T(8,128)S(1)} %fusion.3), channel_id=1, source_target_pairs={{0,2},{2,0},{1,3},{3,1},{4,6},{6,4},{5,7},{7,5},{8,10},{10,8},{9,1... | collective-permute-start | bytes 589832 | tf_op jit(solution)/shard_map/ppermute | solution.py:113
  48.2 3.5 %collective-permute-start.3 = (bf16[128,2048]{1,0:T(8,128)(2,1)S(1)}, bf16[128,2048]{1,0:T(8,128)(2,1)S(1)}, u32[]{:S(2)}, u32[]{:S(2)}) collective-permute-start(bf16[128,2048]{1,0:T(8,128)(2,1)S(1)} %add_convert_fusion.7), channel_id=1, source_target_pairs={{4,8},{8,4},{5,9},{9,5},{6,10},{10,6},{7,11},{11,7},{20,24},{24,20... | collective-permute-start | bytes 1572872 | tf_op jit(solution)/shard_map/ppermute | solution.py:113
  56.3 2.4 %shard_map.85 = f32[2,192,384]{2,1,0:T(8,128)S(1)} custom-call(s32[1]{0:T(128)} %bitcast.14.place_ref, bf16[192,2048]{1,0:T(8,128)(2,1)S(1)} %get-tuple-element.45.err_own_ref.own_ref, bf16[192,2048]{1,0:T(8,128)(2,1)S(1)} %collective-permute-done.1.err_other_ref.other_ref, bf16[128,2048]{1,0:T(8,128)(2,1)S(1)} %broadcast_select_fusion.refs_0_, ...), custom_call_target="tpu_custom_call" | custom-call | tf_op jit(solution)/shard_map/pallas_call | solution.py:33
  59.0 3.5 %collective-permute-done.3 = bf16[128,2048]{1,0:T(8,128)(2,1)S(1)} collective-permute-done((bf16[128,2048]{1,0:T(8,128)(2,1)S(1)}, bf16[128,2048]{1,0:T(8,128)(2,1)S(1)}, u32[]{:S(2)}, u32[]{:S(2)}) %collective-permute-start.3) | collective-permute-done | bytes 524320 | tf_op jit(solution)/shard_map/ppermute | solution.py:113
  62.7 1.6 %collective-permute-start.16 = (f32[192,384]{1,0:T(8,128)S(1)}, f32[192,384]{1,0:T(8,128)S(1)}, u32[]{:S(2)}, u32[]{:S(2)}) collective-permute-start(f32[192,384]{1,0:T(8,128)S(1)} %fusion.2), channel_id=1, source_target_pairs={{0,2},{2,0},{1,3},{3,1},{4,6},{6,4},{5,7},{7,5},{8,10},{10,8},{9,1... | collective-permute-start | bytes 884744 | tf_op jit(solution)/shard_map/ppermute | solution.py:113
  64.2 4.2 %collective-permute-done.5 = bf16[128,2048]{1,0:T(8,128)(2,1)S(1)} collective-permute-done((bf16[128,2048]{1,0:T(8,128)(2,1)S(1)}, bf16[128,2048]{1,0:T(8,128)(2,1)S(1)}, u32[]{:S(2)}, u32[]{:S(2)}) %collective-permute-start.5) | collective-permute-done | bytes 524320 | tf_op jit(solution)/shard_map/ppermute | solution.py:113
  70.2 2.5 %collective-permute-start.4 = (bf16[128,2048]{1,0:T(8,128)(2,1)S(1)}, bf16[128,2048]{1,0:T(8,128)(2,1)S(1)}, u32[]{:S(2)}, u32[]{:S(2)}) collective-permute-start(bf16[128,2048]{1,0:T(8,128)(2,1)S(1)} %add_convert_fusion.6), channel_id=1, source_target_pairs={{0,4},{4,0},{8,12},{12,8},{1,5},{5,1},{9,13},{13,9},{2,6},{6,2},{1... | collective-permute-start | bytes 1572872 | tf_op jit(solution)/shard_map/ppermute | solution.py:113
  73.2 3.8 %collective-permute-done.18 = bf16[128,2048]{1,0:T(8,128)(2,1)S(1)} collective-permute-done((bf16[128,2048]{1,0:T(8,128)(2,1)S(1)}, bf16[128,2048]{1,0:T(8,128)(2,1)S(1)}, u32[]{:S(2)}, u32[]{:S(2)}) %collective-permute-start.18) | collective-permute-done | bytes 524320 | tf_op jit(solution)/shard_map/ppermute | solution.py:113
  77.1 2.2 %collective-permute-start.19 = (bf16[128,2048]{1,0:T(8,128)(2,1)S(1)}, bf16[128,2048]{1,0:T(8,128)(2,1)S(1)}, u32[]{:S(2)}, u32[]{:S(2)}) collective-permute-start(bf16[128,2048]{1,0:T(8,128)(2,1)S(1)} %add_convert_fusion.3), channel_id=1, source_target_pairs={{4,8},{8,4},{5,9},{9,5},{6,10},{10,6},{7,11},{11,7},{20,24},{24,20... | collective-permute-start | bytes 1572872 | tf_op jit(solution)/shard_map/ppermute | solution.py:113
  80.6 3.6 %collective-permute-start.6 = (bf16[128,2048]{1,0:T(8,128)(2,1)S(1)}, bf16[128,2048]{1,0:T(8,128)(2,1)S(1)}, u32[]{:S(2)}, u32[]{:S(2)}) collective-permute-start(bf16[128,2048]{1,0:T(8,128)(2,1)S(1)} %add_convert_fusion.5), channel_id=1, source_target_pairs={{4,8},{8,4},{5,9},{9,5},{6,10},{10,6},{7,11},{11,7},{20,24},{24,20... | collective-permute-start | bytes 1572872 | tf_op jit(solution)/shard_map/ppermute | solution.py:113
  85.2 3.0 %collective-permute-done.4 = bf16[128,2048]{1,0:T(8,128)(2,1)S(1)} collective-permute-done((bf16[128,2048]{1,0:T(8,128)(2,1)S(1)}, bf16[128,2048]{1,0:T(8,128)(2,1)S(1)}, u32[]{:S(2)}, u32[]{:S(2)}) %collective-permute-start.4) | collective-permute-done | bytes 524320 | tf_op jit(solution)/shard_map/ppermute | solution.py:113
  88.2 5.6 %collective-permute-done.19 = bf16[128,2048]{1,0:T(8,128)(2,1)S(1)} collective-permute-done((bf16[128,2048]{1,0:T(8,128)(2,1)S(1)}, bf16[128,2048]{1,0:T(8,128)(2,1)S(1)}, u32[]{:S(2)}, u32[]{:S(2)}) %collective-permute-start.19) | collective-permute-done | bytes 524320 | tf_op jit(solution)/shard_map/ppermute | solution.py:113
  94.0 5.4 %collective-permute-done.21 = bf16[128,2048]{1,0:T(8,128)(2,1)S(1)} collective-permute-done((bf16[128,2048]{1,0:T(8,128)(2,1)S(1)}, bf16[128,2048]{1,0:T(8,128)(2,1)S(1)}, u32[]{:S(2)}, u32[]{:S(2)}) %collective-permute-start.21) | collective-permute-done | bytes 524320 | tf_op jit(solution)/shard_map/ppermute | solution.py:113
  99.5 2.2 %collective-permute-start.22 = (bf16[128,2048]{1,0:T(8,128)(2,1)S(1)}, bf16[128,2048]{1,0:T(8,128)(2,1)S(1)}, u32[]{:S(2)}, u32[]{:S(2)}) collective-permute-start(bf16[128,2048]{1,0:T(8,128)(2,1)S(1)} %add_convert_fusion.1), channel_id=1, source_target_pairs={{4,8},{8,4},{5,9},{9,5},{6,10},{10,6},{7,11},{11,7},{20,24},{24,20... | collective-permute-start | bytes 1572872 | tf_op jit(solution)/shard_map/ppermute | solution.py:113
  103.8 5.4 %collective-permute-done.20 = bf16[128,2048]{1,0:T(8,128)(2,1)S(1)} collective-permute-done((bf16[128,2048]{1,0:T(8,128)(2,1)S(1)}, bf16[128,2048]{1,0:T(8,128)(2,1)S(1)}, u32[]{:S(2)}, u32[]{:S(2)}) %collective-permute-start.20) | collective-permute-done | bytes 524320 | tf_op jit(solution)/shard_map/ppermute | solution.py:113
  109.2 3.2 %collective-permute-done.22 = bf16[128,2048]{1,0:T(8,128)(2,1)S(1)} collective-permute-done((bf16[128,2048]{1,0:T(8,128)(2,1)S(1)}, bf16[128,2048]{1,0:T(8,128)(2,1)S(1)}, u32[]{:S(2)}, u32[]{:S(2)}) %collective-permute-start.22) | collective-permute-done | bytes 524320 | tf_op jit(solution)/shard_map/ppermute | solution.py:113
  (89 shorter events, 21.0 us)
Async XLA Ops:
  0.6 11.4 %all-to-all-start = ((bf16[4,192,128]{2,1,0:T(8,128)(2,1)}), bf16[4,192,128]{2,1,0:T(8,128)(2,1)S(1)}, u32[]{:S(2)}, u32[]{:S(2)}) async-start(bf16[4,192,128]{2,1,0:T(8,128)(2,1)} %bitcast.49), calls=%async_computation | async-start | bytes 393216 | tf_op jit(solution)/shard_map/all_to_all | solution.py:128
  8.6 23.3 %collective-permute-start.1 = (bf16[192,2048]{1,0:T(8,128)(2,1)}, bf16[192,2048]{1,0:T(8,128)(2,1)S(1)}, u32[]{:S(2)}, u32[]{:S(2)}) collective-permute-start(bf16[192,2048]{1,0:T(8,128)(2,1)} %get-tuple-element.44), channel_id=1, source_target_pairs={{0,2},{2,0},{1,3},{3,1},{4,6},{6,4},{5,7},{7,5},{8,10},{10,8},{9,1... | collective-permute-start | bytes 2359304 | tf_op jit(solution)/shard_map/ppermute | solution.py:113
  10.1 24.7 %collective-permute-start.13 = (bf16[128,2048]{1,0:T(8,128)(2,1)S(1)}, bf16[128,2048]{1,0:T(8,128)(2,1)}, u32[]{:S(2)}, u32[]{:S(2)}) collective-permute-start(bf16[128,2048]{1,0:T(8,128)(2,1)S(1)} %dynamic-slice_bitcast_fusion.2.refs_0_), channel_id=1, source_target_pairs={{0,4},{4,0},{8,12},{12,8},{1,5},{5,1},{9,13},{13,9},{2,6},{6,2},{1... | collective-permute-start | bytes 1572872 | tf_op jit(solution)/shard_map/ppermute | solution.py:113
  12.1 21.6 %collective-permute-start.7 = (bf16[128,2048]{1,0:T(8,128)(2,1)S(1)}, bf16[128,2048]{1,0:T(8,128)(2,1)S(1)}, u32[]{:S(2)}, u32[]{:S(2)}) collective-permute-start(bf16[128,2048]{1,0:T(8,128)(2,1)S(1)} %dynamic-slice_bitcast_fusion.2.refs_0_), channel_id=1, source_target_pairs={{0,12},{12,0},{1,13},{13,1},{2,14},{14,2},{3,15},{15,3},{16,28},{2... | collective-permute-start | bytes 1572872 | tf_op jit(solution)/shard_map/ppermute | solution.py:113
  12.8 26.9 %collective-permute-start.11 = (bf16[128,2048]{1,0:T(8,128)(2,1)S(1)}, bf16[128,2048]{1,0:T(8,128)(2,1)S(1)}, u32[]{:S(2)}, u32[]{:S(2)}) collective-permute-start(bf16[128,2048]{1,0:T(8,128)(2,1)S(1)} %dynamic-slice_bitcast_fusion.2.refs_0_), channel_id=1, source_target_pairs={{4,8},{8,4},{5,9},{9,5},{6,10},{10,6},{7,11},{11,7},{20,24},{24,20... | collective-permute-start | bytes 1572872 | tf_op jit(solution)/shard_map/ppermute | solution.py:113
  17.5 14.2 %collective-permute-start = (bf16[4,192,128]{2,1,0:T(8,128)(2,1)S(1)}, bf16[4,192,128]{2,1,0:T(8,128)(2,1)S(1)}, u32[]{:S(2)}, u32[]{:S(2)}) collective-permute-start(bf16[4,192,128]{2,1,0:T(8,128)(2,1)S(1)} %all-to-all-done), channel_id=1, source_target_pairs={{0,2},{2,0},{1,3},{3,1},{4,6},{6,4},{5,7},{7,5},{8,10},{10,8},{9,1... | collective-permute-start | bytes 589832 | tf_op jit(solution)/shard_map/ppermute | solution.py:113
  32.4 14.1 %collective-permute-start.2 = (bf16[128,2048]{1,0:T(8,128)(2,1)S(1)}, bf16[128,2048]{1,0:T(8,128)(2,1)S(1)}, u32[]{:S(2)}, u32[]{:S(2)}) collective-permute-start(bf16[128,2048]{1,0:T(8,128)(2,1)S(1)} %shard_map.80), channel_id=1, source_target_pairs={{0,4},{12,8},{1,5},{13,9},{2,6},{14,10},{3,7},{15,11},{16,20},{28,... | collective-permute-start | bytes 1572872 | tf_op jit(solution)/shard_map/ppermute | solution.py:113
  34.7 7.2 %collective-permute-start.8 = (f32[192,256]{1,0:T(8,128)S(1)}, f32[192,256]{1,0:T(8,128)S(1)}, u32[]{:S(2)}, u32[]{:S(2)}) collective-permute-start(f32[192,256]{1,0:T(8,128)S(1)} %slice_bitcast_fusion.2), channel_id=1, source_target_pairs={{0,1},{1,0},{2,3},{3,2},{4,5},{5,4},{6,7},{7,6},{8,9},{9,8},{10,11... | collective-permute-start | bytes 589832 | tf_op jit(solution)/shard_map/ppermute | solution.py:113
  34.8 18.4 %collective-permute-start.14 = (bf16[128,2048]{1,0:T(8,128)(2,1)}, bf16[128,2048]{1,0:T(8,128)(2,1)S(1)}, u32[]{:S(2)}, u32[]{:S(2)}) collective-permute-start(bf16[128,2048]{1,0:T(8,128)(2,1)} %collective-permute-done.13.refs_2_), channel_id=1, source_target_pairs={{4,8},{8,4},{5,9},{9,5},{6,10},{10,6},{7,11},{11,7},{20,24},{24,20... | collective-permute-start | bytes 1572872 | tf_op jit(solution)/shard_map/ppermute | solution.py:113
  39.7 14.0 %collective-permute-start.12 = (bf16[128,2048]{1,0:T(8,128)(2,1)S(1)}, bf16[128,2048]{1,0:T(8,128)(2,1)S(1)}, u32[]{:S(2)}, u32[]{:S(2)}) collective-permute-start(bf16[128,2048]{1,0:T(8,128)(2,1)S(1)} %collective-permute-done.11.refs_1_), channel_id=1, source_target_pairs={{4,0},{8,12},{5,1},{9,13},{6,2},{10,14},{7,3},{11,15},{20,16},{24,... | collective-permute-start | bytes 1572872 | tf_op jit(solution)/shard_map/ppermute | solution.py:113
  46.5 6.5 %collective-permute-start.9 = (f32[192,256]{1,0:T(8,128)S(1)}, f32[192,256]{1,0:T(8,128)S(1)}, u32[]{:S(2)}, u32[]{:S(2)}) collective-permute-start(f32[192,256]{1,0:T(8,128)S(1)} %fusion.3), channel_id=1, source_target_pairs={{0,2},{2,0},{1,3},{3,1},{4,6},{6,4},{5,7},{7,5},{8,10},{10,8},{9,1... | collective-permute-start | bytes 589832 | tf_op jit(solution)/shard_map/ppermute | solution.py:113
  48.2 14.3 %collective-permute-start.3 = (bf16[128,2048]{1,0:T(8,128)(2,1)S(1)}, bf16[128,2048]{1,0:T(8,128)(2,1)S(1)}, u32[]{:S(2)}, u32[]{:S(2)}) collective-permute-start(bf16[128,2048]{1,0:T(8,128)(2,1)S(1)} %add_convert_fusion.7), channel_id=1, source_target_pairs={{4,8},{8,4},{5,9},{9,5},{6,10},{10,6},{7,11},{11,7},{20,24},{24,20... | collective-permute-start | bytes 1572872 | tf_op jit(solution)/shard_map/ppermute | solution.py:113
  51.7 16.8 %collective-permute-start.5 = (bf16[128,2048]{1,0:T(8,128)(2,1)S(1)}, bf16[128,2048]{1,0:T(8,128)(2,1)S(1)}, u32[]{:S(2)}, u32[]{:S(2)}) collective-permute-start(bf16[128,2048]{1,0:T(8,128)(2,1)S(1)} %add_convert_fusion.7), channel_id=1, source_target_pairs={{0,4},{12,8},{1,5},{13,9},{2,6},{14,10},{3,7},{15,11},{16,20},{28,... | collective-permute-start | bytes 1572872 | tf_op jit(solution)/shard_map/ppermute | solution.py:113
  53.2 1.4 %collective-permute-start.10 = (bf16[192,256]{1,0:T(8,128)(2,1)S(1)}, bf16[192,256]{1,0:T(8,128)(2,1)S(1)}, u32[]{:S(2)}, u32[]{:S(2)}) collective-permute-start(bf16[192,256]{1,0:T(8,128)(2,1)S(1)} %pad_maximum_fusion.1), channel_id=1, source_target_pairs={{0,1},{1,0},{2,3},{3,2},{4,5},{5,4},{6,7},{7,6},{8,9},{9,8},{10,11... | collective-permute-start | bytes 294920 | tf_op jit(solution)/shard_map/ppermute | solution.py:113
  55.0 21.9 %collective-permute-start.18 = (bf16[128,2048]{1,0:T(8,128)(2,1)S(1)}, bf16[128,2048]{1,0:T(8,128)(2,1)S(1)}, u32[]{:S(2)}, u32[]{:S(2)}) collective-permute-start(bf16[128,2048]{1,0:T(8,128)(2,1)S(1)} %shard_map.84), channel_id=1, source_target_pairs={{0,4},{12,8},{1,5},{13,9},{2,6},{14,10},{3,7},{15,11},{16,20},{28,... | collective-permute-start | bytes 1572872 | tf_op jit(solution)/shard_map/ppermute | solution.py:113
  58.8 3.8 %collective-permute-start.15 = (f32[192,384]{1,0:T(8,128)S(1)}, f32[192,384]{1,0:T(8,128)S(1)}, u32[]{:S(2)}, u32[]{:S(2)}) collective-permute-start(f32[192,384]{1,0:T(8,128)S(1)} %slice_bitcast_fusion), channel_id=1, source_target_pairs={{0,1},{1,0},{2,3},{3,2},{4,5},{5,4},{6,7},{7,6},{8,9},{9,8},{10,11... | collective-permute-start | bytes 884744 | tf_op jit(solution)/shard_map/ppermute | solution.py:113
  62.7 7.2 %collective-permute-start.16 = (f32[192,384]{1,0:T(8,128)S(1)}, f32[192,384]{1,0:T(8,128)S(1)}, u32[]{:S(2)}, u32[]{:S(2)}) collective-permute-start(f32[192,384]{1,0:T(8,128)S(1)} %fusion.2), channel_id=1, source_target_pairs={{0,2},{2,0},{1,3},{3,1},{4,6},{6,4},{5,7},{7,5},{8,10},{10,8},{9,1... | collective-permute-start | bytes 884744 | tf_op jit(solution)/shard_map/ppermute | solution.py:113
  70.1 2.6 %collective-permute-start.17 = (bf16[192,384]{1,0:T(8,128)(2,1)S(1)}, bf16[192,384]{1,0:T(8,128)(2,1)S(1)}, u32[]{:S(2)}, u32[]{:S(2)}) collective-permute-start(bf16[192,384]{1,0:T(8,128)(2,1)S(1)} %pad_maximum_fusion), channel_id=1, source_target_pairs={{0,1},{1,0},{2,3},{3,2},{4,5},{5,4},{6,7},{7,6},{8,9},{9,8},{10,11... | collective-permute-start | bytes 442376 | tf_op jit(solution)/shard_map/ppermute | solution.py:113
  70.2 18.0 %collective-permute-start.4 = (bf16[128,2048]{1,0:T(8,128)(2,1)S(1)}, bf16[128,2048]{1,0:T(8,128)(2,1)S(1)}, u32[]{:S(2)}, u32[]{:S(2)}) collective-permute-start(bf16[128,2048]{1,0:T(8,128)(2,1)S(1)} %add_convert_fusion.6), channel_id=1, source_target_pairs={{0,4},{4,0},{8,12},{12,8},{1,5},{5,1},{9,13},{13,9},{2,6},{6,2},{1... | collective-permute-start | bytes 1572872 | tf_op jit(solution)/shard_map/ppermute | solution.py:113
  77.1 16.8 %collective-permute-start.19 = (bf16[128,2048]{1,0:T(8,128)(2,1)S(1)}, bf16[128,2048]{1,0:T(8,128)(2,1)S(1)}, u32[]{:S(2)}, u32[]{:S(2)}) collective-permute-start(bf16[128,2048]{1,0:T(8,128)(2,1)S(1)} %add_convert_fusion.3), channel_id=1, source_target_pairs={{4,8},{8,4},{5,9},{9,5},{6,10},{10,6},{7,11},{11,7},{20,24},{24,20... | collective-permute-start | bytes 1572872 | tf_op jit(solution)/shard_map/ppermute | solution.py:113
  79.3 20.1 %collective-permute-start.21 = (bf16[128,2048]{1,0:T(8,128)(2,1)S(1)}, bf16[128,2048]{1,0:T(8,128)(2,1)S(1)}, u32[]{:S(2)}, u32[]{:S(2)}) collective-permute-start(bf16[128,2048]{1,0:T(8,128)(2,1)S(1)} %add_convert_fusion.3), channel_id=1, source_target_pairs={{0,4},{12,8},{1,5},{13,9},{2,6},{14,10},{3,7},{15,11},{16,20},{28,... | collective-permute-start | bytes 1572872 | tf_op jit(solution)/shard_map/ppermute | solution.py:113
  80.6 22.1 %collective-permute-start.6 = (bf16[128,2048]{1,0:T(8,128)(2,1)S(1)}, bf16[128,2048]{1,0:T(8,128)(2,1)S(1)}, u32[]{:S(2)}, u32[]{:S(2)}) collective-permute-start(bf16[128,2048]{1,0:T(8,128)(2,1)S(1)} %add_convert_fusion.5), channel_id=1, source_target_pairs={{4,8},{8,4},{5,9},{9,5},{6,10},{10,6},{7,11},{11,7},{20,24},{24,20... | collective-permute-start | bytes 1572872 | tf_op jit(solution)/shard_map/ppermute | solution.py:113
  93.9 15.3 %collective-permute-start.20 = (bf16[128,2048]{1,0:T(8,128)(2,1)S(1)}, bf16[128,2048]{1,0:T(8,128)(2,1)S(1)}, u32[]{:S(2)}, u32[]{:S(2)}) collective-permute-start(bf16[128,2048]{1,0:T(8,128)(2,1)S(1)} %add_convert_fusion.2), channel_id=1, source_target_pairs={{0,4},{4,0},{8,12},{12,8},{1,5},{5,1},{9,13},{13,9},{2,6},{6,2},{1... | collective-permute-start | bytes 1572872 | tf_op jit(solution)/shard_map/ppermute | solution.py:113
  99.5 12.9 %collective-permute-start.22 = (bf16[128,2048]{1,0:T(8,128)(2,1)S(1)}, bf16[128,2048]{1,0:T(8,128)(2,1)S(1)}, u32[]{:S(2)}, u32[]{:S(2)}) collective-permute-start(bf16[128,2048]{1,0:T(8,128)(2,1)S(1)} %add_convert_fusion.1), channel_id=1, source_target_pairs={{4,8},{8,4},{5,9},{9,5},{6,10},{10,6},{7,11},{11,7},{20,24},{24,20... | collective-permute-start | bytes 1572872 | tf_op jit(solution)/shard_map/ppermute | solution.py:113
  (4 other events, 24.1 us)
